TPU v7x, 32 devices: a whole 2x2x4 slice. The times are simulated.
32 devices in a mesh: blk: 32 (over z, y, x, core).
Axes of the slice: x: 2, y: 2, z: 4, core: 2. Of those that a mesh axis runs over, the one named last changes fastest.
Arguments:
- estimate: float32 [32, 110592], P('blk'), may hold values from 0.3 to 1.5
- observed: bfloat16 [32, 6, 110592], P('blk'), may hold values from 0.19921875 to 2
- psf_cells: float32 [32, 6, 4913], P('blk'), may hold values from 0.005 to 1.8, as said below
- tissue: int32 [32], P('blk'), may hold values from 0 to 1, as said below
- neighbours: int32 [32, 6], P('blk'), may hold values from -1 to 31, as said below
- psf_list: int32 [32, 6, 2], P('blk'), may hold values from 0 to 31
- psf_blend: float32 [32, 6, 2], P('blk'), may hold values from 0.1 to 1
- cell_row: int32 [32], replicated, may hold values from 0 to 31, each once
- view_order: int32 [6], replicated, may hold values from 0 to 5, each once
Outputs:
- refined: float32 [32, 110592], P('blk')
Inputs may be any that keep to these rules, and one draw needn't show every extreme that they name: Block b sits on device b; blocks 0 to 1 and 16 to 17 are always tissue. With h the top bit of a block's number and r the number without it: bit 3j of r is bit j of the first grid coordinate, bit 3j + 1 of the second, bit 3j + 2 is bit j + 1 of the third, whose lowest bit is h. neighbours[b, f] is the block next to b across face f in that grid if both are tissue, else -1. `cell_row`: each grid cell in exactly one row. `view_order`: each view once; the first 2 entries are used. `psf_cells`: Positive.
All inputs are finite; a program needn't handle non-finite values.
Results may differ from a plain program's by a relative error of at most 0.0003.
Values may be sent and summed in bfloat16 or wider, within the bound.
No kernel may reach another device: no remote copies, remote signals or barrier semaphores. Data moves between devices by JAX's collectives and lax.ppermute only.
A program may use at most 128 MiB of HBM per device.

v0:
```python
import math

import jax
import jax.numpy as jnp
from jax import lax
from jax.sharding import PartitionSpec as P

E = 48
MARGIN = 8
UPDATES = 2
PAD = 64
KS = 17
E3 = 110592
KS3 = 4913
FACE = 18432


HIGHEST = lax.Precision.HIGHEST


def dft_tables(length):
    numbers = jnp.arange(length, dtype=jnp.int32)
    phase = (numbers[:, None] * numbers[None, :] % length).astype(jnp.float32) * (
        2.0 * math.pi / length
    )
    cosine = jnp.cos(phase)
    sine_table = jnp.sin(phase)
    forward_table = jnp.stack(
        [jnp.stack([cosine, sine_table], axis=1), jnp.stack([-sine_table, cosine], axis=1)], axis=0
    )
    inverse_table = jnp.stack(
        [jnp.stack([cosine, -sine_table], axis=1), jnp.stack([sine_table, cosine], axis=1)], axis=0
    )
    return (forward_table, inverse_table)


def forward(values_in, forward_table):
    pair = jnp.einsum("ckn,abn->ckab", forward_table[:, :, 0, :], values_in, precision=HIGHEST)
    for section in range(2):
        pair = jnp.einsum("cksn,sabn->ckab", forward_table, pair, precision=HIGHEST)
    return pair


def inverse_real(pair, inverse_table):
    for section in range(2):
        pair = jnp.einsum("cksn,sabn->ckab", inverse_table, pair, precision=HIGHEST)
    result = jnp.einsum("ksn,sabn->kab", inverse_table[0], pair, precision=HIGHEST)
    return result


def times_spectrum(pair, kernel_pair, conjugate):
    sign = -1.0 if conjugate else 1.0
    real_part = pair[0] * kernel_pair[0] - sign * pair[1] * kernel_pair[1]
    imag_part = pair[1] * kernel_pair[0] + sign * pair[0] * kernel_pair[1]
    return jnp.stack([real_part, imag_part], axis=0)


def side_slab(volume, face_index):
    axis_number = volume.ndim - 3 + face_index // 2
    start_now = 0 if face_index % 2 == 0 else E - MARGIN
    return lax.slice_in_dim(volume, start_now, start_now + MARGIN, axis=axis_number)


def assemble(core_block, margin_rows):
    padded = jnp.zeros((PAD, PAD, PAD), jnp.float32)
    padded = padded.at[MARGIN : MARGIN + E, MARGIN : MARGIN + E, MARGIN : MARGIN + E].set(
        core_block
    )
    for face_index in range(6):
        axis_number = face_index // 2
        shape_now = [E, E, E]
        shape_now[axis_number] = MARGIN
        slab_now = margin_rows[face_index].astype(jnp.float32).reshape(shape_now)
        start_now = [MARGIN, MARGIN, MARGIN]
        start_now[axis_number] = 0 if face_index % 2 == 0 else MARGIN + E
        padded = lax.dynamic_update_slice(padded, slab_now, start_now)
    return padded


def place_kernel(kernel):
    grid_cube = jnp.zeros((PAD, PAD, PAD), jnp.float32)
    grid_cube = grid_cube.at[0:KS, 0:KS, 0:KS].set(kernel.reshape(KS, KS, KS))
    return jnp.roll(grid_cube, (-MARGIN, -MARGIN, -MARGIN), axis=(0, 1, 2))


def refine(core_block, margin_rows, kernel, observed_block, forward_table, inverse_table):
    scale_back = 1.0 / float(PAD * PAD * PAD)
    padded = assemble(core_block, margin_rows)
    kernel_pair = forward(place_kernel(kernel), forward_table)
    field_pair = forward(padded, forward_table)
    blurred = inverse_real(times_spectrum(field_pair, kernel_pair, False), inverse_table)
    blurred = blurred[MARGIN : MARGIN + E, MARGIN : MARGIN + E, MARGIN : MARGIN + E] * scale_back
    quotient = observed_block.astype(jnp.float32) / blurred
    holder = jnp.zeros((PAD, PAD, PAD), jnp.float32)
    holder = holder.at[MARGIN : MARGIN + E, MARGIN : MARGIN + E, MARGIN : MARGIN + E].set(quotient)
    ratio_pair = forward(holder, forward_table)
    correction = inverse_real(times_spectrum(ratio_pair, kernel_pair, True), inverse_table)
    correction = (
        correction[MARGIN : MARGIN + E, MARGIN : MARGIN + E, MARGIN : MARGIN + E] * scale_back
    )
    return core_block * correction


def blend_cells(running, shard_rows, cell_rows, weights):
    row_count = shard_rows.shape[0]
    picks = cell_rows[:, :, None] == jnp.arange(row_count, dtype=jnp.int32)[None, None, :]
    picks = picks.astype(jnp.float32) * weights[:, :, None]
    scaled = shard_rows / jnp.sum(shard_rows, axis=1, keepdims=True)
    return running + jnp.einsum("bkr,rc->bc", picks, scaled, precision=HIGHEST)


def local(
    estimate, observed, psf_cells, tissue, neighbours, psf_list, psf_blend, cell_row, view_order
):
    blocks = estimate.shape[0]
    devices = lax.axis_size("blk")
    own_device = lax.axis_index("blk")
    forward_table, inverse_table = dft_tables(PAD)
    opposite = jnp.array([1, 0, 3, 2, 5, 4], jnp.int32)
    owners = jnp.where(neighbours >= 0, neighbours // blocks, -1)
    slot_ids = jnp.maximum(neighbours, 0) % blocks
    present = neighbours >= 0
    current = estimate.reshape(blocks, E, E, E)
    view_list = [view_order[update] for update in range(UPDATES)]
    rows_list = []
    weight_list = []
    for update in range(UPDATES):
        listed = lax.dynamic_index_in_dim(psf_list, view_list[update], 1, keepdims=False)
        rows_list.append(cell_row[listed])
        weights = lax.dynamic_index_in_dim(psf_blend, view_list[update], 1, keepdims=False)
        weight_list.append(weights / jnp.sum(weights, axis=1, keepdims=True))
    stacked_cells = jnp.stack(
        [
            lax.dynamic_index_in_dim(psf_cells, view_list[update], 1, keepdims=False)
            for update in range(UPDATES)
        ],
        axis=1,
    )

    def add_views(running, shard_rows):
        return jnp.stack(
            [
                blend_cells(
                    running[update], shard_rows[:, update], rows_list[update], weight_list[update]
                )
                for update in range(UPDATES)
            ],
            axis=0,
        )

    all_kernels = add_views(
        jnp.zeros((UPDATES, blocks, KS3), jnp.float32),
        lax.all_gather(stacked_cells.astype(jnp.bfloat16), "blk", axis=0, tiled=True).astype(
            jnp.float32
        ),
    )
    kernel_list = [all_kernels[update] for update in range(UPDATES)]
    for update in range(UPDATES):
        view_now = view_list[update]
        kernels = kernel_list[update]
        side_slabs = jnp.stack(
            [side_slab(current, face_index).reshape(blocks, FACE) for face_index in range(6)],
            axis=1,
        )
        side_slabs = side_slabs.astype(jnp.bfloat16)
        chosen = (owners[:, :, None] == jnp.arange(devices, dtype=jnp.int32)[None, None, :]) & (
            owners[:, :, None] != own_device
        )
        outgoing = jnp.einsum(
            "sfp,sfc->psc",
            chosen.astype(jnp.bfloat16),
            side_slabs,
            preferred_element_type=jnp.float32,
        ).astype(jnp.bfloat16)
        arrived = lax.all_to_all(outgoing, "blk", split_axis=0, concat_axis=0, tiled=True)
        remote = arrived.reshape(devices * blocks, FACE)[jnp.maximum(neighbours, 0)]
        local_slabs = side_slabs[slot_ids, opposite[None, :]]
        margins = jnp.where((owners == own_device)[:, :, None], local_slabs, remote)
        margins = jnp.where(present[:, :, None], margins, jnp.zeros_like(margins))
        seen_now = lax.dynamic_index_in_dim(observed, view_now, 1, keepdims=False)
        core_block = current[0]
        observed_block = seen_now[0].reshape(E, E, E)
        refined = jnp.where(
            tissue[0] > 0,
            refine(
                core_block, margins[0], kernels[0], observed_block, forward_table, inverse_table
            ),
            core_block,
        )
        updated = [refined]
        current = jnp.stack(updated, axis=0)
    return current.reshape(blocks, E3)


def solution(mesh):
    return jax.shard_map(
        local,
        mesh=mesh,
        in_specs=(
            P("blk", None),
            P("blk", None, None),
            P("blk", None, None),
            P("blk"),
            P("blk", None),
            P("blk", None, None),
            P("blk", None, None),
            P(),
            P(),
        ),
        out_specs=P("blk", None),
        check_vma=False,
    )
```

profile of v0, /device:TPU:0, one launch (start us, length us, event | category | flops | bytes accessed | tf_op | source)
XLA Modules:
  0.0 677.3 jit_solution(1253485544691847126)
XLA Ops:
  21.9 51.4 %all_gather.3 = bf16[32,2,4913]{2,1,0:T(2,128)(2,1)S(1)} all-gather(bf16[1,2,4913]{2,1,0:T(2,128)(2,1)S(1)} %pad_maximum_fusion.11), channel_id=1, replica_groups=mesh['blk'=32] {'blk'}, dimensions={0}, use_global_device_ids=true | all-gather | bytes 648516 | tf_op jit(solution)/shard_map/all_gather | solution.py:153
  90.0 17.4 %fusion.227 = f32[1,17,17,17]{3,0,2,1:T(1,128)S(1)} fusion(f32[17,17,17,32]{3,2,1,0:T(8,128)S(1)} %dot_general.115, f32[32]{0:T(128)S(1)} %fusion.217), kind=kOutput, calls=%fused_computation.278 | convolution fusion | flops 1886592 | bytes 648644 | tf_op jit(solution)/shard_map/bkr,rc->bc/dot_general | solution.py:109
  143.3 8.9 %fusion.76 = f32[2,64,64,64]{3,1,2,0:T(8,128)S(1)} fusion(f32[2,64,64,64]{3,1,2,0:T(8,128)S(1)} %fusion.132, f32[1,64,2,64]{3,1,0,2:T(8,128)S(1)} %get-tuple-element.124, f32[1,64,2,64]{3,1,0,2:T(8,128)S(1)} %get-tuple-element.127), kind=kOutput, calls=%fused_computation.88 | convolution fusion | flops 805322752 | bytes 4259840 | tf_op jit(solution)/shard_map/cksn,sabn->ckab/dot_general | solution.py:40
  152.2 10.8 %fusion.79 = f32[2,64,64,64]{3,1,2,0:T(8,128)} fusion(f32[2,64,64,64]{3,1,2,0:T(8,128)S(1)} %fusion.76, f32[1,64,2,64]{3,1,0,2:T(8,128)S(1)} %get-tuple-element.124, f32[1,64,2,64]{3,1,0,2:T(8,128)S(1)} %get-tuple-element.127), kind=kOutput, calls=%fused_computation.89 | convolution fusion | flops 805322752 | bytes 4259840 | tf_op jit(solution)/shard_map/cksn,sabn->ckab/dot_general | solution.py:40
  188.7 15.1 %dynamic_update_slice.38 = f32[64,64,64]{2,1,0:T(8,128)S(1)} dynamic-update-slice(f32[64,64,64]{2,1,0:T(8,128)S(1)} %dynamic_update_slice.37, f32[48,8,48]{2,1,0:T(8,128)} %reshape.1082, s32[]{:T(128)} %constant.223.clone.1, s32[]{:T(128)} %constant.214.clone.1, s32[]{:T(128)} %constant.223.clone.1) | dynamic-update-slice | bytes 147460 | tf_op jit(solution)/shard_map/dynamic_update_slice | solution.py:76
  203.8 15.0 %dynamic_update_slice.39 = f32[64,64,64]{2,1,0:T(8,128)S(1)} dynamic-update-slice(f32[64,64,64]{2,1,0:T(8,128)S(1)} %dynamic_update_slice.38, f32[48,8,48]{2,1,0:T(8,128)} %reshape.1083, s32[]{:T(128)} %constant.223.clone.1, s32[]{:T(128)} %constant.224.clone.1, s32[]{:T(128)} %constant.223.clone.1) | dynamic-update-slice | bytes 147460 | tf_op jit(solution)/shard_map/dynamic_update_slice | solution.py:76
  218.8 20.3 %dynamic_update_slice.40 = f32[64,64,64]{2,1,0:T(8,128)S(1)} dynamic-update-slice(f32[64,64,64]{2,1,0:T(8,128)S(1)} %dynamic_update_slice.39, f32[48,48,8]{2,1,0:T(8,128)S(1)} %reshape.1084, s32[]{:T(128)} %constant.223.clone.1, s32[]{:T(128)} %constant.223.clone.1, s32[]{:T(128)} %constant.214.clone.1) | dynamic-update-slice | bytes 147460 | tf_op jit(solution)/shard_map/dynamic_update_slice | solution.py:76
  239.1 29.7 %dynamic_update_slice.41 = f32[64,64,64]{2,1,0:T(8,128)S(1)} dynamic-update-slice(f32[64,64,64]{2,1,0:T(8,128)S(1)} %dynamic_update_slice.40, f32[48,48,8]{2,1,0:T(8,128)} %reshape.1085, s32[]{:T(128)} %constant.223.clone.1, s32[]{:T(128)} %constant.223.clone.1, s32[]{:T(128)} %constant.224.clone.1) | dynamic-update-slice | bytes 147460 | tf_op jit(solution)/shard_map/dynamic_update_slice | solution.py:76
  275.4 8.5 %fusion.70 = f32[2,64,64,64]{3,1,2,0:T(8,128)S(1)} fusion(f32[2,64,64,64]{3,1,2,0:T(8,128)S(1)} %fusion.144, f32[1,64,2,64]{3,1,0,2:T(8,128)S(1)} %get-tuple-element.124, f32[1,64,2,64]{3,1,0,2:T(8,128)S(1)} %get-tuple-element.127), kind=kOutput, calls=%fused_computation.86 | convolution fusion | flops 805322752 | bytes 4259840 | tf_op jit(solution)/shard_map/cksn,sabn->ckab/dot_general | solution.py:40
  284.0 8.7 %fusion.73 = f32[2,64,64,64]{3,1,2,0:T(8,128)S(1)} fusion(f32[2,64,64,64]{3,1,2,0:T(8,128)S(1)} %fusion.70, f32[1,64,2,64]{3,1,0,2:T(8,128)S(1)} %get-tuple-element.124, f32[1,64,2,64]{3,1,0,2:T(8,128)S(1)} %get-tuple-element.127), kind=kOutput, calls=%fused_computation.87 | convolution fusion | flops 805322752 | bytes 4259840 | tf_op jit(solution)/shard_map/cksn,sabn->ckab/dot_general | solution.py:40
  294.6 8.9 %fusion.82 = f32[2,64,64,64]{3,1,2,0:T(8,128)S(1)} fusion(f32[2,64,64,64]{3,1,2,0:T(8,128)S(1)} %pad_maximum_fusion, f32[1,64,2,64]{3,1,2,0:T(8,128)S(1)} %get-tuple-element.128, f32[1,64,2,64]{3,1,2,0:T(8,128)S(1)} %get-tuple-element.123), kind=kOutput, calls=%fused_computation.90 | convolution fusion | flops 805322752 | bytes 4259840 | tf_op jit(solution)/shard_map/cksn,sabn->ckab/dot_general | solution.py:46
  303.6 8.5 %fusion.85 = f32[2,64,64,64]{3,1,2,0:T(8,128)S(1)} fusion(f32[2,64,64,64]{3,1,2,0:T(8,128)S(1)} %fusion.82, f32[1,64,2,64]{3,1,2,0:T(8,128)S(1)} %get-tuple-element.128, f32[1,64,2,64]{3,1,2,0:T(8,128)S(1)} %get-tuple-element.123), kind=kOutput, calls=%fused_computation.91 | convolution fusion | flops 805322752 | bytes 4259840 | tf_op jit(solution)/shard_map/cksn,sabn->ckab/dot_general | solution.py:46
  312.1 8.3 %fusion.150 = f32[64,64,64]{2,0,1:T(8,128)S(1)} fusion(f32[2,64,64,64]{3,1,2,0:T(8,128)S(1)} %fusion.85, f32[64,1,64]{2,0,1:T(8,128)S(1)} %copy-done.27, f32[64,1,64]{2,0,1:T(8,128)S(1)} %copy-done.23), kind=kOutput, calls=%fused_computation.144 | convolution fusion | flops 402661376 | bytes 3178496 | tf_op jit(solution)/shard_map/ksn,sabn->kab/dot_general | solution.py:47
  326.9 8.7 %fusion.88 = f32[2,64,64,64]{3,1,2,0:T(8,128)S(1)} fusion(f32[2,64,64,64]{3,1,2,0:T(8,128)S(1)} %fusion.142, f32[1,64,2,64]{3,1,0,2:T(8,128)S(1)} %get-tuple-element.124, f32[1,64,2,64]{3,1,0,2:T(8,128)S(1)} %get-tuple-element.127), kind=kOutput, calls=%fused_computation.92 | convolution fusion | flops 805322752 | bytes 4259840 | tf_op jit(solution)/shard_map/cksn,sabn->ckab/dot_general | solution.py:40
  335.7 8.9 %fusion.91 = f32[2,64,64,64]{3,1,2,0:T(8,128)S(1)} fusion(f32[2,64,64,64]{3,1,2,0:T(8,128)S(1)} %fusion.88, f32[1,64,2,64]{3,1,0,2:T(8,128)S(1)} %get-tuple-element.124, f32[1,64,2,64]{3,1,0,2:T(8,128)S(1)} %get-tuple-element.127), kind=kOutput, calls=%fused_computation.93 | convolution fusion | flops 805322752 | bytes 4259840 | tf_op jit(solution)/shard_map/cksn,sabn->ckab/dot_general | solution.py:40
  346.5 8.5 %fusion.94 = f32[2,64,64,64]{3,1,2,0:T(8,128)S(1)} fusion(f32[2,64,64,64]{3,1,2,0:T(8,128)S(1)} %pad_maximum_fusion.1, f32[1,64,2,64]{3,1,2,0:T(8,128)S(1)} %get-tuple-element.128, f32[1,64,2,64]{3,1,2,0:T(8,128)S(1)} %get-tuple-element.123), kind=kOutput, calls=%fused_computation.94 | convolution fusion | flops 805322752 | bytes 4259840 | tf_op jit(solution)/shard_map/cksn,sabn->ckab/dot_general | solution.py:46
  355.1 8.7 %fusion.97 = f32[2,64,64,64]{3,1,2,0:T(8,128)S(1)} fusion(f32[2,64,64,64]{3,1,2,0:T(8,128)S(1)} %fusion.94, f32[1,64,2,64]{3,1,2,0:T(8,128)S(1)} %get-tuple-element.128, f32[1,64,2,64]{3,1,2,0:T(8,128)S(1)} %get-tuple-element.123), kind=kOutput, calls=%fused_computation.95 | convolution fusion | flops 805322752 | bytes 4259840 | tf_op jit(solution)/shard_map/cksn,sabn->ckab/dot_general | solution.py:46
  398.2 19.4 %fusion.225 = f32[1,17,17,17]{3,0,2,1:T(1,128)S(1)} fusion(f32[17,17,17,32]{3,2,1,0:T(8,128)} %dot_general.134, f32[32]{0:T(128)S(1)} %fusion.218), kind=kOutput, calls=%fused_computation.276 | convolution fusion | flops 1886592 | bytes 648644 | tf_op jit(solution)/shard_map/bkr,rc->bc/dot_general | solution.py:109
  433.8 8.5 %fusion.106 = f32[2,64,64,64]{3,1,2,0:T(8,128)S(1)} fusion(f32[2,64,64,64]{3,1,2,0:T(8,128)S(1)} %fusion.135, f32[1,64,2,64]{3,1,0,2:T(8,128)S(1)} %get-tuple-element.124, f32[1,64,2,64]{3,1,0,2:T(8,128)S(1)} %get-tuple-element.127), kind=kOutput, calls=%fused_computation.98 | convolution fusion | flops 805322752 | bytes 4259840 | tf_op jit(solution)/shard_map/cksn,sabn->ckab/dot_general | solution.py:40
  442.4 11.2 %fusion.109 = f32[2,64,64,64]{3,1,2,0:T(8,128)} fusion(f32[2,64,64,64]{3,1,2,0:T(8,128)S(1)} %fusion.106, f32[1,64,2,64]{3,1,0,2:T(8,128)S(1)} %get-tuple-element.124, f32[1,64,2,64]{3,1,0,2:T(8,128)S(1)} %get-tuple-element.127), kind=kOutput, calls=%fused_computation.99 | convolution fusion | flops 805322752 | bytes 4259840 | tf_op jit(solution)/shard_map/cksn,sabn->ckab/dot_general | solution.py:40
  491.8 18.5 %dynamic_update_slice.44 = f32[64,64,64]{1,2,0:T(8,128)S(1)} dynamic-update-slice(f32[64,64,64]{1,2,0:T(8,128)S(1)} %dynamic_update_slice.43, f32[48,8,48]{1,2,0:T(8,128)} %copy.287, s32[]{:T(128)} %constant.223.clone.1, s32[]{:T(128)} %constant.214.clone.1, s32[]{:T(128)} %constant.223.clone.1) | dynamic-update-slice | bytes 147460 | tf_op jit(solution)/shard_map/dynamic_update_slice | solution.py:76
  510.3 29.6 %dynamic_update_slice.45 = f32[64,64,64]{1,2,0:T(8,128)S(1)} dynamic-update-slice(f32[64,64,64]{1,2,0:T(8,128)S(1)} %dynamic_update_slice.44, f32[48,8,48]{1,2,0:T(8,128)} %copy.288, s32[]{:T(128)} %constant.223.clone.1, s32[]{:T(128)} %constant.224.clone.1, s32[]{:T(128)} %constant.223.clone.1) | dynamic-update-slice | bytes 147460 | tf_op jit(solution)/shard_map/dynamic_update_slice | solution.py:76
  539.8 15.1 %dynamic_update_slice.46 = f32[64,64,64]{1,2,0:T(8,128)S(1)} dynamic-update-slice(f32[64,64,64]{1,2,0:T(8,128)S(1)} %dynamic_update_slice.45, f32[48,48,8]{1,2,0:T(8,128)} %copy.289, s32[]{:T(128)} %constant.223.clone.1, s32[]{:T(128)} %constant.223.clone.1, s32[]{:T(128)} %constant.214.clone.1) | dynamic-update-slice | bytes 147460 | tf_op jit(solution)/shard_map/dynamic_update_slice | solution.py:76
  554.9 15.2 %dynamic_update_slice.47 = f32[64,64,64]{1,2,0:T(8,128)S(1)} dynamic-update-slice(f32[64,64,64]{1,2,0:T(8,128)S(1)} %dynamic_update_slice.46, f32[48,48,8]{1,2,0:T(8,128)} %copy.290, s32[]{:T(128)} %constant.223.clone.1, s32[]{:T(128)} %constant.223.clone.1, s32[]{:T(128)} %constant.224.clone.1) | dynamic-update-slice | bytes 147460 | tf_op jit(solution)/shard_map/dynamic_update_slice | solution.py:76
  574.5 8.5 %fusion.100 = f32[2,64,64,64]{3,1,2,0:T(8,128)S(1)} fusion(f32[2,64,64,64]{3,1,2,0:T(8,128)S(1)} %fusion.140, f32[1,64,2,64]{3,1,0,2:T(8,128)S(1)} %get-tuple-element.124, f32[1,64,2,64]{3,1,0,2:T(8,128)S(1)} %get-tuple-element.127), kind=kOutput, calls=%fused_computation.96 | convolution fusion | flops 805322752 | bytes 4259840 | tf_op jit(solution)/shard_map/cksn,sabn->ckab/dot_general | solution.py:40
  583.0 8.7 %fusion.103 = f32[2,64,64,64]{3,1,2,0:T(8,128)S(1)} fusion(f32[2,64,64,64]{3,1,2,0:T(8,128)S(1)} %fusion.100, f32[1,64,2,64]{3,1,0,2:T(8,128)S(1)} %get-tuple-element.124, f32[1,64,2,64]{3,1,0,2:T(8,128)S(1)} %get-tuple-element.127), kind=kOutput, calls=%fused_computation.97 | convolution fusion | flops 805322752 | bytes 4259840 | tf_op jit(solution)/shard_map/cksn,sabn->ckab/dot_general | solution.py:40
  593.5 8.9 %fusion.112 = f32[2,64,64,64]{3,1,2,0:T(8,128)S(1)} fusion(f32[2,64,64,64]{3,1,2,0:T(8,128)S(1)} %pad_maximum_fusion.2, f32[1,64,2,64]{3,1,2,0:T(8,128)S(1)} %get-tuple-element.128, f32[1,64,2,64]{3,1,2,0:T(8,128)S(1)} %get-tuple-element.123), kind=kOutput, calls=%fused_computation.100 | convolution fusion | flops 805322752 | bytes 4259840 | tf_op jit(solution)/shard_map/cksn,sabn->ckab/dot_general | solution.py:46
  602.5 8.5 %fusion.115 = f32[2,64,64,64]{3,1,2,0:T(8,128)S(1)} fusion(f32[2,64,64,64]{3,1,2,0:T(8,128)S(1)} %fusion.112, f32[1,64,2,64]{3,1,2,0:T(8,128)S(1)} %get-tuple-element.128, f32[1,64,2,64]{3,1,2,0:T(8,128)S(1)} %get-tuple-element.123), kind=kOutput, calls=%fused_computation.101 | convolution fusion | flops 805322752 | bytes 4259840 | tf_op jit(solution)/shard_map/cksn,sabn->ckab/dot_general | solution.py:46
  628.3 8.7 %fusion.118 = f32[2,64,64,64]{3,1,2,0:T(8,128)S(1)} fusion(f32[2,64,64,64]{3,1,2,0:T(8,128)S(1)} %fusion.138, f32[1,64,2,64]{3,1,0,2:T(8,128)S(1)} %get-tuple-element.124, f32[1,64,2,64]{3,1,0,2:T(8,128)S(1)} %get-tuple-element.127), kind=kOutput, calls=%fused_computation.102 | convolution fusion | flops 805322752 | bytes 4259840 | tf_op jit(solution)/shard_map/cksn,sabn->ckab/dot_general | solution.py:40
  637.0 8.5 %fusion.121 = f32[2,64,64,64]{3,1,2,0:T(8,128)S(1)} fusion(f32[2,64,64,64]{3,1,2,0:T(8,128)S(1)} %fusion.118, f32[1,64,2,64]{3,1,0,2:T(8,128)S(1)} %get-tuple-element.124, f32[1,64,2,64]{3,1,0,2:T(8,128)S(1)} %get-tuple-element.127), kind=kOutput, calls=%fused_computation.103 | convolution fusion | flops 805322752 | bytes 4259840 | tf_op jit(solution)/shard_map/cksn,sabn->ckab/dot_general | solution.py:40
  648.2 8.5 %fusion.124 = f32[2,64,64,64]{3,1,2,0:T(8,128)S(1)} fusion(f32[2,64,64,64]{3,1,2,0:T(8,128)S(1)} %pad_maximum_fusion.3, f32[1,64,2,64]{3,1,2,0:T(8,128)S(1)} %get-tuple-element.128, f32[1,64,2,64]{3,1,2,0:T(8,128)S(1)} %get-tuple-element.123), kind=kOutput, calls=%fused_computation.104 | convolution fusion | flops 805322752 | bytes 4259840 | tf_op jit(solution)/shard_map/cksn,sabn->ckab/dot_general | solution.py:46
  656.8 8.7 %fusion.127 = f32[2,64,64,64]{3,1,2,0:T(8,128)S(1)} fusion(f32[2,64,64,64]{3,1,2,0:T(8,128)S(1)} %fusion.124, f32[1,64,2,64]{3,1,2,0:T(8,128)S(1)} %get-tuple-element.128, f32[1,64,2,64]{3,1,2,0:T(8,128)S(1)} %get-tuple-element.123), kind=kOutput, calls=%fused_computation.105 | convolution fusion | flops 805322752 | bytes 4259840 | tf_op jit(solution)/shard_map/cksn,sabn->ckab/dot_general | solution.py:46
  (289 shorter events, 238.2 us)
Async XLA Ops:
  0.0 88.0 %copy-start = (s32[32]{0:T(128)S(1)}, s32[32]{0:T(128)}, u32[]{:S(2)}) copy-start(s32[32]{0:T(128)} %param.29) | copy-start | bytes 388
  7.7 9.2 %copy-start.54 = (s32[6]{0:T(128)S(1)}, s32[6]{0:T(128)}, u32[]{:S(2)}) copy-start(s32[6]{0:T(128)} %param.30) | copy-start | bytes 76
  9.5 153.5 %all-to-all-start = ((bf16[32,2,9216]{2,1,0:T(2,128)(2,1)}), bf16[32,2,9216]{2,1,0:T(2,128)(2,1)}, u32[]{:S(2)}, u32[]{:S(2)}) async-start(bf16[32,2,9216]{2,1,0:T(2,128)(2,1)} %reshape.1300), calls=%async_computation | async-start | bytes 2359296 | tf_op jit(solution)/shard_map/all_to_all | solution.py:175
  107.4 5.1 copy-start.35
  127.1 5.5 copy-start.47
  130.0 5.0 copy-start.59
  135.0 8.2 %copy-start.17 = (f32[2,64,64,1]{2,1,3,0:T(8,128)}, f32[2,64,64,1]{2,1,3,0:T(8,128)S(1)}, u32[]{:S(2)}) copy-start(f32[2,64,64,1]{2,1,3,0:T(8,128)S(1)} %fusion.183) | copy-start | bytes 98308
  135.1 36.8 %copy-start.48 = (pred[6]{0:T(512)(128)(4,1)}, pred[6]{0:T(512)(128)(4,1)S(1)}, u32[]{:S(2)}) copy-start(pred[6]{0:T(512)(128)(4,1)S(1)} %get-tuple-element.130) | copy-start | bytes 22
  172.0 8.6 %copy-start.6 = (f32[64,64,64]{2,1,0:T(8,128)S(1)}, f32[64,64,64]{2,1,0:T(8,128)}, u32[]{:S(2)}) copy-start(f32[64,64,64]{2,1,0:T(8,128)} %scatter.20) | copy-start | bytes 3145732
  239.1 29.7 %copy-start.18 = (f32[2,64,64,1]{2,1,3,0:T(8,128)S(1)}, f32[2,64,64,1]{2,1,3,0:T(8,128)}, u32[]{:S(2)}) copy-start(f32[2,64,64,1]{2,1,3,0:T(8,128)} %copy-done.17) | copy-start | bytes 98308
  284.0 8.8 %copy-start.4 = (f32[2,64,64,64]{3,1,2,0:T(8,128)S(1)}, f32[2,64,64,64]{3,1,2,0:T(8,128)}, u32[]{:S(2)}) copy-start(f32[2,64,64,64]{3,1,2,0:T(8,128)} %fusion.79) | copy-start | bytes 6291460
  303.6 8.6 %copy-start.23 = (f32[64,1,64]{2,0,1:T(8,128)S(1)}, f32[64,1,64]{2,0,1:T(8,128)}, u32[]{:S(2)}) copy-start(f32[64,1,64]{2,0,1:T(8,128)} %copy-done.22) | copy-start | bytes 49156
  303.6 8.6 %copy-start.27 = (f32[64,1,64]{2,0,1:T(8,128)S(1)}, f32[64,1,64]{2,0,1:T(8,128)}, u32[]{:S(2)}) copy-start(f32[64,1,64]{2,0,1:T(8,128)} %copy-done.26) | copy-start | bytes 49156
  335.7 8.9 %copy-start.5 = (f32[2,64,64,64]{3,1,2,0:T(8,128)S(1)}, f32[2,64,64,64]{3,1,2,0:T(8,128)}, u32[]{:S(2)}) copy-start(f32[2,64,64,64]{3,1,2,0:T(8,128)} %fusion.79) | copy-start | bytes 6291460
  376.9 4.8 copy-start.10
  377.2 4.5 copy-start.12
  385.2 6.2 copy-start.20
  388.0 71.5 %all-to-all-start.1 = ((bf16[32,2,9216]{2,1,0:T(2,128)(2,1)}), bf16[32,2,9216]{2,1,0:T(2,128)(2,1)}, u32[]{:S(2)}, u32[]{:S(2)}) async-start(bf16[32,2,9216]{2,1,0:T(2,128)(2,1)} %reshape.1302), calls=%async_computation.1 | async-start | bytes 2359296 | tf_op jit(solution)/shard_map/all_to_all | solution.py:175
  393.4 4.6 copy-start.56
  442.4 11.3 %copy-start.43 = (bf16[1,48,8,48]{3,2,1,0:T(8,128)(2,1)S(1)}, bf16[1,48,8,48]{3,2,1,0:T(8,128)(2,1)}, u32[]{:S(2)}) copy-start(bf16[1,48,8,48]{3,2,1,0:T(8,128)(2,1)} %copy-done.42) | copy-start | bytes 110596
  442.4 11.4 %copy-start.45 = (bf16[1,48,8,48]{3,2,1,0:T(8,128)(2,1)S(1)}, bf16[1,48,8,48]{3,2,1,0:T(8,128)(2,1)}, u32[]{:S(2)}) copy-start(bf16[1,48,8,48]{3,2,1,0:T(8,128)(2,1)} %copy-done.44) | copy-start | bytes 110596
  442.4 11.6 %copy-start.11 = (bf16[1,48,48,8]{3,2,1,0:T(8,128)(2,1)S(1)}, bf16[1,48,48,8]{3,2,1,0:T(8,128)(2,1)}, u32[]{:S(2)}) copy-start(bf16[1,48,48,8]{3,2,1,0:T(8,128)(2,1)} %copy-done.10) | copy-start | bytes 110596
  442.4 12.2 %copy-start.13 = (bf16[1,48,48,8]{3,2,1,0:T(8,128)(2,1)S(1)}, bf16[1,48,48,8]{3,2,1,0:T(8,128)(2,1)}, u32[]{:S(2)}) copy-start(bf16[1,48,48,8]{3,2,1,0:T(8,128)(2,1)} %copy-done.12) | copy-start | bytes 110596
  442.4 12.8 %copy-start.31 = (bf16[1,8,48,48]{3,2,1,0:T(8,128)(2,1)S(1)}, bf16[1,8,48,48]{3,2,1,0:T(8,128)(2,1)}, u32[]{:S(2)}) copy-start(bf16[1,8,48,48]{3,2,1,0:T(8,128)(2,1)} %copy-done.30) | copy-start | bytes 110596
  442.4 12.9 %copy-start.33 = (bf16[1,8,48,48]{3,2,1,0:T(8,128)(2,1)S(1)}, bf16[1,8,48,48]{3,2,1,0:T(8,128)(2,1)}, u32[]{:S(2)}) copy-start(bf16[1,8,48,48]{3,2,1,0:T(8,128)(2,1)} %copy-done.32) | copy-start | bytes 110596
  476.3 7.3 %copy-start.7 = (f32[64,64,64]{1,2,0:T(8,128)S(1)}, f32[64,64,64]{1,2,0:T(8,128)}, u32[]{:S(2)}) copy-start(f32[64,64,64]{1,2,0:T(8,128)} %scatter.25) | copy-start | bytes 3145732
  583.0 8.7 %copy-start.2 = (f32[2,64,64,64]{3,1,2,0:T(8,128)S(1)}, f32[2,64,64,64]{3,1,2,0:T(8,128)}, u32[]{:S(2)}) copy-start(f32[2,64,64,64]{3,1,2,0:T(8,128)} %fusion.109) | copy-start | bytes 6291460
  602.5 8.5 %copy-start.24 = (f32[64,1,64]{2,0,1:T(8,128)S(1)}, f32[64,1,64]{2,0,1:T(8,128)}, u32[]{:S(2)}) copy-start(f32[64,1,64]{2,0,1:T(8,128)} %copy-done.22) | copy-start | bytes 49156
  602.5 8.5 %copy-start.28 = (f32[64,1,64]{2,0,1:T(8,128)S(1)}, f32[64,1,64]{2,0,1:T(8,128)}, u32[]{:S(2)}) copy-start(f32[64,1,64]{2,0,1:T(8,128)} %copy-done.26) | copy-start | bytes 49156
  637.0 8.6 %copy-start.3 = (f32[2,64,64,64]{3,1,2,0:T(8,128)S(1)}, f32[2,64,64,64]{3,1,2,0:T(8,128)}, u32[]{:S(2)}) copy-start(f32[2,64,64,64]{3,1,2,0:T(8,128)} %fusion.109) | copy-start | bytes 6291460
  656.8 8.8 %copy-start.25 = (f32[64,1,64]{2,0,1:T(8,128)S(1)}, f32[64,1,64]{2,0,1:T(8,128)}, u32[]{:S(2)}) copy-start(f32[64,1,64]{2,0,1:T(8,128)} %copy-done.22) | copy-start | bytes 49156
  656.8 8.8 %copy-start.29 = (f32[64,1,64]{2,0,1:T(8,128)S(1)}, f32[64,1,64]{2,0,1:T(8,128)}, u32[]{:S(2)}) copy-start(f32[64,1,64]{2,0,1:T(8,128)} %copy-done.26) | copy-start | bytes 49156
  (30 other events, 84.1 us)
where the time goes:
time: 686 us; the launch traced here: 677 us
  local copies, waits for them, and re-layouts  290 us (42%)
  matrix products  284 us (41%)
  blocking collectives  51.4 us (7%)
  other arithmetic  35.4 us (5%)
  starting transfers between devices  10.8 us (2%)
    dynamic_update_slice x12, local copies, waits for them, and re-layouts, assemble(): padded = lax.dynamic_update_slice(padded, slab_now, start_now)  175 us
    dot_general x12, matrix products, forward(): pair = jnp.einsum('cksn,sabn->ckab', forward_table, pair, precision=HIGHEST)  109 us
    dot_general x8, matrix products, inverse_real(): pair = jnp.einsum('cksn,sabn->ckab', inverse_table, pair, precision=HIGHEST)  69.4 us
    all_gather x1, blocking collectives, local(): lax.all_gather(stacked_cells.astype(jnp.bfloat16), 'blk', axis=0, tiled=T...  51.4 us
    dot_general x2, matrix products, blend_cells(): return running + jnp.einsum('bkr,rc->bc', picks, scaled, precision=HIGHEST)  36.9 us
    dot_general x6, matrix products, forward(): jnp.einsum('ckn,abn->ckab', forward_table[:, :, 0, :], values_in, precisi...  33.8 us
    dot_general x4, matrix products, inverse_real(): jnp.einsum('ksn,sabn->kab', inverse_table[0], pair, precision=HIGHEST)  33 us
    unnamed x131, local copies, waits for them, and re-layouts  28.8 us
  transfers between devices with their start and end apart: 2, of which 0 were waited for; matrix products, arithmetic and copies ran while one was open for 23% of the time, Pallas kernels for 0%

commit v1 on v0

v1 whole, which is shorter than its diff:
```python
import numpy as np

import jax
import jax.numpy as jnp
import ml_dtypes
from jax import lax
from jax.experimental import pallas as pl
from jax.experimental.pallas import tpu as pltpu
from jax.sharding import PartitionSpec as P

E = 48
MARGIN = 8
UPDATES = 2
PAD = 64
KS = 17
KS2 = KS * KS
KS3 = 4913
SLOTS = 16
LANES = 256
TAPROWS = 32
CELLPAD = 5120
FLAT = 864

F32 = jnp.float32
BF16 = jnp.bfloat16


def two_terms(table):
    high = table.astype(ml_dtypes.bfloat16)
    low = (table - high.astype(np.float64)).astype(ml_dtypes.bfloat16)
    return high, low


def stacked(table, axis):
    high, low = two_terms(table)
    return np.concatenate([high, high, low], axis=axis)


def x_positions():
    x = np.arange(PAD)
    return np.where(x < PAD - MARGIN, x, x - PAD)


def table_space_to_lines():
    z4, k4, kx = np.arange(4), np.arange(4), np.arange(32)
    angle = -2.0 * np.pi * (
        z4[:, None, None, None] * k4[None, None, :, None] / 4.0
        + (kx[None, None, None, :] + 0.5) * x_positions()[None, :, None, None] / PAD
    )
    angle = angle.reshape(LANES, 128)
    return np.concatenate([np.cos(angle), np.sin(angle)], axis=1)


def table_lines_to_space():
    back = table_space_to_lines().T.copy()
    back = back.reshape(LANES, 4, PAD)
    back[:, 3, :] = 0.0
    back[:, :, E:] = 0.0
    return back.reshape(LANES, LANES)


def complex_rows(angle):
    cosine, sine = np.cos(angle), np.sin(angle)
    return np.concatenate(
        [np.concatenate([cosine, -sine], axis=1), np.concatenate([sine, cosine], axis=1)], axis=0
    )


def table_y(count):
    ky, y = np.arange(PAD), np.arange(count)
    return complex_rows(-2.0 * np.pi * (ky[:, None] * y[None, :] % PAD) / PAD)


def table_y_back():
    ky, y = np.arange(PAD), np.arange(E)
    return complex_rows(2.0 * np.pi * (y[:, None] * ky[None, :] % PAD) / PAD)


def table_y_taps():
    ky, tap = np.arange(PAD), np.arange(TAPROWS) - MARGIN
    angle = -2.0 * np.pi * ky[:, None] * tap[None, :] / PAD
    return complex_rows(angle)


def table_taps(z4):
    k4, kx = np.arange(4), np.arange(32)
    tap_x = np.arange(384) % KS - MARGIN
    angle = -2.0 * np.pi * (
        z4 * k4[None, :, None] / 4.0 + (kx[None, None, :] + 0.5) * tap_x[:, None, None] / PAD
    )
    angle = angle.reshape(384, 128)
    table = np.concatenate([np.cos(angle), np.sin(angle)], axis=1)
    table[KS2:] = 0.0
    return table


def table_tap_mask():
    place = np.arange(384)
    return (place[None, :] // KS == np.arange(TAPROWS)[:, None]).astype(np.float32) * (
        place[None, :] < KS2
    )


def table_twiddle():
    k4 = np.repeat(np.arange(4), 32)
    angle = -2.0 * np.pi * np.arange(SLOTS)[:, None] * k4[None, :] / PAD
    both = np.stack([np.cos(angle), np.sin(angle)], axis=0)
    return np.broadcast_to(both[:, :, None, :], (2, SLOTS, 8, 128)).astype(np.float32)


def table_pack_x():
    table = np.zeros((4, 4, PAD, 2, 4, 4, MARGIN), np.float32)
    for group in range(4):
        for z4 in range(3):
            for step in range(MARGIN):
                table[group, z4, step, 0, group, z4, step] = 1.0
                table[group, z4, E - MARGIN + step, 1, group, z4, step] = 1.0
    return table.reshape(4 * LANES, LANES).astype(ml_dtypes.bfloat16)


def table_unpack_x():
    table = np.zeros((2, 4, 4, MARGIN, 4, 4, PAD), np.float32)
    for group in range(4):
        for z4 in range(3):
            for step in range(MARGIN):
                table[0, group, z4, step, group, z4, PAD - MARGIN + step] = 1.0
                table[1, group, z4, step, group, z4, E + step] = 1.0
    return table.reshape(LANES, 4 * LANES).astype(ml_dtypes.bfloat16)


def split(value):
    high = value.astype(BF16)
    low = (value - high.astype(F32)).astype(BF16)
    return high, low


def dot(left, right):
    return jnp.dot(left, right, preferred_element_type=F32)


def both_halves(rows_ref, rows):
    return jnp.concatenate([rows_ref[0, rows, :], rows_ref[1, rows, :]], axis=1)


def lane_iota(shape):
    return lax.broadcasted_iota(jnp.int32, shape, 1)


def cut(pieces, piece, target):
    offset = E * piece
    first, start = offset // 128, offset % 128
    shift = (target - start) % 128
    one = pltpu.roll(pieces[first], shift, 1) if shift else pieces[first]
    if start + E <= 128:
        return one
    two = pltpu.roll(pieces[first + 1], shift, 1) if shift else pieces[first + 1]
    edge = target + 128 - start
    return jnp.where(lane_iota(one.shape) < edge, one, two)


def unflatten(flat_ref, out_ref):
    lane = lane_iota((8, 128))
    zero = jnp.zeros((8, 128), F32)
    for block in range(12):
        parts = []
        for z4 in range(3):
            first = 3 * (96 * z4 + 8 * block)
            parts.append([flat_ref[pl.ds(first + m, 8, stride=3), :] for m in range(3)])
        for piece in range(8):
            low = cut(parts[0], piece, 0)
            mid = cut(parts[1], piece, 64)
            top = cut(parts[2], piece, 0)
            left = jnp.where(lane < E, low, jnp.where(lane < 64, zero, mid))
            left = jnp.where(lane < 64 + E, left, zero)
            rows = pl.ds(64 * block + piece, 8, stride=8)
            out_ref[0, rows, :] = left
            out_ref[1, rows, :] = jnp.where(lane < E, top, zero)


def flatten(rows_ref, flat_ref):
    lane = lane_iota((8, 128))
    for block in range(12):
        found = []
        for piece in range(8):
            rows = pl.ds(64 * block + piece, 8, stride=8)
            found.append((rows_ref[0, rows, :], rows_ref[1, rows, :]))
        for z4 in range(3):
            first = 3 * (96 * z4 + 8 * block)
            out = [None, None, None]
            for piece in range(8):
                value = found[piece][0] if z4 < 2 else found[piece][1]
                source = 64 if z4 == 1 else 0
                offset = E * piece
                spot, start = offset // 128, offset % 128
                shift = (start - source) % 128
                moved = pltpu.roll(value, shift, 1) if shift else value
                if out[spot] is None:
                    out[spot] = moved
                else:
                    out[spot] = jnp.where(lane < start, out[spot], moved)
                if start + E > 128:
                    out[spot + 1] = moved
            for m in range(3):
                flat_ref[pl.ds(first + m, 8, stride=3), :] = out[m]


def pack_slabs(rows_ref, pack_x, x0, x1, y0, y1, z0, z1):
    high = both_halves(rows_ref, slice(None)).astype(BF16)
    wide = jnp.concatenate([high[192 * g : 192 * (g + 1)] for g in range(4)], axis=1)
    both = dot(wide, pack_x[...]).astype(BF16)
    x0[...] = both[:, 0:128]
    x1[...] = both[:, 128:256]
    low_rows, high_rows = [], []
    for slot in range(SLOTS):
        low_rows.append(both_halves(rows_ref, slice(E * slot, E * slot + MARGIN)))
        high_rows.append(both_halves(rows_ref, slice(E * slot + E - MARGIN, E * (slot + 1))))
    y0[...] = jnp.concatenate(low_rows, axis=0).astype(BF16)
    y1[...] = jnp.concatenate(high_rows, axis=0).astype(BF16)
    lane = lane_iota((192, 128))
    first = rows_ref[0, 0:192, :]
    second = pltpu.roll(rows_ref[0, 192:384, :], 64, 1)
    z0[...] = jnp.where(lane < 64, first, second).astype(BF16)
    first = rows_ref[1, 384:576, :]
    second = pltpu.roll(rows_ref[1, 576:768, :], 64, 1)
    z1[...] = jnp.where(lane < 64, first, second).astype(BF16)


def assemble(present, rows_ref, unpack_x, margins, high_ref, low_ref):
    zm, zp, ym, yp, xm, xp = margins
    on = [present[0, face] >= 0 for face in range(6)]
    zero_x = jnp.zeros((192, 128), BF16)
    wide = jnp.concatenate(
        [jnp.where(on[4], xm[...], zero_x), jnp.where(on[5], xp[...], zero_x)], axis=1
    )
    side = dot(wide, unpack_x[...])
    scale = [jnp.where(on[face], 1.0, 0.0).astype(F32) for face in range(6)]
    yp_rows = yp[...].astype(F32) * scale[3]
    ym_rows = ym[...].astype(F32) * scale[2]
    z_sides = []
    for ref, face in ((zp, 1), (zm, 0)):
        value = ref[...].astype(F32) * scale[face]
        z_sides.append(pltpu.roll(value, 64, 1))
        z_sides.append(value)
    lane = lane_iota((E, 128))
    for slot in range(SLOTS):
        group, inner = slot // 4, slot % 4
        core = both_halves(rows_ref, slice(E * slot, E * (slot + 1)))
        high, low = split(core)
        added = side[E * inner : E * (inner + 1), LANES * group : LANES * (group + 1)]
        full = high.astype(F32) + added
        z_side = z_sides[group][E * inner : E * (inner + 1), :]
        right = jnp.where(lane < 64, full[:, 128:256], z_side)
        high_ref[PAD * slot : PAD * slot + E, 0:128] = full[:, 0:128].astype(BF16)
        high_ref[PAD * slot : PAD * slot + E, 128:256] = right.astype(BF16)
        rows = slice(MARGIN * slot, MARGIN * (slot + 1))
        outer = jnp.concatenate([yp_rows[rows], ym_rows[rows]], axis=0)
        high_ref[PAD * slot + E : PAD * (slot + 1), :] = outer.astype(BF16)
        low_ref[PAD * slot : PAD * slot + E, :] = low
        low_ref[PAD * slot + E : PAD * (slot + 1), :] = jnp.zeros((PAD - E, LANES), BF16)


def lines_stage(high, low, table, out_ref, rows, step):
    for start in range(0, rows, step):
        part = slice(start, start + step)
        wide = jnp.concatenate([high[part, :], low[part, :], high[part, :]], axis=1)
        out_ref[part, :] = dot(wide, table[...])


def y_stage(lines_ref, table, count, out_ref):
    for pair in range(SLOTS // 2):
        one = lines_ref[count * 2 * pair : count * (2 * pair + 1), :]
        two = lines_ref[count * (2 * pair + 1) : count * (2 * pair + 2), :]
        real = jnp.concatenate([one[:, 0:128], two[:, 0:128]], axis=1)
        imag = jnp.concatenate([one[:, 128:256], two[:, 128:256]], axis=1)
        high, low = split(jnp.concatenate([real, imag], axis=0))
        out = dot(table[...], jnp.concatenate([high, low, high], axis=0))
        out_ref[2 * pair] = out[:, 0:128]
        out_ref[2 * pair + 1] = out[:, 128:256]


def y_back_stage(planes_ref, table, out_ref):
    for pair in range(SLOTS // 2):
        both = jnp.concatenate([planes_ref[2 * pair], planes_ref[2 * pair + 1]], axis=1)
        high, low = split(both)
        out = dot(table[...], jnp.concatenate([high, low, high], axis=0))
        for which in range(2):
            rows = slice(E * (2 * pair + which), E * (2 * pair + which + 1))
            lanes = slice(128 * which, 128 * (which + 1))
            out_ref[rows, 0:128] = out[0:E, lanes]
            out_ref[rows, 128:256] = out[E : 2 * E, lanes]


def turn(value, cosine, sine):
    real, imag = value
    return real * cosine - imag * sine, real * sine + imag * cosine


def dft4(values, sign):
    (ar, ai), (br, bi), (cr, ci), (dr, di) = values
    sr, si, mr, mi = ar + cr, ai + ci, ar - cr, ai - ci
    pr, pi, qr, qi = br + dr, bi + di, br - dr, bi - di
    if sign > 0:
        first, third = (mr - qi, mi + qr), (mr + qi, mi - qr)
    else:
        first, third = (mr + qi, mi - qr), (mr - qi, mi + qr)
    return [(sr + pr, si + pi), first, (sr - pr, si - pi), third]


def dft16(values, sign):
    inner = []
    for low in range(4):
        line = dft4([values[4 * top + low] for top in range(4)], sign)
        moved = []
        for k in range(4):
            turns = low * k
            real, imag = line[k]
            if turns == 0:
                moved.append((real, imag))
            elif turns == 4:
                moved.append((-imag, real) if sign > 0 else (imag, -real))
            elif turns in (2, 6):
                root = float(np.sqrt(0.5))
                a, b = root * real, root * imag
                if turns == 2:
                    moved.append((a - b, a + b) if sign > 0 else (a + b, b - a))
                else:
                    moved.append((-a - b, a - b) if sign > 0 else (b - a, -a - b))
            else:
                angle = sign * 2.0 * np.pi * turns / SLOTS
                moved.append(turn((real, imag), float(np.cos(angle)), float(np.sin(angle))))
        inner.append(moved)
    out = [None] * SLOTS
    for k in range(4):
        line = dft4([inner[low][k] for low in range(4)], sign)
        for top in range(4):
            out[k + 4 * top] = line[top]
    return out


def z_forward(planes_ref, twiddle, rows, rows_imag):
    values = []
    for slot in range(SLOTS):
        value = (planes_ref[slot, rows, :], planes_ref[slot, rows_imag, :])
        if slot:
            value = turn(value, twiddle[0, slot], twiddle[1, slot])
        values.append(value)
    return dft16(values, -1)


def z_stage(planes_ref, twiddle, out_ref):
    @pl.loop(0, PAD // 8)
    def _(step):
        rows = pl.ds(pl.multiple_of(8 * step, 8), 8)
        rows_imag = pl.ds(pl.multiple_of(8 * step + PAD, 8), 8)
        values = z_forward(planes_ref, twiddle, rows, rows_imag)
        for slot in range(SLOTS):
            out_ref[slot, rows, :] = values[slot][0]
            out_ref[slot, rows_imag, :] = values[slot][1]


def filter_stage(planes_ref, kernel_ref, twiddle, conjugate, out_ref):
    @pl.loop(0, PAD // 8)
    def _(step):
        rows = pl.ds(pl.multiple_of(8 * step, 8), 8)
        rows_imag = pl.ds(pl.multiple_of(8 * step + PAD, 8), 8)
        values = z_forward(planes_ref, twiddle, rows, rows_imag)
        for slot in range(SLOTS):
            cosine, sine = kernel_ref[slot, rows, :], kernel_ref[slot, rows_imag, :]
            if conjugate:
                real, imag = values[slot]
                values[slot] = (real * cosine + imag * sine, imag * cosine - real * sine)
            else:
                values[slot] = turn(values[slot], cosine, sine)
        values = dft16(values, 1)
        for slot in range(SLOTS):
            real, imag = values[slot]
            if slot:
                cosine, sine = twiddle[0, slot], twiddle[1, slot]
                real, imag = real * cosine + imag * sine, imag * cosine - real * sine
            out_ref[slot, rows, :] = real
            out_ref[slot, rows_imag, :] = imag


def tap_stage(flat, mask, table0, table3, table_y_ref, planes_ref):
    lines = []
    for tap in range(KS):
        offset = KS2 * tap
        start = offset // 128 * 128
        shift = offset - start
        window = flat[:, start : start + 512]
        if shift:
            window = pltpu.roll(window, 512 - shift, 1)
        lines.append(window[:, 0:384])
    spread = []
    for line in lines:
        spread.append(jnp.broadcast_to(line, (TAPROWS, 384)) * mask)

    def first_stage(taps, table):
        high, low = split(jnp.concatenate(taps, axis=0))
        return dot(jnp.concatenate([high, low, high], axis=1), table[...])

    ahead = first_stage(spread[MARGIN:], table0)
    behind = first_stage(spread[:MARGIN], table3)
    slots = []
    for slot in range(MARGIN):
        slots.append(ahead[TAPROWS * slot : TAPROWS * (slot + 1)])
    slots.append(ahead[TAPROWS * MARGIN :] + behind[0:TAPROWS])
    for slot in range(MARGIN + 1, SLOTS):
        at = slot - MARGIN
        slots.append(behind[TAPROWS * at : TAPROWS * (at + 1)])
    for pair in range(SLOTS // 2):
        one, two = slots[2 * pair], slots[2 * pair + 1]
        real = jnp.concatenate([one[:, 0:128], two[:, 0:128]], axis=1)
        imag = jnp.concatenate([one[:, 128:256], two[:, 128:256]], axis=1)
        high, low = split(jnp.concatenate([real, imag], axis=0))
        out = dot(table_y_ref[...], jnp.concatenate([high, low, high], axis=0))
        planes_ref[2 * pair] = out[:, 0:128]
        planes_ref[2 * pair + 1] = out[:, 128:256]


def spectrum_body(update, order, lists, blend, cell_row, cells, mask, table0, table3, table_y_ref, twiddle, out_ref, got, planes, sems):
    view = order[update]
    copies = []
    for k in range(2):
        row = cell_row[lists[0, view, k]]
        copy = pltpu.make_async_copy(cells.at[row], got.at[k], sems.at[k])
        copy.start()
        copies.append(copy)
    for copy in copies:
        copy.wait()
    total = blend[0, view, 0] + blend[0, view, 1]
    flat = None
    for k in range(2):
        line = got[k].astype(F32)[update : update + 1, :]
        weight = blend[0, view, k] / total * (2.0 / float(PAD**3))
        part = line * (weight / jnp.sum(line, axis=1, keepdims=True))
        flat = part if flat is None else flat + part
    tap_stage(flat, mask[...], table0, table3, table_y_ref, planes)
    z_stage(planes, twiddle, out_ref)


def prep_kernel(est, obs0, obs1, pack_x, u_out, o0_out, o1_out, z0, z1, y0, y1, x0, x1):
    unflatten(est, u_out)
    pack_slabs(u_out, pack_x, x0, x1, y0, y1, z0, z1)
    unflatten(obs0, o0_out)
    unflatten(obs1, o1_out)


def field_kernel(present, u, zm, zp, ym, yp, xm, xp, unpack_x, ea, gy, out, high, low, lines):
    assemble(present, u, unpack_x, (zm, zp, ym, yp, xm, xp), high, low)
    lines_stage(high, low, ea, lines, SLOTS * PAD, 256)
    y_stage(lines, gy, PAD, out)


def update_body(tissue, planes, kernel, u, o, tables, scratch, new_ref):
    ea, ei, gh, gb, twiddle = tables
    planes2, lines = scratch
    filter_stage(planes, kernel, twiddle, False, planes2)
    y_back_stage(planes2, gb, lines)
    rows = SLOTS * E
    lane = lane_iota((rows, LANES))
    valid = (lane % PAD < E) & (lane < 3 * PAD)
    high, low = split(lines[...])
    blurred = dot(jnp.concatenate([high, low, high], axis=1), ei[...])
    quotient = jnp.where(valid, both_halves(o, slice(None)) / blurred, 0.0)
    high, low = split(quotient)
    lines[...] = dot(jnp.concatenate([high, low, high], axis=1), ea[...])
    y_stage(lines, gh, E, planes2)
    filter_stage(planes2, kernel, twiddle, True, planes2)
    y_back_stage(planes2, gb, lines)
    high, low = split(lines[...])
    correction = dot(jnp.concatenate([high, low, high], axis=1), ei[...])
    alive = tissue[0] > 0
    for half in range(2):
        core = u[half]
        new_ref[half] = jnp.where(alive, core * correction[:, 128 * half : 128 * (half + 1)], core)


def spectrum_kernel(update, *refs):
    spectrum_body(update, *refs)


def first_kernel(tissue, planes, kernel, u, o, ea, ei, gh, gb, twiddle, pack_x, u_out, z0, z1, y0, y1, x0, x1, planes2, lines):
    update_body(tissue, planes, kernel, u, o, (ea, ei, gh, gb, twiddle), (planes2, lines), u_out)
    pack_slabs(u_out, pack_x, x0, x1, y0, y1, z0, z1)


def last_kernel(tissue, planes, kernel, u, o, ea, ei, gh, gb, twiddle, out, planes2, lines, fresh):
    update_body(tissue, planes, kernel, u, o, (ea, ei, gh, gb, twiddle), (planes2, lines), fresh)
    flatten(fresh, out)


VM = pl.BlockSpec(memory_space=pltpu.VMEM)
SM = pl.BlockSpec(memory_space=pltpu.SMEM)
ANY = pl.BlockSpec(memory_space=pl.ANY)
PARAMS = pltpu.CompilerParams(vmem_limit_bytes=48 * 1024 * 1024)


def shape(dims, kind=F32):
    return jax.ShapeDtypeStruct(dims, kind)


SLABS = [shape((192, 128), BF16)] * 2 + [shape((128, 256), BF16)] * 2 + [shape((192, 128), BF16)] * 2
ROWS = shape((2, SLOTS * E, 128))
ROWS_V = pltpu.VMEM((2, SLOTS * E, 128), F32)
PLANES = shape((SLOTS, 128, 128))
PLANES_V = pltpu.VMEM((SLOTS, 128, 128), F32)
LINES_V = pltpu.VMEM((SLOTS * E, LANES), F32)


def call(body, ins, outs, args, scratch=(), name=None):
    many = isinstance(outs, list)
    return pl.pallas_call(
        body,
        in_specs=ins,
        out_specs=[VM] * len(outs) if many else VM,
        out_shape=outs,
        scratch_shapes=list(scratch),
        compiler_params=PARAMS,
        name=name,
    )(*args)


def neighbour_pairs(count):
    low_count = count.bit_length() - 2
    places = []
    for number in range(count):
        at = [0, 0, 0]
        for bit in range(low_count):
            at[bit % 3] += number // 2**bit % 2 * 2 ** (bit // 3)
        at[2] = 2 * at[2] + number // 2**low_count % 2
        places.append(tuple(at))
    number_at = {at: number for number, at in enumerate(places)}
    pairs = []
    for face in range(6):
        axis, step = face // 2, -1 if face % 2 == 0 else 1
        found = []
        for number, at in enumerate(places):
            moved = list(at)
            moved[axis] += step
            if tuple(moved) in number_at:
                found.append((number_at[tuple(moved)], number))
        pairs.append(found)
    return pairs


def exchange(slabs, pairs):
    out = []
    for face in range(6):
        sent = slabs[face ^ 1]
        out.append(lax.ppermute(sent, "blk", pairs[face]) if pairs[face] else jnp.zeros_like(sent))
    return out


def local(estimate, observed, psf_cells, tissue, neighbours, psf_list, psf_blend, cell_row, view_order):
    count = lax.axis_size("blk")
    pairs = neighbour_pairs(count)
    ea = jnp.asarray(stacked(table_space_to_lines(), 0))
    ei = jnp.asarray(stacked(table_lines_to_space(), 0))
    gy = jnp.asarray(stacked(table_y(PAD), 1))
    gh = jnp.asarray(stacked(table_y(E), 1))
    gb = jnp.asarray(stacked(table_y_back(), 1))
    gt = jnp.asarray(stacked(table_y_taps(), 1))
    taps0 = jnp.asarray(stacked(table_taps(0), 0))
    taps3 = jnp.asarray(stacked(table_taps(3), 0))
    mask = jnp.asarray(table_tap_mask().astype(np.float32))
    twiddle = jnp.asarray(table_twiddle())
    pack_x = jnp.asarray(table_pack_x())
    unpack_x = jnp.asarray(table_unpack_x())

    views = jnp.concatenate(
        [lax.dynamic_slice_in_dim(psf_cells[0], view_order[u], 1, 0) for u in range(UPDATES)], axis=0
    )
    views = jnp.pad(views.astype(BF16), ((0, 0), (0, CELLPAD - KS3)))
    cells = lax.all_gather(views, "blk", axis=0, tiled=False)

    seen = [
        lax.dynamic_index_in_dim(observed[0], view_order[u], 0, keepdims=False).astype(F32).reshape(FLAT, 128)
        for u in range(UPDATES)
    ]
    flat = estimate.reshape(FLAT, 128)
    prep = call(
        prep_kernel, [VM] * 4, [ROWS, ROWS, ROWS] + SLABS, (flat, seen[0], seen[1], pack_x), name="prep"
    )
    rows, targets, slabs = prep[0], prep[1:3], prep[3:]

    def spectrum(update):
        return call(
            lambda *refs: spectrum_kernel(update, *refs),
            [SM] * 4 + [ANY] + [VM] * 5,
            PLANES,
            (view_order, psf_list, psf_blend, cell_row, cells, mask, taps0, taps3, gt, twiddle),
            [pltpu.VMEM((2, 2, CELLPAD), BF16), PLANES_V, pltpu.SemaphoreType.DMA((2,))],
            name="spectrum",
        )

    def field(rows, margins):
        return call(
            field_kernel,
            [SM] + [VM] * 10,
            PLANES,
            (neighbours, rows, *margins, unpack_x, ea, gy),
            [pltpu.VMEM((SLOTS * PAD, LANES), BF16)] * 2 + [pltpu.VMEM((SLOTS * PAD, LANES), F32)],
            name="field",
        )

    margins = exchange(slabs, pairs)
    planes = field(rows, margins)
    kernel = spectrum(0)
    first = call(
        first_kernel,
        [SM] + [VM] * 10,
        [ROWS] + SLABS,
        (tissue, planes, kernel, rows, targets[0], ea, ei, gh, gb, twiddle, pack_x),
        [PLANES_V, LINES_V],
        name="first",
    )
    rows, slabs = first[0], first[1:]
    margins = exchange(slabs, pairs)
    kernel = spectrum(1)
    planes = field(rows, margins)
    out = call(
        last_kernel,
        [SM] + [VM] * 9,
        shape((FLAT, 128)),
        (tissue, planes, kernel, rows, targets[1], ea, ei, gh, gb, twiddle),
        [PLANES_V, LINES_V, ROWS_V],
        name="last",
    )
    return out.reshape(1, FLAT * 128)


def solution(mesh):
    return jax.shard_map(
        local,
        mesh=mesh,
        in_specs=(
            P("blk", None),
            P("blk", None, None),
            P("blk", None, None),
            P("blk"),
            P("blk", None),
            P("blk", None, None),
            P("blk", None, None),
            P(),
            P(),
        ),
        out_specs=P("blk", None),
        check_vma=False,
    )
```

time: 686 us -> 112 us (0.16)
  the two profiles are of different devices: /device:TPU:0 before, /device:TPU:23 now
where the time goes in v1:
time: 112 us; the launch traced here: 111 us
  starting transfers between devices  41.4 us (37%)
  blocking collectives  33.3 us (30%)
  Pallas kernels  20.9 us (19%)
  local copies, waits for them, and re-layouts  6.56 us (6%)
  between operations  5.01 us (4%)
  other arithmetic  2.92 us (3%)
    ppermute x12, starting transfers between devices, exchange(): lax.ppermute(sent, 'blk', pairs[face])  41.4 us
    all_gather x1, blocking collectives, local(): cells = lax.all_gather(views, 'blk', axis=0, tiled=False)  33.3 us
    pallas_call x7, Pallas kernels, call(): pl.pallas_call(body, in_specs=ins, out_specs=[VM] * len(outs) if many els...  20.9 us
    unnamed x50, local copies, waits for them, and re-layouts  4.46 us
    convert_element_type x1, other arithmetic, local(): lax.dynamic_index_in_dim(observed[0], view_order[u], 0, keepdims=False)  2.87 us
  transfers between devices with their start and end apart: 12, of which 1 were waited for; matrix products, arithmetic and copies ran while one was open for 2% of the time, Pallas kernels for 4%

profile of v1, /device:TPU:23, one launch (start us, length us, event | category | flops | bytes accessed | tf_op | source)
XLA Modules:
  0.0 111.1 jit_solution(5912067953253304003)
XLA Ops:
  0.0 1.3 %fusion.4 = (s32[1]{0:T(128)}, s32[1]{0:T(128)}) fusion(s32[6]{0:T(128)} %refs_0_.3), kind=kLoop, calls=%fused_computation.9 | loop fusion | bytes 16 | tf_op jit(solution)/shard_map/slice | solution.py:578
  5.1 2.9 %dynamic-slice_convert_fusion = (f32[1,1,110592]{2,1,0:T(1,128)S(1)}, f32[1,1,110592]{2,1,0:T(1,128)S(1)}) fusion(bf16[1,6,110592]{2,1,0:T(8,128)(2,1)} %param.22, s32[]{:T(128)S(6)} %select_n.10, s32[]{:T(128)S(6)} %select_n.9), kind=kLoop, calls=%fused_computation | loop fusion | flops 221184 | bytes 1327112 | tf_op jit(solution)/shard_map/convert_element_type | solution.py:578
  8.0 0.0 copy-start.2
  8.1 1.9 %prep.1 = (f32[2,768,128]{2,1,0:T(8,128)S(1)}, f32[2,768,128]{2,1,0:T(8,128)S(1)}, f32[2,768,128]{2,1,0:T(8,128)S(1)}, bf16[192,128]{1,0:T(8,128)(2,1)}, bf16[19...) custom-call(f32[864,128]{1,0:T(8,128)S(1)} %bitcast.14, ...), custom_call_target="tpu_custom_call" | custom-call | tf_op jit(solution)/shard_map/prep/pallas_call | solution.py:513
  10.0 0.9 copy-done.9
  10.9 0.9 copy-done.11
  11.7 1.3 %collective-permute-start.2 = (bf16[128,256]{1,0:T(8,128)(2,1)}, bf16[128,256]{1,0:T(8,128)(2,1)S(1)}, u32[]{:S(2)}, u32[]{:S(2)}) collective-permute-start(bf16[128,256]{1,0:T(8,128)(2,1)} %get-tuple-element.24), channel_id=1, source_target_pairs={{0,2},{1,3},{4,6},{5,7},{8,10},{9,11},{12,14},{13,15},{16,18},{17,... | collective-permute-start | bytes 196616 | tf_op jit(solution)/shard_map/ppermute | solution.py:551
  13.0 4.0 %collective-permute-start.3 = (bf16[128,256]{1,0:T(8,128)(2,1)}, bf16[128,256]{1,0:T(8,128)(2,1)S(1)}, u32[]{:S(2)}, u32[]{:S(2)}) collective-permute-start(bf16[128,256]{1,0:T(8,128)(2,1)} %get-tuple-element.25), channel_id=1, source_target_pairs={{2,0},{3,1},{6,4},{7,5},{10,8},{11,9},{14,12},{15,13},{18,16},{19,... | collective-permute-start | bytes 196616 | tf_op jit(solution)/shard_map/ppermute | solution.py:551
  17.0 4.3 %collective-permute-start = (bf16[192,128]{1,0:T(8,128)(2,1)S(1)}, bf16[192,128]{1,0:T(8,128)(2,1)S(1)}, u32[]{:S(2)}, u32[]{:S(2)}) collective-permute-start(bf16[192,128]{1,0:T(8,128)(2,1)S(1)} %get-tuple-element.22), channel_id=1, source_target_pairs={{0,1},{2,3},{4,5},{6,7},{1,8},{8,9},{3,10},{10,11},{5,12},{12,13},... | collective-permute-start | bytes 147464 | tf_op jit(solution)/shard_map/ppermute | solution.py:551
  21.4 1.9 %collective-permute-start.1 = (bf16[192,128]{1,0:T(8,128)(2,1)}, bf16[192,128]{1,0:T(8,128)(2,1)}, u32[]{:S(2)}, u32[]{:S(2)}) collective-permute-start(bf16[192,128]{1,0:T(8,128)(2,1)} %get-tuple-element.23), channel_id=1, source_target_pairs={{1,0},{8,1},{3,2},{10,3},{5,4},{12,5},{7,6},{14,7},{9,8},{11,10},{... | collective-permute-start | bytes 147464 | tf_op jit(solution)/shard_map/ppermute | solution.py:551
  23.3 1.3 %collective-permute-start.4 = (bf16[192,128]{1,0:T(8,128)(2,1)}, bf16[192,128]{1,0:T(8,128)(2,1)}, u32[]{:S(2)}, u32[]{:S(2)}) collective-permute-start(bf16[192,128]{1,0:T(8,128)(2,1)} %get-tuple-element.26), channel_id=1, source_target_pairs={{16,4},{17,5},{18,6},{19,7},{24,12},{25,13},{26,14},{27,15},{0,16}... | collective-permute-start | bytes 147464 | tf_op jit(solution)/shard_map/ppermute | solution.py:551
  24.6 0.8 convert_bitcast_fusion.1
  25.4 0.1 fusion.3
  25.5 5.6 %collective-permute-start.5 = (bf16[192,128]{1,0:T(8,128)(2,1)}, bf16[192,128]{1,0:T(8,128)(2,1)}, u32[]{:S(2)}, u32[]{:S(2)}) collective-permute-start(bf16[192,128]{1,0:T(8,128)(2,1)} %get-tuple-element.27), channel_id=1, source_target_pairs={{16,0},{17,1},{18,2},{19,3},{20,4},{21,5},{22,6},{23,7},{24,8},{25... | collective-permute-start | bytes 147464 | tf_op jit(solution)/shard_map/ppermute | solution.py:551
  31.1 33.3 %all-gather.1.refs_4_ = bf16[32,2,5120]{2,1,0:T(2,128)(2,1)S(1)} all-gather(bf16[1,2,5120]{2,1,0:T(2,128)(2,1)S(1)} %fusion.3), channel_id=2, replica_groups=mesh['blk'=32] {'blk'}, dimensions={0}, use_global_device_ids=true | all-gather | bytes 675840 | tf_op jit(solution)/shard_map/all_gather | solution.py:575
  64.4 0.1 copy.26.refs_1_
  64.5 0.8 copy.27.refs_2_
  66.0 2.3 %spectrum.2.kernel = f32[16,128,128]{2,1,0:T(8,128)S(1)} custom-call(s32[6]{0:T(128)S(1)} %copy-done.19, s32[1,6,2]{2,1,0:T(8,128)S(1)} %copy.26.refs_1_, f32[1,6,2]{2,1,0:T(8,128)S(1)} %copy.27.refs_2_, s32[32]{0:T(128)S(1)} %copy-done.20, bf16[32,2,5120]{2,1,0:T(2,128)(2,1)S(1)} %all-gather.1.refs_4_, f32[32,384]{1,0:T(8,128)S(1)} %copy-done.18, ...), custom_call_target="tpu_custom_call" | custom-call | tf_op jit(solution)/shard_map/spectrum/pallas_call | solution.py:513
  68.3 1.0 copy-done.1
  69.4 0.8 copy-done.21
  70.2 1.9 %field.2.planes = f32[16,128,128]{2,1,0:T(8,128)S(1)} custom-call(s32[1,6]{1,0:T(1,128)S(1)} %copy-done.21, f32[2,768,128]{2,1,0:T(8,128)S(1)} %get-tuple-element.21.u, bf16[192,128]{1,0:T(8,128)(2,1)S(1)} %collective-permute-done.zm, bf16[192,128]{1,0:T(8,128)(2,1)} %collective-permute-done.1.zp, bf16[128,256]{1,0:T(8,128)(2,1)S(1)} %collective-permute-done.2.ym, ...), custom_call_target="tpu_custom_call" | custom-call | tf_op jit(solution)/shard_map/field/pallas_call | solution.py:513
  72.1 5.7 %first.1 = (f32[2,768,128]{2,1,0:T(8,128)S(1)}, bf16[192,128]{1,0:T(8,128)(2,1)S(1)}, bf16[192,128]{1,0:T(8,128)(2,1)S(1)}, bf16[128,256]{1,0:T(8,128)(2,1)S(1)}...) custom-call(s32[1]{0:T(128)S(6)} %copy.30.tissue, ...), custom_call_target="tpu_custom_call" | custom-call | tf_op jit(solution)/shard_map/first/pallas_call | solution.py:513
  77.8 1.3 %collective-permute-start.10 = (bf16[192,128]{1,0:T(8,128)(2,1)S(1)}, bf16[192,128]{1,0:T(8,128)(2,1)S(1)}, u32[]{:S(2)}, u32[]{:S(2)}) collective-permute-start(bf16[192,128]{1,0:T(8,128)(2,1)S(1)} %get-tuple-element.34), channel_id=1, source_target_pairs={{16,4},{17,5},{18,6},{19,7},{24,12},{25,13},{26,14},{27,15},{0,16}... | collective-permute-start | bytes 147464 | tf_op jit(solution)/shard_map/ppermute | solution.py:551
  79.1 1.3 %collective-permute-start.8 = (bf16[128,256]{1,0:T(8,128)(2,1)S(1)}, bf16[128,256]{1,0:T(8,128)(2,1)S(1)}, u32[]{:S(2)}, u32[]{:S(2)}) collective-permute-start(bf16[128,256]{1,0:T(8,128)(2,1)S(1)} %get-tuple-element.32), channel_id=1, source_target_pairs={{0,2},{1,3},{4,6},{5,7},{8,10},{9,11},{12,14},{13,15},{16,18},{17,... | collective-permute-start | bytes 196616 | tf_op jit(solution)/shard_map/ppermute | solution.py:551
  80.4 4.0 %collective-permute-start.9 = (bf16[128,256]{1,0:T(8,128)(2,1)S(1)}, bf16[128,256]{1,0:T(8,128)(2,1)S(1)}, u32[]{:S(2)}, u32[]{:S(2)}) collective-permute-start(bf16[128,256]{1,0:T(8,128)(2,1)S(1)} %get-tuple-element.33), channel_id=1, source_target_pairs={{2,0},{3,1},{6,4},{7,5},{10,8},{11,9},{14,12},{15,13},{18,16},{19,... | collective-permute-start | bytes 196616 | tf_op jit(solution)/shard_map/ppermute | solution.py:551
  84.4 8.3 %collective-permute-start.11 = (bf16[192,128]{1,0:T(8,128)(2,1)S(1)}, bf16[192,128]{1,0:T(8,128)(2,1)S(1)}, u32[]{:S(2)}, u32[]{:S(2)}) collective-permute-start(bf16[192,128]{1,0:T(8,128)(2,1)S(1)} %get-tuple-element.35), channel_id=1, source_target_pairs={{16,0},{17,1},{18,2},{19,3},{20,4},{21,5},{22,6},{23,7},{24,8},{25... | collective-permute-start | bytes 147464 | tf_op jit(solution)/shard_map/ppermute | solution.py:551
  92.8 6.0 %collective-permute-start.6 = (bf16[192,128]{1,0:T(8,128)(2,1)S(1)}, bf16[192,128]{1,0:T(8,128)(2,1)S(1)}, u32[]{:S(2)}, u32[]{:S(2)}) collective-permute-start(bf16[192,128]{1,0:T(8,128)(2,1)S(1)} %get-tuple-element.30), channel_id=1, source_target_pairs={{0,1},{2,3},{4,5},{6,7},{1,8},{8,9},{3,10},{10,11},{5,12},{12,13},... | collective-permute-start | bytes 147464 | tf_op jit(solution)/shard_map/ppermute | solution.py:551
  98.8 2.1 %collective-permute-start.7 = (bf16[192,128]{1,0:T(8,128)(2,1)S(1)}, bf16[192,128]{1,0:T(8,128)(2,1)S(1)}, u32[]{:S(2)}, u32[]{:S(2)}) collective-permute-start(bf16[192,128]{1,0:T(8,128)(2,1)S(1)} %get-tuple-element.31), channel_id=1, source_target_pairs={{1,0},{8,1},{3,2},{10,3},{5,4},{12,5},{7,6},{14,7},{9,8},{11,10},{... | collective-permute-start | bytes 147464 | tf_op jit(solution)/shard_map/ppermute | solution.py:551
  100.9 2.3 %spectrum.3.kernel = f32[16,128,128]{2,1,0:T(8,128)S(1)} custom-call(s32[6]{0:T(128)S(1)} %copy-done.19, s32[1,6,2]{2,1,0:T(8,128)S(1)} %copy.26.refs_1_, f32[1,6,2]{2,1,0:T(8,128)S(1)} %copy.27.refs_2_, s32[32]{0:T(128)S(1)} %copy-done.20, bf16[32,2,5120]{2,1,0:T(2,128)(2,1)S(1)} %all-gather.1.refs_4_, f32[32,384]{1,0:T(8,128)S(1)} %copy-done.18, ...), custom_call_target="tpu_custom_call" | custom-call | tf_op jit(solution)/shard_map/spectrum/pallas_call | solution.py:513
  103.2 1.0 collective-permute-done.7.zp
  104.2 1.6 %field.3.planes = f32[16,128,128]{2,1,0:T(8,128)S(1)} custom-call(s32[1,6]{1,0:T(1,128)S(1)} %copy-done.22, f32[2,768,128]{2,1,0:T(8,128)S(1)} %get-tuple-element.29.u, bf16[192,128]{1,0:T(8,128)(2,1)S(1)} %collective-permute-done.6.zm, bf16[192,128]{1,0:T(8,128)(2,1)S(1)} %collective-permute-done.7.zp, bf16[128,256]{1,0:T(8,128)(2,1)S(1)} %collective-permute-done.8.ym, ...), custom_call_target="tpu_custom_call" | custom-call | tf_op jit(solution)/shard_map/field/pallas_call | solution.py:513
  105.8 5.3 %last.1 = f32[864,128]{1,0:T(8,128)} custom-call(s32[1]{0:T(128)S(6)} %copy.30.tissue, f32[16,128,128]{2,1,0:T(8,128)S(1)} %field.3.planes, f32[16,128,128]{2,1,0:T(8,128)S(1)} %spectrum.3.kernel, f32[2,768,128]{2,1,0:T(8,128)S(1)} %get-tuple-element.29.u, f32[2,768,128]{2,1,0:T(8,128)S(1)} %copy-done.10, bf16[768,256]{1,0:T(8,128)(2,1)S(1)} %copy-done, ...), custom_call_target="tpu_custom_call" | custom-call | tf_op jit(solution)/shard_map/last/pallas_call | solution.py:513
  (54 shorter events, 0.1 us)
Async XLA Ops:
  0.0 8.1 %copy-start.6 = (bf16[1024,256]{1,0:T(8,128)(2,1)S(1)}, bf16[1024,256]{1,0:T(8,128)(2,1)}, u32[]{:S(2)}) copy-start(bf16[1024,256]{1,0:T(8,128)(2,1)} %constant.50.clone.pack_x) | copy-start | bytes 1572868
  5.1 3.0 %copy-start.13 = (f32[1,110592]{1,0:T(1,128)S(1)}, f32[1,110592]{1,0:T(1,128)}, u32[]{:S(2)}) copy-start(f32[1,110592]{1,0:T(1,128)} %param.21) | copy-start | bytes 1327108
  8.0 56.4 %copy-start.23 = (s32[1,6,2]{1,2,0:T(2,128)S(1)}, s32[1,6,2]{1,2,0:T(2,128)}, u32[]{:S(2)}) copy-start(s32[1,6,2]{1,2,0:T(2,128)} %param.26) | copy-start | bytes 148
  8.0 57.9 %copy-start.2 = (bf16[1152,256]{1,0:T(8,128)(2,1)S(1)}, bf16[1152,256]{1,0:T(8,128)(2,1)}, u32[]{:S(2)}) copy-start(bf16[1152,256]{1,0:T(8,128)(2,1)} %constant.46.clone.refs_6_) | copy-start | bytes 1769476
  8.0 57.9 %copy-start.3 = (bf16[1152,256]{1,0:T(8,128)(2,1)S(1)}, bf16[1152,256]{1,0:T(8,128)(2,1)}, u32[]{:S(2)}) copy-start(bf16[1152,256]{1,0:T(8,128)(2,1)} %constant.47.clone.refs_7_) | copy-start | bytes 1769476
  8.0 57.9 %copy-start.4 = (f32[2,16,8,128]{3,2,1,0:T(8,128)S(1)}, f32[2,16,8,128]{3,2,1,0:T(8,128)}, u32[]{:S(2)}) copy-start(f32[2,16,8,128]{3,2,1,0:T(8,128)} %constant.49.clone.refs_9_.twiddle) | copy-start | bytes 393220
  8.1 57.9 %copy-start.17 = (bf16[128,192]{1,0:T(8,128)(2,1)S(1)}, bf16[128,192]{1,0:T(8,128)(2,1)}, u32[]{:S(2)}) copy-start(bf16[128,192]{1,0:T(8,128)(2,1)} %constant.45.clone.refs_8_) | copy-start | bytes 147460
  8.1 57.9 %copy-start.18 = (f32[32,384]{1,0:T(8,128)S(1)}, f32[32,384]{1,0:T(8,128)}, u32[]{:S(2)}) copy-start(f32[32,384]{1,0:T(8,128)} %constant.48.clone.refs_5_) | copy-start | bytes 147460
  8.1 57.9 %copy-start.19 = (s32[6]{0:T(128)S(1)}, s32[6]{0:T(128)}, u32[]{:S(2)}) copy-start(s32[6]{0:T(128)} %refs_0_.3) | copy-start | bytes 76
  8.1 57.9 %copy-start.20 = (s32[32]{0:T(128)S(1)}, s32[32]{0:T(128)}, u32[]{:S(2)}) copy-start(s32[32]{0:T(128)} %refs_3_.3) | copy-start | bytes 388
  11.7 57.6 %collective-permute-start.2 = (bf16[128,256]{1,0:T(8,128)(2,1)}, bf16[128,256]{1,0:T(8,128)(2,1)S(1)}, u32[]{:S(2)}, u32[]{:S(2)}) collective-permute-start(bf16[128,256]{1,0:T(8,128)(2,1)} %get-tuple-element.24), channel_id=1, source_target_pairs={{0,2},{1,3},{4,6},{5,7},{8,10},{9,11},{12,14},{13,15},{16,18},{17,... | collective-permute-start | bytes 196616 | tf_op jit(solution)/shard_map/ppermute | solution.py:551
  13.0 56.3 %collective-permute-start.3 = (bf16[128,256]{1,0:T(8,128)(2,1)}, bf16[128,256]{1,0:T(8,128)(2,1)S(1)}, u32[]{:S(2)}, u32[]{:S(2)}) collective-permute-start(bf16[128,256]{1,0:T(8,128)(2,1)} %get-tuple-element.25), channel_id=1, source_target_pairs={{2,0},{3,1},{6,4},{7,5},{10,8},{11,9},{14,12},{15,13},{18,16},{19,... | collective-permute-start | bytes 196616 | tf_op jit(solution)/shard_map/ppermute | solution.py:551
  17.0 8.4 %collective-permute-start = (bf16[192,128]{1,0:T(8,128)(2,1)S(1)}, bf16[192,128]{1,0:T(8,128)(2,1)S(1)}, u32[]{:S(2)}, u32[]{:S(2)}) collective-permute-start(bf16[192,128]{1,0:T(8,128)(2,1)S(1)} %get-tuple-element.22), channel_id=1, source_target_pairs={{0,1},{2,3},{4,5},{6,7},{1,8},{8,9},{3,10},{10,11},{5,12},{12,13},... | collective-permute-start | bytes 147464 | tf_op jit(solution)/shard_map/ppermute | solution.py:551
  21.4 48.0 %collective-permute-start.1 = (bf16[192,128]{1,0:T(8,128)(2,1)}, bf16[192,128]{1,0:T(8,128)(2,1)}, u32[]{:S(2)}, u32[]{:S(2)}) collective-permute-start(bf16[192,128]{1,0:T(8,128)(2,1)} %get-tuple-element.23), channel_id=1, source_target_pairs={{1,0},{8,1},{3,2},{10,3},{5,4},{12,5},{7,6},{14,7},{9,8},{11,10},{... | collective-permute-start | bytes 147464 | tf_op jit(solution)/shard_map/ppermute | solution.py:551
  23.3 46.0 %collective-permute-start.4 = (bf16[192,128]{1,0:T(8,128)(2,1)}, bf16[192,128]{1,0:T(8,128)(2,1)}, u32[]{:S(2)}, u32[]{:S(2)}) collective-permute-start(bf16[192,128]{1,0:T(8,128)(2,1)} %get-tuple-element.26), channel_id=1, source_target_pairs={{16,4},{17,5},{18,6},{19,7},{24,12},{25,13},{26,14},{27,15},{0,16}... | collective-permute-start | bytes 147464 | tf_op jit(solution)/shard_map/ppermute | solution.py:551
  25.4 43.9 %copy-start = (bf16[768,256]{1,0:T(8,128)(2,1)S(1)}, bf16[768,256]{1,0:T(8,128)(2,1)}, u32[]{:S(2)}) copy-start(bf16[768,256]{1,0:T(8,128)(2,1)} %constant.40.clone.ea) | copy-start | bytes 1179652
  25.5 43.9 %copy-start.15 = (bf16[128,384]{1,0:T(8,128)(2,1)S(1)}, bf16[128,384]{1,0:T(8,128)(2,1)}, u32[]{:S(2)}) copy-start(bf16[128,384]{1,0:T(8,128)(2,1)} %constant.42.clone.gy) | copy-start | bytes 294916
  25.5 43.9 %collective-permute-start.5 = (bf16[192,128]{1,0:T(8,128)(2,1)}, bf16[192,128]{1,0:T(8,128)(2,1)}, u32[]{:S(2)}, u32[]{:S(2)}) collective-permute-start(bf16[192,128]{1,0:T(8,128)(2,1)} %get-tuple-element.27), channel_id=1, source_target_pairs={{16,0},{17,1},{18,2},{19,3},{20,4},{21,5},{22,6},{23,7},{24,8},{25... | collective-permute-start | bytes 147464 | tf_op jit(solution)/shard_map/ppermute | solution.py:551
  65.2 4.2 %copy-start.5 = (bf16[256,1024]{1,0:T(8,128)(2,1)S(1)}, bf16[256,1024]{1,0:T(8,128)(2,1)}, u32[]{:S(2)}) copy-start(bf16[256,1024]{1,0:T(8,128)(2,1)} %constant.51.clone.unpack_x) | copy-start | bytes 1572868
  69.3 2.8 %copy-start.7 = (bf16[1024,256]{1,0:T(8,128)(2,1)S(1)}, bf16[1024,256]{1,0:T(8,128)(2,1)}, u32[]{:S(2)}) copy-start(bf16[1024,256]{1,0:T(8,128)(2,1)} %constant.50.clone.pack_x) | copy-start | bytes 1572868
  69.3 2.8 %copy-start.8 = (bf16[768,256]{1,0:T(8,128)(2,1)S(1)}, bf16[768,256]{1,0:T(8,128)(2,1)}, u32[]{:S(2)}) copy-start(bf16[768,256]{1,0:T(8,128)(2,1)} %constant.41.clone.ei) | copy-start | bytes 1179652
  69.3 2.8 %copy-start.12 = (f32[2,768,128]{2,1,0:T(8,128)S(1)}, f32[2,768,128]{2,1,0:T(8,128)}, u32[]{:S(2)}) copy-start(f32[2,768,128]{2,1,0:T(8,128)} %copy-done.11) | copy-start | bytes 2359300
  69.3 2.8 %copy-start.14 = (bf16[128,288]{1,0:T(8,128)(2,1)S(1)}, bf16[128,288]{1,0:T(8,128)(2,1)}, u32[]{:S(2)}) copy-start(bf16[128,288]{1,0:T(8,128)(2,1)} %constant.43.clone.gh) | copy-start | bytes 221188
  69.3 2.8 %copy-start.16 = (bf16[96,384]{1,0:T(8,128)(2,1)S(1)}, bf16[96,384]{1,0:T(8,128)(2,1)}, u32[]{:S(2)}) copy-start(bf16[96,384]{1,0:T(8,128)(2,1)} %constant.44.clone.gb) | copy-start | bytes 221188
  77.8 26.3 %copy-start.22 = (s32[1,6]{1,0:T(1,128)S(1)}, s32[1,6]{1,0:T(1,128)}, u32[]{:S(2)}) copy-start(s32[1,6]{1,0:T(1,128)} %present.3) | copy-start | bytes 76
  77.8 20.9 %collective-permute-start.10 = (bf16[192,128]{1,0:T(8,128)(2,1)S(1)}, bf16[192,128]{1,0:T(8,128)(2,1)S(1)}, u32[]{:S(2)}, u32[]{:S(2)}) collective-permute-start(bf16[192,128]{1,0:T(8,128)(2,1)S(1)} %get-tuple-element.34), channel_id=1, source_target_pairs={{16,4},{17,5},{18,6},{19,7},{24,12},{25,13},{26,14},{27,15},{0,16}... | collective-permute-start | bytes 147464 | tf_op jit(solution)/shard_map/ppermute | solution.py:551
  79.1 25.0 %collective-permute-start.8 = (bf16[128,256]{1,0:T(8,128)(2,1)S(1)}, bf16[128,256]{1,0:T(8,128)(2,1)S(1)}, u32[]{:S(2)}, u32[]{:S(2)}) collective-permute-start(bf16[128,256]{1,0:T(8,128)(2,1)S(1)} %get-tuple-element.32), channel_id=1, source_target_pairs={{0,2},{1,3},{4,6},{5,7},{8,10},{9,11},{12,14},{13,15},{16,18},{17,... | collective-permute-start | bytes 196616 | tf_op jit(solution)/shard_map/ppermute | solution.py:551
  80.4 23.7 %collective-permute-start.9 = (bf16[128,256]{1,0:T(8,128)(2,1)S(1)}, bf16[128,256]{1,0:T(8,128)(2,1)S(1)}, u32[]{:S(2)}, u32[]{:S(2)}) collective-permute-start(bf16[128,256]{1,0:T(8,128)(2,1)S(1)} %get-tuple-element.33), channel_id=1, source_target_pairs={{2,0},{3,1},{6,4},{7,5},{10,8},{11,9},{14,12},{15,13},{18,16},{19,... | collective-permute-start | bytes 196616 | tf_op jit(solution)/shard_map/ppermute | solution.py:551
  84.4 18.7 %collective-permute-start.11 = (bf16[192,128]{1,0:T(8,128)(2,1)S(1)}, bf16[192,128]{1,0:T(8,128)(2,1)S(1)}, u32[]{:S(2)}, u32[]{:S(2)}) collective-permute-start(bf16[192,128]{1,0:T(8,128)(2,1)S(1)} %get-tuple-element.35), channel_id=1, source_target_pairs={{16,0},{17,1},{18,2},{19,3},{20,4},{21,5},{22,6},{23,7},{24,8},{25... | collective-permute-start | bytes 147464 | tf_op jit(solution)/shard_map/ppermute | solution.py:551
  92.8 10.4 %collective-permute-start.6 = (bf16[192,128]{1,0:T(8,128)(2,1)S(1)}, bf16[192,128]{1,0:T(8,128)(2,1)S(1)}, u32[]{:S(2)}, u32[]{:S(2)}) collective-permute-start(bf16[192,128]{1,0:T(8,128)(2,1)S(1)} %get-tuple-element.30), channel_id=1, source_target_pairs={{0,1},{2,3},{4,5},{6,7},{1,8},{8,9},{3,10},{10,11},{5,12},{12,13},... | collective-permute-start | bytes 147464 | tf_op jit(solution)/shard_map/ppermute | solution.py:551
  98.8 5.4 %collective-permute-start.7 = (bf16[192,128]{1,0:T(8,128)(2,1)S(1)}, bf16[192,128]{1,0:T(8,128)(2,1)S(1)}, u32[]{:S(2)}, u32[]{:S(2)}) collective-permute-start(bf16[192,128]{1,0:T(8,128)(2,1)S(1)} %get-tuple-element.31), channel_id=1, source_target_pairs={{1,0},{8,1},{3,2},{10,3},{5,4},{12,5},{7,6},{14,7},{9,8},{11,10},{... | collective-permute-start | bytes 147464 | tf_op jit(solution)/shard_map/ppermute | solution.py:551
  103.2 2.6 %copy-start.10 = (f32[2,768,128]{2,1,0:T(8,128)S(1)}, f32[2,768,128]{2,1,0:T(8,128)}, u32[]{:S(2)}) copy-start(f32[2,768,128]{2,1,0:T(8,128)} %copy-done.9) | copy-start | bytes 2359300
  (4 other events, 3.5 us)

commit v2 on v1

--- a/solution.py
+++ b/solution.py
@@ -1,3 +1,5 @@
+import functools
+
 import numpy as np
 
 import jax
@@ -11,14 +13,15 @@
 E = 48
 MARGIN = 8
 UPDATES = 2
+VIEWS = 6
 PAD = 64
 KS = 17
 KS2 = KS * KS
 KS3 = 4913
 SLOTS = 16
 LANES = 256
-TAPROWS = 32
-CELLPAD = 5120
+TAPS = 24
+CELLROWS = 40
 FLAT = 864
 
 F32 = jnp.float32
@@ -77,28 +80,28 @@
 
 
 def table_y_taps():
-    ky, tap = np.arange(PAD), np.arange(TAPROWS) - MARGIN
+    ky, tap = np.arange(PAD), np.arange(TAPS) - MARGIN
     angle = -2.0 * np.pi * ky[:, None] * tap[None, :] / PAD
     return complex_rows(angle)
 
 
-def table_taps(z4):
-    k4, kx = np.arange(4), np.arange(32)
-    tap_x = np.arange(384) % KS - MARGIN
-    angle = -2.0 * np.pi * (
-        z4 * k4[None, :, None] / 4.0 + (kx[None, None, :] + 0.5) * tap_x[:, None, None] / PAD
-    )
-    angle = angle.reshape(384, 128)
-    table = np.concatenate([np.cos(angle), np.sin(angle)], axis=1)
-    table[KS2:] = 0.0
+def table_taps():
+    kx, tap = np.arange(32), np.arange(KS) - MARGIN
+    angle = -2.0 * np.pi * (kx[None, :] + 0.5) * tap[:, None] / PAD
+    full = np.concatenate([np.tile(np.cos(angle), (1, 4)), np.tile(np.sin(angle), (1, 4))], axis=1)
+    high, low = two_terms(full)
+    table = np.zeros((128, LANES), ml_dtypes.bfloat16)
+    for start, term in ((0, high), (32, high), (64, low)):
+        table[start : start + KS] = term
     return table
 
 
-def table_tap_mask():
-    place = np.arange(384)
-    return (place[None, :] // KS == np.arange(TAPROWS)[:, None]).astype(np.float32) * (
-        place[None, :] < KS2
-    )
+def table_tap_turns():
+    k4 = np.repeat(np.arange(4), 32)
+    tap = np.arange(KS) - MARGIN
+    angle = -2.0 * np.pi * tap[:, None] * k4[None, :] / PAD
+    both = np.stack([np.cos(angle), np.sin(angle)], axis=0)
+    return np.broadcast_to(both[:, :, None, :], (2, KS, 8, 128)).astype(np.float32)
 
 
 def table_twiddle():
@@ -106,26 +109,6 @@
     angle = -2.0 * np.pi * np.arange(SLOTS)[:, None] * k4[None, :] / PAD
     both = np.stack([np.cos(angle), np.sin(angle)], axis=0)
     return np.broadcast_to(both[:, :, None, :], (2, SLOTS, 8, 128)).astype(np.float32)
-
-
-def table_pack_x():
-    table = np.zeros((4, 4, PAD, 2, 4, 4, MARGIN), np.float32)
-    for group in range(4):
-        for z4 in range(3):
-            for step in range(MARGIN):
-                table[group, z4, step, 0, group, z4, step] = 1.0
-                table[group, z4, E - MARGIN + step, 1, group, z4, step] = 1.0
-    return table.reshape(4 * LANES, LANES).astype(ml_dtypes.bfloat16)
-
-
-def table_unpack_x():
-    table = np.zeros((2, 4, 4, MARGIN, 4, 4, PAD), np.float32)
-    for group in range(4):
-        for z4 in range(3):
-            for step in range(MARGIN):
-                table[0, group, z4, step, group, z4, PAD - MARGIN + step] = 1.0
-                table[1, group, z4, step, group, z4, E + step] = 1.0
-    return table.reshape(LANES, 4 * LANES).astype(ml_dtypes.bfloat16)
 
 
 def split(value):
@@ -158,14 +141,14 @@
     return jnp.where(lane_iota(one.shape) < edge, one, two)
 
 
-def unflatten(flat_ref, out_ref):
+def unflatten(load, out_ref):
     lane = lane_iota((8, 128))
     zero = jnp.zeros((8, 128), F32)
     for block in range(12):
         parts = []
         for z4 in range(3):
             first = 3 * (96 * z4 + 8 * block)
-            parts.append([flat_ref[pl.ds(first + m, 8, stride=3), :] for m in range(3)])
+            parts.append([load(first + m) for m in range(3)])
         for piece in range(8):
             low = cut(parts[0], piece, 0)
             mid = cut(parts[1], piece, 64)
@@ -204,41 +187,69 @@
                 flat_ref[pl.ds(first + m, 8, stride=3), :] = out[m]
 
 
-def pack_slabs(rows_ref, pack_x, x0, x1, y0, y1, z0, z1):
+def x_picks(wide, packed, low_start, high_start):
+    place = packed % 128
+    start = jnp.where(packed >= 128, high_start, low_start)
+    here = (wide // PAD == place // MARGIN) & (wide % PAD == start + place % MARGIN) & (place < 3 * MARGIN)
+    return jnp.where(here, 1.0, 0.0).astype(BF16)
+
+
+def both_iotas():
+    dims = (LANES, LANES)
+    return lax.broadcasted_iota(jnp.int32, dims, 0), lax.broadcasted_iota(jnp.int32, dims, 1)
+
+
+def pack_slabs(rows_ref):
     high = both_halves(rows_ref, slice(None)).astype(BF16)
-    wide = jnp.concatenate([high[192 * g : 192 * (g + 1)] for g in range(4)], axis=1)
-    both = dot(wide, pack_x[...]).astype(BF16)
-    x0[...] = both[:, 0:128]
-    x1[...] = both[:, 128:256]
+    rows, columns = both_iotas()
+    found = dot(high, x_picks(rows, columns, 0, E - MARGIN))
+    faces = []
+    for face in range(2):
+        value = found[0:192, 128 * face : 128 * (face + 1)]
+        for group in range(1, 4):
+            part = found[192 * group : 192 * (group + 1), 128 * face : 128 * (face + 1)]
+            value = value + pltpu.roll(part, 32 * group, 1)
+        faces.append(value.astype(BF16))
+    x0, x1 = faces
     low_rows, high_rows = [], []
     for slot in range(SLOTS):
         low_rows.append(both_halves(rows_ref, slice(E * slot, E * slot + MARGIN)))
         high_rows.append(both_halves(rows_ref, slice(E * slot + E - MARGIN, E * (slot + 1))))
-    y0[...] = jnp.concatenate(low_rows, axis=0).astype(BF16)
-    y1[...] = jnp.concatenate(high_rows, axis=0).astype(BF16)
+    y0, y1 = jnp.concatenate(low_rows, axis=0), jnp.concatenate(high_rows, axis=0)
+    y0, y1 = [jnp.concatenate([v[:, 0:128], v[:, 128:256]], axis=0).astype(BF16) for v in (y0, y1)]
     lane = lane_iota((192, 128))
     first = rows_ref[0, 0:192, :]
     second = pltpu.roll(rows_ref[0, 192:384, :], 64, 1)
-    z0[...] = jnp.where(lane < 64, first, second).astype(BF16)
+    z0 = jnp.where(lane < 64, first, second).astype(BF16)
     first = rows_ref[1, 384:576, :]
     second = pltpu.roll(rows_ref[1, 576:768, :], 64, 1)
-    z1[...] = jnp.where(lane < 64, first, second).astype(BF16)
-
-
-def assemble(present, rows_ref, unpack_x, margins, high_ref, low_ref):
-    zm, zp, ym, yp, xm, xp = margins
-    on = [present[0, face] >= 0 for face in range(6)]
-    zero_x = jnp.zeros((192, 128), BF16)
-    wide = jnp.concatenate(
-        [jnp.where(on[4], xm[...], zero_x), jnp.where(on[5], xp[...], zero_x)], axis=1
-    )
-    side = dot(wide, unpack_x[...])
-    scale = [jnp.where(on[face], 1.0, 0.0).astype(F32) for face in range(6)]
-    yp_rows = yp[...].astype(F32) * scale[3]
-    ym_rows = ym[...].astype(F32) * scale[2]
+    z1 = jnp.where(lane < 64, first, second).astype(BF16)
+    return (z0, z1), (y0, y1), (x0, x1)
+
+
+def sort_margins(present, odd, axis, pair):
+    on = [present[0, 2 * axis + side] >= 0 for side in range(2)]
+    pair = [value.astype(F32) for value in pair]
+    low = jnp.where(odd, pair[0], pair[1])
+    high = jnp.where(odd, pair[1], pair[0])
+    zero = jnp.zeros_like(low)
+    return jnp.where(on[0], low, zero), jnp.where(on[1], high, zero)
+
+
+def assemble(present, odds, rows_ref, margins, high_ref, low_ref):
+    (zm, zp), (ym, yp), (xm, xp) = [
+        sort_margins(present, odds[axis], axis, margins[axis]) for axis in range(3)
+    ]
+    rows, columns = both_iotas()
+    picks = x_picks(columns, rows, PAD - MARGIN, E)
+    parts = []
+    for group in range(4):
+        pair = [pltpu.roll(v, 128 - 32 * group, 1) if group else v for v in (xm, xp)]
+        parts.append(jnp.concatenate(pair, axis=1))
+    side = dot(jnp.concatenate(parts, axis=0).astype(BF16), picks)
+    ym_rows, yp_rows = [jnp.concatenate([v[0:128], v[128:256]], axis=1) for v in (ym, yp)]
     z_sides = []
-    for ref, face in ((zp, 1), (zm, 0)):
-        value = ref[...].astype(F32) * scale[face]
+    for value in (zp, zm):
         z_sides.append(pltpu.roll(value, 64, 1))
         z_sides.append(value)
     lane = lane_iota((E, 128))
@@ -246,7 +257,7 @@
         group, inner = slot // 4, slot % 4
         core = both_halves(rows_ref, slice(E * slot, E * (slot + 1)))
         high, low = split(core)
-        added = side[E * inner : E * (inner + 1), LANES * group : LANES * (group + 1)]
+        added = side[E * slot : E * (slot + 1)]
         full = high.astype(F32) + added
         z_side = z_sides[group][E * inner : E * (inner + 1), :]
         right = jnp.where(lane < 64, full[:, 128:256], z_side)
@@ -347,12 +358,13 @@
     return dft16(values, -1)
 
 
-def z_stage(planes_ref, twiddle, out_ref):
+def z_stage(planes_ref, out_ref):
     @pl.loop(0, PAD // 8)
     def _(step):
         rows = pl.ds(pl.multiple_of(8 * step, 8), 8)
         rows_imag = pl.ds(pl.multiple_of(8 * step + PAD, 8), 8)
-        values = z_forward(planes_ref, twiddle, rows, rows_imag)
+        values = [(planes_ref[slot, rows, :], planes_ref[slot, rows_imag, :]) for slot in range(SLOTS)]
+        values = dft16(values, -1)
         for slot in range(SLOTS):
             out_ref[slot, rows, :] = values[slot][0]
             out_ref[slot, rows_imag, :] = values[slot][1]
@@ -381,73 +393,156 @@
             out_ref[slot, rows_imag, :] = imag
 
 
-def tap_stage(flat, mask, table0, table3, table_y_ref, planes_ref):
-    lines = []
+def tap_stage(flat_ref, lines, spread, table, turns, table_y_ref, planes_ref):
+    lane = lane_iota((3, 128))
     for tap in range(KS):
-        offset = KS2 * tap
-        start = offset // 128 * 128
-        shift = offset - start
-        window = flat[:, start : start + 512]
-        if shift:
-            window = pltpu.roll(window, 512 - shift, 1)
-        lines.append(window[:, 0:384])
-    spread = []
-    for line in lines:
-        spread.append(jnp.broadcast_to(line, (TAPROWS, 384)) * mask)
-
-    def first_stage(taps, table):
-        high, low = split(jnp.concatenate(taps, axis=0))
-        return dot(jnp.concatenate([high, low, high], axis=1), table[...])
-
-    ahead = first_stage(spread[MARGIN:], table0)
-    behind = first_stage(spread[:MARGIN], table3)
-    slots = []
-    for slot in range(MARGIN):
-        slots.append(ahead[TAPROWS * slot : TAPROWS * (slot + 1)])
-    slots.append(ahead[TAPROWS * MARGIN :] + behind[0:TAPROWS])
-    for slot in range(MARGIN + 1, SLOTS):
-        at = slot - MARGIN
-        slots.append(behind[TAPROWS * at : TAPROWS * (at + 1)])
+        row, start = KS2 * tap // 128, KS2 * tap % 128
+        value = flat_ref[row : row + 3, :]
+        if start:
+            value = pltpu.roll(value, 128 - start, 1)
+            after = pltpu.roll(flat_ref[row + 1 : row + 4, :], 128 - start, 1)
+            value = jnp.where(lane < 128 - start, value, after)
+        for part in range(3):
+            lines[part, tap : tap + 1, :] = value[part : part + 1]
+    lane = lane_iota((TAPS, 128))
+    for line in range(KS):
+        part, start = KS * line // 128, KS * line % 128
+        value = lines[part]
+        if start:
+            value = pltpu.roll(value, 128 - start, 1)
+            if start + KS > 128:
+                after = pltpu.roll(lines[part + 1], 128 - start, 1)
+                value = jnp.where(lane < 128 - start, value, after)
+        spread[TAPS * line : TAPS * (line + 1), :] = jnp.where(lane < KS, value, 0.0)
+    for line in range(KS, TAPS):
+        spread[TAPS * line : TAPS * (line + 1), :] = jnp.zeros((TAPS, 128), F32)
+    rows = jnp.concatenate([spread[pl.ds(tap, TAPS, stride=TAPS), :] for tap in range(KS)], axis=0)
+    high = rows.astype(BF16).astype(F32)
+    low = rows - high
+    wide = high + pltpu.roll(low, 32, 1) + pltpu.roll(high, 64, 1)
+    out = dot(wide.astype(BF16), table[...])
+    slots = [None] * SLOTS
+    for tap in range(KS):
+        part = out[TAPS * tap : TAPS * (tap + 1)]
+        value = part[:, 0:128], part[:, 128:256]
+        if tap != MARGIN:
+            cosine, sine = [jnp.concatenate([turns[i, tap]] * 3, axis=0) for i in range(2)]
+            value = turn(value, cosine, sine)
+        slot = (tap - MARGIN) % SLOTS
+        if slots[slot] is not None:
+            value = value[0] + slots[slot][0], value[1] + slots[slot][1]
+        slots[slot] = value
     for pair in range(SLOTS // 2):
         one, two = slots[2 * pair], slots[2 * pair + 1]
-        real = jnp.concatenate([one[:, 0:128], two[:, 0:128]], axis=1)
-        imag = jnp.concatenate([one[:, 128:256], two[:, 128:256]], axis=1)
+        real = jnp.concatenate([one[0], two[0]], axis=1)
+        imag = jnp.concatenate([one[1], two[1]], axis=1)
         high, low = split(jnp.concatenate([real, imag], axis=0))
         out = dot(table_y_ref[...], jnp.concatenate([high, low, high], axis=0))
         planes_ref[2 * pair] = out[:, 0:128]
         planes_ref[2 * pair + 1] = out[:, 128:256]
 
 
-def spectrum_body(update, order, lists, blend, cell_row, cells, mask, table0, table3, table_y_ref, twiddle, out_ref, got, planes, sems):
+def gathered_place(count, distance):
+    place, size = 0, 1
+    for bits in gather_rounds(count):
+        for bit in bits:
+            place = place + size * ((distance >> bit) & 1)
+            size *= 2
+    return place
+
+
+def spectrum_kernel(update, count, order, lists, blend, cell_row, near, far, table, turns, table_y_ref, out_ref, got, flat, lines, spread, planes, sems):
     view = order[update]
-    copies = []
+    own = lax.axis_index("blk")
+    half = count // 2
     for k in range(2):
-        row = cell_row[lists[0, view, k]]
-        copy = pltpu.make_async_copy(cells.at[row], got.at[k], sems.at[k])
-        copy.start()
-        copies.append(copy)
-    for copy in copies:
-        copy.wait()
-    total = blend[0, view, 0] + blend[0, view, 1]
-    flat = None
+        place = gathered_place(count, cell_row[lists[0, k, view]] ^ own)
+
+        @pl.when(place < half)
+        def _():
+            pltpu.make_async_copy(near.at[place], got.at[k], sems.at[k]).start()
+
+        @pl.when(place >= half)
+        def _():
+            pltpu.make_async_copy(far.at[place - half], got.at[k], sems.at[k]).start()
+
     for k in range(2):
-        line = got[k].astype(F32)[update : update + 1, :]
-        weight = blend[0, view, k] / total * (2.0 / float(PAD**3))
-        part = line * (weight / jnp.sum(line, axis=1, keepdims=True))
-        flat = part if flat is None else flat + part
-    tap_stage(flat, mask[...], table0, table3, table_y_ref, planes)
-    z_stage(planes, twiddle, out_ref)
-
-
-def prep_kernel(est, obs0, obs1, pack_x, u_out, o0_out, o1_out, z0, z1, y0, y1, x0, x1):
-    unflatten(est, u_out)
-    pack_slabs(u_out, pack_x, x0, x1, y0, y1, z0, z1)
-    unflatten(obs0, o0_out)
-    unflatten(obs1, o1_out)
-
-
-def field_kernel(present, u, zm, zp, ym, yp, xm, xp, unpack_x, ea, gy, out, high, low, lines):
-    assemble(present, u, unpack_x, (zm, zp, ym, yp, xm, xp), high, low)
+        pltpu.make_async_copy(near.at[0], got.at[k], sems.at[k]).wait()
+    total = blend[0, 0, view] + blend[0, 1, view]
+    value = None
+    for k in range(2):
+        line = got[k].astype(F32)[CELLROWS * update : CELLROWS * (update + 1), :]
+        weight = blend[0, k, view] / total * (2.0 / float(PAD**3))
+        part = line * (weight / jnp.sum(line))
+        value = part if value is None else value + part
+    flat[...] = value
+    tap_stage(flat, lines, spread, table, turns, table_y_ref, planes)
+    z_stage(planes, out_ref)
+
+
+def grid_bits(count):
+    low_count = count.bit_length() - 2
+    bits = [[bit for bit in range(low_count) if bit % 3 == axis] for axis in range(3)]
+    bits[2] = [low_count] + bits[2]
+    return bits
+
+
+def gather_rounds(count):
+    bits = list(range(count.bit_length() - 1))
+    rounds = [bits[:1]]
+    bits = bits[1:]
+    while bits:
+        rounds.append(bits[:2])
+        bits = bits[2:]
+    return rounds[::-1]
+
+
+def odd_places(count):
+    own = lax.axis_index("blk")
+    return [((own >> bits[0]) & 1) == 1 if bits else own < 0 for bits in grid_bits(count)]
+
+
+def store_slabs(count, slabs, outs):
+    for odd, pair, refs in zip(odd_places(count), slabs, outs):
+        low, high = pair
+        refs[0][...] = jnp.where(odd, low, high)
+        refs[1][...] = jnp.where(odd, high, low)
+
+
+def start_kernel(count, order, cells, est, u_out, cells_out, first_out, z0, z1, y0, y1, x1, pad):
+    zero = jnp.zeros((2, CELLROWS * 128), F32)
+    pad[...] = zero
+    for update in range(UPDATES):
+        pad[update : update + 1, 0:KS3] = cells[order[update]]
+    wide = pad[...].astype(BF16).astype(F32)
+    for update in range(UPDATES):
+        rows = [wide[update : update + 1, 128 * row : 128 * (row + 1)] for row in range(CELLROWS)]
+        block = jnp.concatenate(rows, axis=0).astype(BF16)
+        here = slice(CELLROWS * update, CELLROWS * (update + 1))
+        cells_out[here, :] = block
+        first_out[here, :] = block
+    unflatten(lambda row: est[pl.ds(row, 8, stride=3), :], u_out)
+    store_slabs(count, pack_slabs(u_out), ((z0, z1), (y0, y1), (first_out.at[2 * CELLROWS :], x1)))
+
+
+def views_kernel(order, observed, o0, o1, wide):
+    step_rows = 32
+
+    @pl.loop(0, FLAT // step_rows)
+    def _(step):
+        for row in range(step_rows):
+            at = step * step_rows + row
+            lanes = pl.ds(pl.multiple_of(at * 128, 128), 128)
+            wide[pl.ds(pl.multiple_of(at * 8, 8), VIEWS), :] = observed[0, :, lanes].astype(F32)
+
+    for update, out in enumerate((o0, o1)):
+        view = order[update]
+        unflatten(lambda row: wide[pl.ds(8 * row + view, 8, stride=24), :], out)
+
+
+def field_kernel(count, present, u, z0, z1, y0, y1, x0, x1, ea, gy, out, high, low, lines):
+    margins = ((z0[...], z1[...]), (y0[...], y1[...]), (x0[2 * CELLROWS :, :] if x0.shape[0] > 192 else x0[...], x1[...]))
+    assemble(present, odd_places(count), u, margins, high, low)
     lines_stage(high, low, ea, lines, SLOTS * PAD, 256)
     y_stage(lines, gy, PAD, out)
 
@@ -476,13 +571,9 @@
         new_ref[half] = jnp.where(alive, core * correction[:, 128 * half : 128 * (half + 1)], core)
 
 
-def spectrum_kernel(update, *refs):
-    spectrum_body(update, *refs)
-
-
-def first_kernel(tissue, planes, kernel, u, o, ea, ei, gh, gb, twiddle, pack_x, u_out, z0, z1, y0, y1, x0, x1, planes2, lines):
+def first_kernel(count, tissue, planes, kernel, u, o, ea, ei, gh, gb, twiddle, u_out, z0, z1, y0, y1, x0, x1, planes2, lines):
     update_body(tissue, planes, kernel, u, o, (ea, ei, gh, gb, twiddle), (planes2, lines), u_out)
-    pack_slabs(u_out, pack_x, x0, x1, y0, y1, z0, z1)
+    store_slabs(count, pack_slabs(u_out), ((z0, z1), (y0, y1), (x0, x1)))
 
 
 def last_kernel(tissue, planes, kernel, u, o, ea, ei, gh, gb, twiddle, out, planes2, lines, fresh):
@@ -500,7 +591,9 @@
     return jax.ShapeDtypeStruct(dims, kind)
 
 
-SLABS = [shape((192, 128), BF16)] * 2 + [shape((128, 256), BF16)] * 2 + [shape((192, 128), BF16)] * 2
+SLAB = shape((192, 128), BF16)
+WIDE_SLAB = shape((256, 128), BF16)
+CELLS = shape((UPDATES * CELLROWS, 128), BF16)
 ROWS = shape((2, SLOTS * E, 128))
 ROWS_V = pltpu.VMEM((2, SLOTS * E, 128), F32)
 PLANES = shape((SLOTS, 128, 128))
@@ -521,102 +614,131 @@
     )(*args)
 
 
-def neighbour_pairs(count):
-    low_count = count.bit_length() - 2
-    places = []
+def far_pairs(count, axis):
+    bits = grid_bits(count)[axis]
+    extent = 2 ** len(bits)
+    pairs = []
     for number in range(count):
-        at = [0, 0, 0]
-        for bit in range(low_count):
-            at[bit % 3] += number // 2**bit % 2 * 2 ** (bit // 3)
-        at[2] = 2 * at[2] + number // 2**low_count % 2
-        places.append(tuple(at))
-    number_at = {at: number for number, at in enumerate(places)}
-    pairs = []
-    for face in range(6):
-        axis, step = face // 2, -1 if face % 2 == 0 else 1
-        found = []
-        for number, at in enumerate(places):
-            moved = list(at)
-            moved[axis] += step
-            if tuple(moved) in number_at:
-                found.append((number_at[tuple(moved)], number))
-        pairs.append(found)
+        at = sum(((number >> bit) & 1) << level for level, bit in enumerate(bits))
+        moved = at + 1 if at % 2 else at - 1
+        if 0 <= moved < extent:
+            other = number
+            for level, bit in enumerate(bits):
+                other = other & ~(1 << bit) | ((moved >> level) & 1) << bit
+            pairs.append((number, other))
     return pairs
 
 
-def exchange(slabs, pairs):
-    out = []
-    for face in range(6):
-        sent = slabs[face ^ 1]
-        out.append(lax.ppermute(sent, "blk", pairs[face]) if pairs[face] else jnp.zeros_like(sent))
-    return out
+def swap(value, distance, count):
+    return lax.ppermute(value, "blk", [(number, number ^ distance) for number in range(count)])
+
+
+def near_swap(value, axis, count):
+    bits = grid_bits(count)[axis]
+    return swap(value, 1 << bits[0], count) if bits else jnp.zeros_like(value)
+
+
+def far_swap(value, axis, count):
+    pairs = far_pairs(count, axis)
+    return lax.ppermute(value, "blk", pairs) if pairs else jnp.zeros_like(value)
 
 
 def local(estimate, observed, psf_cells, tissue, neighbours, psf_list, psf_blend, cell_row, view_order):
     count = lax.axis_size("blk")
-    pairs = neighbour_pairs(count)
     ea = jnp.asarray(stacked(table_space_to_lines(), 0))
     ei = jnp.asarray(stacked(table_lines_to_space(), 0))
     gy = jnp.asarray(stacked(table_y(PAD), 1))
     gh = jnp.asarray(stacked(table_y(E), 1))
     gb = jnp.asarray(stacked(table_y_back(), 1))
     gt = jnp.asarray(stacked(table_y_taps(), 1))
-    taps0 = jnp.asarray(stacked(table_taps(0), 0))
-    taps3 = jnp.asarray(stacked(table_taps(3), 0))
-    mask = jnp.asarray(table_tap_mask().astype(np.float32))
+    taps = jnp.asarray(table_taps())
+    turns = jnp.asarray(table_tap_turns())
     twiddle = jnp.asarray(table_twiddle())
-    pack_x = jnp.asarray(table_pack_x())
-    unpack_x = jnp.asarray(table_unpack_x())
-
-    views = jnp.concatenate(
-        [lax.dynamic_slice_in_dim(psf_cells[0], view_order[u], 1, 0) for u in range(UPDATES)], axis=0
+    lists = jnp.swapaxes(psf_list, 1, 2)
+    blend = jnp.swapaxes(psf_blend, 1, 2)
+
+    rows, cells, first, z0, z1, y0, y1, x1 = call(
+        functools.partial(start_kernel, count),
+        [SM, VM, VM],
+        [ROWS, CELLS, shape((UPDATES * CELLROWS + 192, 128), BF16), SLAB, SLAB, WIDE_SLAB, WIDE_SLAB, SLAB],
+        (view_order, jnp.swapaxes(psf_cells, 0, 1), estimate.reshape(FLAT, 128)),
+        [pltpu.VMEM((UPDATES, CELLROWS * 128), F32)],
+        name="start",
     )
-    views = jnp.pad(views.astype(BF16), ((0, 0), (0, CELLPAD - KS3)))
-    cells = lax.all_gather(views, "blk", axis=0, tiled=False)
-
-    seen = [
-        lax.dynamic_index_in_dim(observed[0], view_order[u], 0, keepdims=False).astype(F32).reshape(FLAT, 128)
-        for u in range(UPDATES)
-    ]
-    flat = estimate.reshape(FLAT, 128)
-    prep = call(
-        prep_kernel, [VM] * 4, [ROWS, ROWS, ROWS] + SLABS, (flat, seen[0], seen[1], pack_x), name="prep"
+    targets = call(
+        views_kernel, [SM, VM], [ROWS, ROWS], (view_order, observed), [pltpu.VMEM((8 * FLAT, 128), F32)], name="views"
     )
-    rows, targets, slabs = prep[0], prep[1:3], prep[3:]
+    pair_bits = [bits[0] if bits else None for bits in grid_bits(count)]
+    near_x, near_y = None, None
+    held = cells
+    rounds = gather_rounds(count)
+    for bits in rounds[:-1]:
+        arrived = [held]
+        size = held.shape[0]
+        for part in range(1, 2 ** len(bits)):
+            distance = sum(((part >> level) & 1) << bit for level, bit in enumerate(bits))
+            sent = held
+            if distance == 1 << pair_bits[2] and held is cells:
+                near_x = swap(first, distance, count)
+                arrived.append(near_x[:size])
+            elif pair_bits[1] is not None and distance == 1 << pair_bits[1]:
+                both = swap(jnp.concatenate([held, y0], axis=0), distance, count)
+                near_y = both[size:]
+                arrived.append(both[:size])
+            else:
+                arrived.append(swap(held, distance, count))
+        held = jnp.concatenate(arrived, axis=0)
+    if near_x is None:
+        near_x = near_swap(first, 2, count)
+    if near_y is None:
+        near_y = near_swap(y0, 1, count)
+    far_z, far_y, far_x = far_swap(z1, 0, count), far_swap(y1, 1, count), far_swap(x1, 2, count)
+    near_z = near_swap(z0, 0, count)
+    other = swap(held, 1, count)
+    near_cells, far_cells = [v.reshape(count // 2, UPDATES * CELLROWS, 128) for v in (held, other)]
 
     def spectrum(update):
         return call(
-            lambda *refs: spectrum_kernel(update, *refs),
-            [SM] * 4 + [ANY] + [VM] * 5,
+            functools.partial(spectrum_kernel, update, count),
+            [SM] * 4 + [ANY] * 2 + [VM] * 3,
             PLANES,
-            (view_order, psf_list, psf_blend, cell_row, cells, mask, taps0, taps3, gt, twiddle),
-            [pltpu.VMEM((2, 2, CELLPAD), BF16), PLANES_V, pltpu.SemaphoreType.DMA((2,))],
+            (view_order, lists, blend, cell_row, near_cells, far_cells, taps, turns, gt),
+            [
+                pltpu.VMEM((2, UPDATES * CELLROWS, 128), BF16),
+                pltpu.VMEM((CELLROWS, 128), F32),
+                pltpu.VMEM((3, TAPS, 128), F32),
+                pltpu.VMEM((TAPS * TAPS, 128), F32),
+                PLANES_V,
+                pltpu.SemaphoreType.DMA((2,)),
+            ],
             name="spectrum",
         )
 
     def field(rows, margins):
         return call(
-            field_kernel,
-            [SM] + [VM] * 10,
+            functools.partial(field_kernel, count),
+            [SM] + [VM] * 9,
             PLANES,
-            (neighbours, rows, *margins, unpack_x, ea, gy),
+            (neighbours, rows, *margins, ea, gy),
             [pltpu.VMEM((SLOTS * PAD, LANES), BF16)] * 2 + [pltpu.VMEM((SLOTS * PAD, LANES), F32)],
             name="field",
         )
 
-    margins = exchange(slabs, pairs)
-    planes = field(rows, margins)
+    planes = field(rows, (near_z, far_z, near_y, far_y, near_x, far_x))
     kernel = spectrum(0)
     first = call(
-        first_kernel,
-        [SM] + [VM] * 10,
-        [ROWS] + SLABS,
-        (tissue, planes, kernel, rows, targets[0], ea, ei, gh, gb, twiddle, pack_x),
+        functools.partial(first_kernel, count),
+        [SM] + [VM] * 9,
+        [ROWS, SLAB, SLAB, WIDE_SLAB, WIDE_SLAB, SLAB, SLAB],
+        (tissue, planes, kernel, rows, targets[0], ea, ei, gh, gb, twiddle),
         [PLANES_V, LINES_V],
         name="first",
     )
     rows, slabs = first[0], first[1:]
-    margins = exchange(slabs, pairs)
+    margins = []
+    for axis in range(3):
+        margins.append(near_swap(slabs[2 * axis], axis, count))
+        margins.append(far_swap(slabs[2 * axis + 1], axis, count))
     kernel = spectrum(1)
     planes = field(rows, margins)
     out = call(

time: 112 us -> 61 us (0.54)
  the two profiles are of different devices: /device:TPU:23 before, /device:TPU:12 now
where the time goes in v2:
time: 61 us; the launch traced here: 60.8 us
  starting transfers between devices  22.3 us (37%)
  Pallas kernels  21.9 us (36%)
  waiting for transfers between devices  11.2 us (18%)
  local copies, waits for them, and re-layouts  4.23 us (7%)
  between operations  1.04 us (2%)
    pallas_call x8, Pallas kernels, call(): pl.pallas_call(body, in_specs=ins, out_specs=[VM] * len(outs) if many els...  21.9 us
    ppermute x4, starting transfers between devices, far_swap(): return lax.ppermute(value, 'blk', pairs) if pairs else jnp.zeros_like(value)  12.3 us
    ppermute x11, starting transfers between devices, swap(): lax.ppermute(value, 'blk', [(number, number ^ distance) for number in ran...  10 us
    ppermute x11, waiting for transfers between devices, swap(): lax.ppermute(value, 'blk', [(number, number ^ distance) for number in ran...  8.4 us
    unnamed x41, local copies, waits for them, and re-layouts  4.18 us
    ppermute x4, waiting for transfers between devices, far_swap(): return lax.ppermute(value, 'blk', pairs) if pairs else jnp.zeros_like(value)  2.81 us
  transfers between devices with their start and end apart: 15, of which 5 were waited for; matrix products, arithmetic and copies ran while one was open for 0% of the time, Pallas kernels for 10%

profile of v2, /device:TPU:12, one launch (start us, length us, event | category | flops | bytes accessed | tf_op | source)
XLA Modules:
  0.0 60.8 jit_solution(8538187284745795613)
XLA Ops:
  0.0 1.0 %copy-done.5 = f32[1,110592]{1,0:T(1,128)S(1)} copy-done((f32[1,110592]{1,0:T(1,128)S(1)}, f32[1,110592]{1,0:T(1,128)}, u32[]{:S(2)}) %copy-start.5) | copy-done | bytes 442392
  1.0 0.9 %copy-done.11 = f32[1,6,4913]{2,0,1:T(1,128)S(1)} copy-done((f32[1,6,4913]{2,0,1:T(1,128)S(1)}, f32[1,6,4913]{2,0,1:T(1,128)}, u32[]{:S(2)}) %copy-start.11) | copy-done | bytes 117936
  1.9 0.7 %copy-done.12 = s32[6]{0:T(128)S(1)} copy-done((s32[6]{0:T(128)S(1)}, s32[6]{0:T(128)}, u32[]{:S(2)}) %copy-start.12) | copy-done | bytes 48
  2.6 1.7 %start.1 = (f32[2,768,128]{2,1,0:T(8,128)S(1)}, bf16[80,128]{1,0:T(8,128)(2,1)S(1)}, bf16[272,128]{1,0:T(8,128)(2,1)S(1)}, bf16[192,128]{1,0:T(8,128)(2,1)S(1)},...) custom-call(s32[6]{0:T(128)S(1)} %copy-done.12, ...), custom_call_target="tpu_custom_call" | custom-call | tf_op jit(solution)/shard_map/start/pallas_call | solution.py:606
  4.2 0.5 collective-permute-start.2
  4.7 2.7 %collective-permute-start.4 = (bf16[80,128]{1,0:T(8,128)(2,1)S(1)}, bf16[80,128]{1,0:T(8,128)(2,1)S(1)}, u32[]{:S(2)}, u32[]{:S(2)}) collective-permute-start(bf16[80,128]{1,0:T(8,128)(2,1)S(1)} %get-tuple-element.23), channel_id=1, source_target_pairs={{0,24},{1,25},{2,26},{3,27},{4,28},{5,29},{6,30},{7,31},{8,16},{9,... | collective-permute-start | bytes 61448 | tf_op jit(solution)/shard_map/ppermute | solution.py:633
  7.4 1.2 %collective-permute-start.3 = (bf16[272,128]{1,0:T(8,128)(2,1)S(1)}, bf16[272,128]{1,0:T(8,128)(2,1)S(1)}, u32[]{:S(2)}, u32[]{:S(2)}) collective-permute-start(bf16[272,128]{1,0:T(8,128)(2,1)S(1)} %get-tuple-element.24), channel_id=1, source_target_pairs={{0,16},{1,17},{2,18},{3,19},{4,20},{5,21},{6,22},{7,23},{8,24},{9,... | collective-permute-start | bytes 208904 | tf_op jit(solution)/shard_map/ppermute | solution.py:633
  8.6 4.1 %collective-permute-done.3.x0 = bf16[272,128]{1,0:T(8,128)(2,1)S(1)} collective-permute-done((bf16[272,128]{1,0:T(8,128)(2,1)S(1)}, bf16[272,128]{1,0:T(8,128)(2,1)S(1)}, u32[]{:S(2)}, u32[]{:S(2)}) %collective-permute-start.3) | collective-permute-done | bytes 69664 | tf_op jit(solution)/shard_map/ppermute | solution.py:633
  12.8 1.6 %collective-permute-start.5 = (bf16[576,128]{1,0:T(8,128)(2,1)S(1)}, bf16[576,128]{1,0:T(8,128)(2,1)S(1)}, u32[]{:S(2)}, u32[]{:S(2)}) collective-permute-start(bf16[576,128]{1,0:T(8,128)(2,1)S(1)} %constant_dynamic-update-slice_fusion), channel_id=1, source_target_pairs={{0,2},{1,3},{2,0},{3,1},{4,6},{5,7},{6,4},{7,5},{8,10},{9,11},{10,... | collective-permute-start | bytes 442376 | tf_op jit(solution)/shard_map/ppermute | solution.py:633
  14.3 0.5 collective-permute-start.7
  14.8 1.5 %collective-permute-start.8 = (bf16[320,128]{1,0:T(8,128)(2,1)S(1)}, bf16[320,128]{1,0:T(8,128)(2,1)S(1)}, u32[]{:S(2)}, u32[]{:S(2)}) collective-permute-start(bf16[320,128]{1,0:T(8,128)(2,1)S(1)} %pad_maximum_fusion), channel_id=1, source_target_pairs={{0,6},{1,7},{2,4},{3,5},{4,2},{5,3},{6,0},{7,1},{8,14},{9,15},{10,... | collective-permute-start | bytes 245768 | tf_op jit(solution)/shard_map/ppermute | solution.py:633
  16.3 2.5 %collective-permute-done.5 = bf16[576,128]{1,0:T(8,128)(2,1)S(1)} collective-permute-done((bf16[576,128]{1,0:T(8,128)(2,1)S(1)}, bf16[576,128]{1,0:T(8,128)(2,1)S(1)}, u32[]{:S(2)}, u32[]{:S(2)}) %collective-permute-start.5) | collective-permute-done | bytes 147488 | tf_op jit(solution)/shard_map/ppermute | solution.py:633
  18.9 0.0 collective-permute-done.7
  18.9 1.3 %collective-permute-done.8 = bf16[320,128]{1,0:T(8,128)(2,1)S(1)} collective-permute-done((bf16[320,128]{1,0:T(8,128)(2,1)S(1)}, bf16[320,128]{1,0:T(8,128)(2,1)S(1)}, u32[]{:S(2)}, u32[]{:S(2)}) %collective-permute-start.8) | collective-permute-done | bytes 81952 | tf_op jit(solution)/shard_map/ppermute | solution.py:633
  20.2 0.1 collective-permute-start.9
  20.3 0.5 collective-permute-start
  20.8 3.6 %collective-permute-start.1 = (bf16[192,128]{1,0:T(8,128)(2,1)S(1)}, bf16[192,128]{1,0:T(8,128)(2,1)S(1)}, u32[]{:S(2)}, u32[]{:S(2)}) collective-permute-start(bf16[192,128]{1,0:T(8,128)(2,1)S(1)} %get-tuple-element.22), channel_id=1, source_target_pairs={{1,8},{3,10},{5,12},{7,14},{8,1},{10,3},{12,5},{14,7},{17,24},{19,... | collective-permute-start | bytes 147464 | tf_op jit(solution)/shard_map/ppermute | solution.py:643
  24.4 3.3 %collective-permute-start.6 = (bf16[192,128]{1,0:T(8,128)(2,1)S(1)}, bf16[192,128]{1,0:T(8,128)(2,1)S(1)}, u32[]{:S(2)}, u32[]{:S(2)}) collective-permute-start(bf16[192,128]{1,0:T(8,128)(2,1)S(1)} %get-tuple-element.26), channel_id=1, source_target_pairs={{4,16},{5,17},{6,18},{7,19},{12,24},{13,25},{14,26},{15,27},{16,4}... | collective-permute-start | bytes 147464 | tf_op jit(solution)/shard_map/ppermute | solution.py:643
  28.4 1.5 %copy-done.1 = bf16[1,6,110592]{2,1,0:T(8,128)(2,1)S(1)} copy-done((bf16[1,6,110592]{2,1,0:T(8,128)(2,1)S(1)}, bf16[1,6,110592]{2,1,0:T(8,128)(2,1)}, u32[]{:S(2)}) %copy-start.1) | copy-done | bytes 1327128
  29.8 2.4 %views.1 = (f32[2,768,128]{2,1,0:T(8,128)S(1)}, f32[2,768,128]{2,1,0:T(8,128)S(1)}) custom-call(s32[6]{0:T(128)S(1)} %copy-done.12, bf16[1,6,110592]{2,1,0:T(8,128)(2,1)S(1)} %copy-done.1), custom_call_target="tpu_custom_call" | custom-call | tf_op jit(solution)/shard_map/views/pallas_call | solution.py:606
  32.4 1.7 %field.2.planes = f32[16,128,128]{2,1,0:T(8,128)S(1)} custom-call(s32[1,6]{1,0:T(1,128)S(1)} %copy-done.16, f32[2,768,128]{2,1,0:T(8,128)S(1)} %get-tuple-element.20.u, bf16[192,128]{1,0:T(8,128)(2,1)S(1)} %collective-permute-done.z0, bf16[192,128]{1,0:T(8,128)(2,1)S(1)} %collective-permute-done.1.z1, bf16[256,128]{1,0:T(8,128)(2,1)S(1)} %slice.13.y0, ...), custom_call_target="tpu_custom_call" | custom-call | tf_op jit(solution)/shard_map/field/pallas_call | solution.py:606
  34.2 2.1 %spectrum.2.kernel = f32[16,128,128]{2,1,0:T(8,128)S(1)} custom-call(s32[6]{0:T(128)S(1)} %copy-done.13, s32[1,2,6]{2,1,0:T(2,128)S(1)} %bitcast.13, f32[1,2,6]{2,1,0:T(2,128)S(1)} %bitcast.15, s32[32]{0:T(128)S(1)} %copy-done.17, bf16[16,80,128]{2,1,0:T(8,128)(2,1)S(1)} %bitcast.7, bf16[16,80,128]{2,1,0:T(8,128)(2,1)S(1)} %bitcast.9, ...), custom_call_target="tpu_custom_call" | custom-call | tf_op jit(solution)/shard_map/spectrum/pallas_call | solution.py:606
  36.4 5.0 %first.1 = (f32[2,768,128]{2,1,0:T(8,128)S(1)}, bf16[192,128]{1,0:T(8,128)(2,1)S(1)}, bf16[192,128]{1,0:T(8,128)(2,1)S(1)}, bf16[256,128]{1,0:T(8,128)(2,1)S(1)}...) custom-call(s32[1]{0:T(128)S(6)} %copy.29.tissue, ...), custom_call_target="tpu_custom_call" | custom-call | tf_op jit(solution)/shard_map/first/pallas_call | solution.py:606
  41.4 1.4 %collective-permute-start.12 = (bf16[256,128]{1,0:T(8,128)(2,1)S(1)}, bf16[256,128]{1,0:T(8,128)(2,1)S(1)}, u32[]{:S(2)}, u32[]{:S(2)}) collective-permute-start(bf16[256,128]{1,0:T(8,128)(2,1)S(1)} %get-tuple-element.31), channel_id=1, source_target_pairs={{0,2},{1,3},{2,0},{3,1},{4,6},{5,7},{6,4},{7,5},{8,10},{9,11},{10,... | collective-permute-start | bytes 196616 | tf_op jit(solution)/shard_map/ppermute | solution.py:633
  42.9 3.1 %collective-permute-start.11 = (bf16[192,128]{1,0:T(8,128)(2,1)S(1)}, bf16[192,128]{1,0:T(8,128)(2,1)S(1)}, u32[]{:S(2)}, u32[]{:S(2)}) collective-permute-start(bf16[192,128]{1,0:T(8,128)(2,1)S(1)} %get-tuple-element.30), channel_id=1, source_target_pairs={{1,8},{3,10},{5,12},{7,14},{8,1},{10,3},{12,5},{14,7},{17,24},{19,... | collective-permute-start | bytes 147464 | tf_op jit(solution)/shard_map/ppermute | solution.py:643
  45.9 0.1 collective-permute-start.13
  46.0 2.3 %collective-permute-start.14 = (bf16[192,128]{1,0:T(8,128)(2,1)S(1)}, bf16[192,128]{1,0:T(8,128)(2,1)S(1)}, u32[]{:S(2)}, u32[]{:S(2)}) collective-permute-start(bf16[192,128]{1,0:T(8,128)(2,1)S(1)} %get-tuple-element.33), channel_id=1, source_target_pairs={{4,16},{5,17},{6,18},{7,19},{12,24},{13,25},{14,26},{15,27},{16,4}... | collective-permute-start | bytes 147464 | tf_op jit(solution)/shard_map/ppermute | solution.py:643
  48.3 2.1 %spectrum.3.kernel = f32[16,128,128]{2,1,0:T(8,128)S(1)} custom-call(s32[6]{0:T(128)S(1)} %copy-done.13, s32[1,2,6]{2,1,0:T(2,128)S(1)} %bitcast.14, f32[1,2,6]{2,1,0:T(2,128)S(1)} %bitcast.16, s32[32]{0:T(128)S(1)} %copy-done.17, bf16[16,80,128]{2,1,0:T(8,128)(2,1)S(1)} %bitcast.8, bf16[16,80,128]{2,1,0:T(8,128)(2,1)S(1)} %bitcast.10, ...), custom_call_target="tpu_custom_call" | custom-call | tf_op jit(solution)/shard_map/spectrum/pallas_call | solution.py:606
  50.5 0.5 collective-permute-done.13.x0
  51.0 2.8 %collective-permute-done.14.x1 = bf16[192,128]{1,0:T(8,128)(2,1)S(1)} collective-permute-done((bf16[192,128]{1,0:T(8,128)(2,1)S(1)}, bf16[192,128]{1,0:T(8,128)(2,1)S(1)}, u32[]{:S(2)}, u32[]{:S(2)}) %collective-permute-start.14) | collective-permute-done | bytes 49184 | tf_op jit(solution)/shard_map/ppermute | solution.py:643
  53.8 1.7 %field.3.planes = f32[16,128,128]{2,1,0:T(8,128)S(1)} custom-call(s32[1,6]{1,0:T(1,128)S(1)} %copy-done.16, f32[2,768,128]{2,1,0:T(8,128)S(1)} %get-tuple-element.28.u, bf16[192,128]{1,0:T(8,128)(2,1)S(1)} %collective-permute-done.10.z0, bf16[192,128]{1,0:T(8,128)(2,1)S(1)} %collective-permute-done.11.z1, bf16[256,128]{1,0:T(8,128)(2,1)S(1)} %collective-permute-done.12.y0, ...), custom_call_target="tpu_custom_call" | custom-call | tf_op jit(solution)/shard_map/field/pallas_call | solution.py:606
  55.5 5.3 %last.1 = f32[864,128]{1,0:T(8,128)} custom-call(s32[1]{0:T(128)S(6)} %copy.29.tissue, f32[16,128,128]{2,1,0:T(8,128)S(1)} %field.3.planes, f32[16,128,128]{2,1,0:T(8,128)S(1)} %spectrum.3.kernel, f32[2,768,128]{2,1,0:T(8,128)S(1)} %get-tuple-element.28.u, f32[2,768,128]{2,1,0:T(8,128)S(1)} %get-tuple-element.34.o, bf16[768,256]{1,0:T(8,128)(2,1)S(1)} %copy-done, ...), custom_call_target="tpu_custom_call" | custom-call | tf_op jit(solution)/shard_map/last/pallas_call | solution.py:606
  (53 shorter events, 0.2 us)
Async XLA Ops:
  0.0 1.0 %copy-start.5 = (f32[1,110592]{1,0:T(1,128)S(1)}, f32[1,110592]{1,0:T(1,128)}, u32[]{:S(2)}) copy-start(f32[1,110592]{1,0:T(1,128)} %param.18) | copy-start | bytes 1327108
  1.0 0.9 %copy-start.11 = (f32[1,6,4913]{2,0,1:T(1,128)S(1)}, f32[1,6,4913]{2,0,1:T(1,128)}, u32[]{:S(2)}) copy-start(f32[1,6,4913]{2,0,1:T(1,128)} %param.20) | copy-start | bytes 353740
  2.6 29.8 %copy-start = (bf16[768,256]{1,0:T(8,128)(2,1)S(1)}, bf16[768,256]{1,0:T(8,128)(2,1)}, u32[]{:S(2)}) copy-start(bf16[768,256]{1,0:T(8,128)(2,1)} %constant.20.clone.ea) | copy-start | bytes 1179652
  2.6 29.8 %copy-start.6 = (bf16[128,384]{1,0:T(8,128)(2,1)S(1)}, bf16[128,384]{1,0:T(8,128)(2,1)}, u32[]{:S(2)}) copy-start(bf16[128,384]{1,0:T(8,128)(2,1)} %constant.22.clone.gy) | copy-start | bytes 294916
  2.6 29.8 %copy-start.16 = (s32[1,6]{1,0:T(1,128)S(1)}, s32[1,6]{1,0:T(1,128)}, u32[]{:S(2)}) copy-start(s32[1,6]{1,0:T(1,128)} %present.3) | copy-start | bytes 76
  4.2 4.4 %collective-permute-start.2 = (bf16[80,128]{1,0:T(8,128)(2,1)S(1)}, bf16[80,128]{1,0:T(8,128)(2,1)S(1)}, u32[]{:S(2)}, u32[]{:S(2)}) collective-permute-start(bf16[80,128]{1,0:T(8,128)(2,1)S(1)} %get-tuple-element.23), channel_id=1, source_target_pairs={{0,8},{1,9},{2,10},{3,11},{4,12},{5,13},{6,14},{7,15},{8,0},{9,1},... | collective-permute-start | bytes 61448 | tf_op jit(solution)/shard_map/ppermute | solution.py:633
  4.7 8.0 %collective-permute-start.4 = (bf16[80,128]{1,0:T(8,128)(2,1)S(1)}, bf16[80,128]{1,0:T(8,128)(2,1)S(1)}, u32[]{:S(2)}, u32[]{:S(2)}) collective-permute-start(bf16[80,128]{1,0:T(8,128)(2,1)S(1)} %get-tuple-element.23), channel_id=1, source_target_pairs={{0,24},{1,25},{2,26},{3,27},{4,28},{5,29},{6,30},{7,31},{8,16},{9,... | collective-permute-start | bytes 61448 | tf_op jit(solution)/shard_map/ppermute | solution.py:633
  7.4 5.3 %collective-permute-start.3 = (bf16[272,128]{1,0:T(8,128)(2,1)S(1)}, bf16[272,128]{1,0:T(8,128)(2,1)S(1)}, u32[]{:S(2)}, u32[]{:S(2)}) collective-permute-start(bf16[272,128]{1,0:T(8,128)(2,1)S(1)} %get-tuple-element.24), channel_id=1, source_target_pairs={{0,16},{1,17},{2,18},{3,19},{4,20},{5,21},{6,22},{7,23},{8,24},{9,... | collective-permute-start | bytes 208904 | tf_op jit(solution)/shard_map/ppermute | solution.py:633
  12.8 6.1 %collective-permute-start.5 = (bf16[576,128]{1,0:T(8,128)(2,1)S(1)}, bf16[576,128]{1,0:T(8,128)(2,1)S(1)}, u32[]{:S(2)}, u32[]{:S(2)}) collective-permute-start(bf16[576,128]{1,0:T(8,128)(2,1)S(1)} %constant_dynamic-update-slice_fusion), channel_id=1, source_target_pairs={{0,2},{1,3},{2,0},{3,1},{4,6},{5,7},{6,4},{7,5},{8,10},{9,11},{10,... | collective-permute-start | bytes 442376 | tf_op jit(solution)/shard_map/ppermute | solution.py:633
  14.3 4.6 %collective-permute-start.7 = (bf16[320,128]{1,0:T(8,128)(2,1)S(1)}, bf16[320,128]{1,0:T(8,128)(2,1)S(1)}, u32[]{:S(2)}, u32[]{:S(2)}) collective-permute-start(bf16[320,128]{1,0:T(8,128)(2,1)S(1)} %pad_maximum_fusion), channel_id=1, source_target_pairs={{0,4},{1,5},{2,6},{3,7},{4,0},{5,1},{6,2},{7,3},{8,12},{9,13},{10,... | collective-permute-start | bytes 245768 | tf_op jit(solution)/shard_map/ppermute | solution.py:633
  14.8 5.3 %collective-permute-start.8 = (bf16[320,128]{1,0:T(8,128)(2,1)S(1)}, bf16[320,128]{1,0:T(8,128)(2,1)S(1)}, u32[]{:S(2)}, u32[]{:S(2)}) collective-permute-start(bf16[320,128]{1,0:T(8,128)(2,1)S(1)} %pad_maximum_fusion), channel_id=1, source_target_pairs={{0,6},{1,7},{2,4},{3,5},{4,2},{5,3},{6,0},{7,1},{8,14},{9,15},{10,... | collective-permute-start | bytes 245768 | tf_op jit(solution)/shard_map/ppermute | solution.py:633
  20.2 13.9 %collective-permute-start.9 = (bf16[1280,128]{1,0:T(8,128)(2,1)S(1)}, bf16[1280,128]{1,0:T(8,128)(2,1)S(1)}, u32[]{:S(2)}, u32[]{:S(2)}) collective-permute-start(bf16[1280,128]{1,0:T(8,128)(2,1)S(1)} %constant_dynamic-update-slice_fusion.5), channel_id=1, source_target_pairs={{0,1},{1,0},{2,3},{3,2},{4,5},{5,4},{6,7},{7,6},{8,9},{9,8},{10,11... | collective-permute-start | bytes 983048 | tf_op jit(solution)/shard_map/ppermute | solution.py:633
  20.3 12.0 %collective-permute-start = (bf16[192,128]{1,0:T(8,128)(2,1)S(1)}, bf16[192,128]{1,0:T(8,128)(2,1)S(1)}, u32[]{:S(2)}, u32[]{:S(2)}) collective-permute-start(bf16[192,128]{1,0:T(8,128)(2,1)S(1)} %get-tuple-element.21), channel_id=1, source_target_pairs={{0,1},{1,0},{2,3},{3,2},{4,5},{5,4},{6,7},{7,6},{8,9},{9,8},{10,11... | collective-permute-start | bytes 147464 | tf_op jit(solution)/shard_map/ppermute | solution.py:633
  20.8 11.6 %collective-permute-start.1 = (bf16[192,128]{1,0:T(8,128)(2,1)S(1)}, bf16[192,128]{1,0:T(8,128)(2,1)S(1)}, u32[]{:S(2)}, u32[]{:S(2)}) collective-permute-start(bf16[192,128]{1,0:T(8,128)(2,1)S(1)} %get-tuple-element.22), channel_id=1, source_target_pairs={{1,8},{3,10},{5,12},{7,14},{8,1},{10,3},{12,5},{14,7},{17,24},{19,... | collective-permute-start | bytes 147464 | tf_op jit(solution)/shard_map/ppermute | solution.py:643
  24.4 8.0 %collective-permute-start.6 = (bf16[192,128]{1,0:T(8,128)(2,1)S(1)}, bf16[192,128]{1,0:T(8,128)(2,1)S(1)}, u32[]{:S(2)}, u32[]{:S(2)}) collective-permute-start(bf16[192,128]{1,0:T(8,128)(2,1)S(1)} %get-tuple-element.26), channel_id=1, source_target_pairs={{4,16},{5,17},{6,18},{7,19},{12,24},{13,25},{14,26},{15,27},{16,4}... | collective-permute-start | bytes 147464 | tf_op jit(solution)/shard_map/ppermute | solution.py:643
  28.4 1.5 %copy-start.1 = (bf16[1,6,110592]{2,1,0:T(8,128)(2,1)S(1)}, bf16[1,6,110592]{2,1,0:T(8,128)(2,1)}, u32[]{:S(2)}) copy-start(bf16[1,6,110592]{2,1,0:T(8,128)(2,1)} %observed.1) | copy-start | bytes 3981316
  32.2 1.9 %copy-start.3 = (f32[2,17,8,128]{3,2,1,0:T(8,128)S(1)}, f32[2,17,8,128]{3,2,1,0:T(8,128)}, u32[]{:S(2)}) copy-start(f32[2,17,8,128]{3,2,1,0:T(8,128)} %constant.27.clone.turns) | copy-start | bytes 417796
  32.2 1.9 %copy-start.9 = (bf16[128,256]{1,0:T(8,128)(2,1)S(1)}, bf16[128,256]{1,0:T(8,128)(2,1)}, u32[]{:S(2)}) copy-start(bf16[128,256]{1,0:T(8,128)(2,1)} %constant.26.clone.table) | copy-start | bytes 196612
  32.2 1.9 %copy-start.10 = (bf16[128,144]{1,0:T(8,128)(2,1)S(1)}, bf16[128,144]{1,0:T(8,128)(2,1)}, u32[]{:S(2)}) copy-start(bf16[128,144]{1,0:T(8,128)(2,1)} %constant.25.clone.table_y_ref) | copy-start | bytes 110596
  32.2 1.9 %copy-start.13 = (s32[6]{0:T(128)S(1)}, s32[6]{0:T(128)}, u32[]{:S(2)}) copy-start(s32[6]{0:T(128)} %order.7) | copy-start | bytes 76
  32.2 1.9 %copy-start.14 = (s32[1,6,2]{1,2,0:T(2,128)S(1)}, s32[1,6,2]{1,2,0:T(2,128)}, u32[]{:S(2)}) copy-start(s32[1,6,2]{1,2,0:T(2,128)} %param.23) | copy-start | bytes 148
  32.3 1.9 %copy-start.15 = (f32[1,6,2]{1,2,0:T(2,128)S(1)}, f32[1,6,2]{1,2,0:T(2,128)}, u32[]{:S(2)}) copy-start(f32[1,6,2]{1,2,0:T(2,128)} %param.24) | copy-start | bytes 148
  32.3 1.9 %copy-start.17 = (s32[32]{0:T(128)S(1)}, s32[32]{0:T(128)}, u32[]{:S(2)}) copy-start(s32[32]{0:T(128)} %cell_row.3) | copy-start | bytes 388
  32.4 4.0 %copy-start.2 = (bf16[768,256]{1,0:T(8,128)(2,1)S(1)}, bf16[768,256]{1,0:T(8,128)(2,1)}, u32[]{:S(2)}) copy-start(bf16[768,256]{1,0:T(8,128)(2,1)} %constant.21.clone.ei) | copy-start | bytes 1179652
  32.4 4.0 %copy-start.4 = (f32[2,16,8,128]{3,2,1,0:T(8,128)S(1)}, f32[2,16,8,128]{3,2,1,0:T(8,128)}, u32[]{:S(2)}) copy-start(f32[2,16,8,128]{3,2,1,0:T(8,128)} %constant.28.clone.twiddle) | copy-start | bytes 393220
  32.4 4.0 %copy-start.7 = (bf16[128,288]{1,0:T(8,128)(2,1)S(1)}, bf16[128,288]{1,0:T(8,128)(2,1)}, u32[]{:S(2)}) copy-start(bf16[128,288]{1,0:T(8,128)(2,1)} %constant.23.clone.gh) | copy-start | bytes 221188
  32.4 4.0 %copy-start.8 = (bf16[96,384]{1,0:T(8,128)(2,1)S(1)}, bf16[96,384]{1,0:T(8,128)(2,1)}, u32[]{:S(2)}) copy-start(bf16[96,384]{1,0:T(8,128)(2,1)} %constant.24.clone.gb) | copy-start | bytes 221188
  41.4 12.4 %collective-permute-start.12 = (bf16[256,128]{1,0:T(8,128)(2,1)S(1)}, bf16[256,128]{1,0:T(8,128)(2,1)S(1)}, u32[]{:S(2)}, u32[]{:S(2)}) collective-permute-start(bf16[256,128]{1,0:T(8,128)(2,1)S(1)} %get-tuple-element.31), channel_id=1, source_target_pairs={{0,2},{1,3},{2,0},{3,1},{4,6},{5,7},{6,4},{7,5},{8,10},{9,11},{10,... | collective-permute-start | bytes 196616 | tf_op jit(solution)/shard_map/ppermute | solution.py:633
  42.9 7.6 %collective-permute-start.10 = (bf16[192,128]{1,0:T(8,128)(2,1)S(1)}, bf16[192,128]{1,0:T(8,128)(2,1)S(1)}, u32[]{:S(2)}, u32[]{:S(2)}) collective-permute-start(bf16[192,128]{1,0:T(8,128)(2,1)S(1)} %get-tuple-element.29), channel_id=1, source_target_pairs={{0,1},{1,0},{2,3},{3,2},{4,5},{5,4},{6,7},{7,6},{8,9},{9,8},{10,11... | collective-permute-start | bytes 147464 | tf_op jit(solution)/shard_map/ppermute | solution.py:633
  42.9 7.6 %collective-permute-start.11 = (bf16[192,128]{1,0:T(8,128)(2,1)S(1)}, bf16[192,128]{1,0:T(8,128)(2,1)S(1)}, u32[]{:S(2)}, u32[]{:S(2)}) collective-permute-start(bf16[192,128]{1,0:T(8,128)(2,1)S(1)} %get-tuple-element.30), channel_id=1, source_target_pairs={{1,8},{3,10},{5,12},{7,14},{8,1},{10,3},{12,5},{14,7},{17,24},{19,... | collective-permute-start | bytes 147464 | tf_op jit(solution)/shard_map/ppermute | solution.py:643
  45.9 5.1 %collective-permute-start.13 = (bf16[192,128]{1,0:T(8,128)(2,1)S(1)}, bf16[192,128]{1,0:T(8,128)(2,1)S(1)}, u32[]{:S(2)}, u32[]{:S(2)}) collective-permute-start(bf16[192,128]{1,0:T(8,128)(2,1)S(1)} %get-tuple-element.32), channel_id=1, source_target_pairs={{0,16},{1,17},{2,18},{3,19},{4,20},{5,21},{6,22},{7,23},{8,24},{9,... | collective-permute-start | bytes 147464 | tf_op jit(solution)/shard_map/ppermute | solution.py:633
  46.0 7.8 %collective-permute-start.14 = (bf16[192,128]{1,0:T(8,128)(2,1)S(1)}, bf16[192,128]{1,0:T(8,128)(2,1)S(1)}, u32[]{:S(2)}, u32[]{:S(2)}) collective-permute-start(bf16[192,128]{1,0:T(8,128)(2,1)S(1)} %get-tuple-element.33), channel_id=1, source_target_pairs={{4,16},{5,17},{6,18},{7,19},{12,24},{13,25},{14,26},{15,27},{16,4}... | collective-permute-start | bytes 147464 | tf_op jit(solution)/shard_map/ppermute | solution.py:643
  (1 other events, 0.7 us)

commit v3 on v2

--- a/solution.py
+++ b/solution.py
@@ -359,7 +359,7 @@
 
 
 def z_stage(planes_ref, out_ref):
-    @pl.loop(0, PAD // 8)
+    @pl.loop(0, PAD // 8, unroll=2)
     def _(step):
         rows = pl.ds(pl.multiple_of(8 * step, 8), 8)
         rows_imag = pl.ds(pl.multiple_of(8 * step + PAD, 8), 8)
@@ -371,7 +371,7 @@
 
 
 def filter_stage(planes_ref, kernel_ref, twiddle, conjugate, out_ref):
-    @pl.loop(0, PAD // 8)
+    @pl.loop(0, PAD // 8, unroll=2)
     def _(step):
         rows = pl.ds(pl.multiple_of(8 * step, 8), 8)
         rows_imag = pl.ds(pl.multiple_of(8 * step + PAD, 8), 8)
@@ -451,27 +451,17 @@
     return place
 
 
-def spectrum_kernel(update, count, order, lists, blend, cell_row, near, far, table, turns, table_y_ref, out_ref, got, flat, lines, spread, planes, sems):
+def spectrum_kernel(update, count, order, lists, blend, cell_row, near, far, table, turns, table_y_ref, out_ref, flat, lines, spread, planes):
     view = order[update]
     own = lax.axis_index("blk")
     half = count // 2
+    total = blend[0, 0, view] + blend[0, 1, view]
+    value = None
+    rows = slice(CELLROWS * update, CELLROWS * (update + 1))
     for k in range(2):
         place = gathered_place(count, cell_row[lists[0, k, view]] ^ own)
-
-        @pl.when(place < half)
-        def _():
-            pltpu.make_async_copy(near.at[place], got.at[k], sems.at[k]).start()
-
-        @pl.when(place >= half)
-        def _():
-            pltpu.make_async_copy(far.at[place - half], got.at[k], sems.at[k]).start()
-
-    for k in range(2):
-        pltpu.make_async_copy(near.at[0], got.at[k], sems.at[k]).wait()
-    total = blend[0, 0, view] + blend[0, 1, view]
-    value = None
-    for k in range(2):
-        line = got[k].astype(F32)[CELLROWS * update : CELLROWS * (update + 1), :]
+        inner = lax.rem(place, half)
+        line = jnp.where(place < half, near[inner].astype(F32), far[inner].astype(F32))[rows]
         weight = blend[0, k, view] / total * (2.0 / float(PAD**3))
         part = line * (weight / jnp.sum(line))
         value = part if value is None else value + part
@@ -502,88 +492,143 @@
     return [((own >> bits[0]) & 1) == 1 if bits else own < 0 for bits in grid_bits(count)]
 
 
+def slab_kinds(count):
+    return [
+        (axis, far)
+        for far in (0, 1)
+        for axis in (2, 1, 0)
+        if len(grid_bits(count)[axis]) > far
+    ]
+
+
 def store_slabs(count, slabs, outs):
-    for odd, pair, refs in zip(odd_places(count), slabs, outs):
-        low, high = pair
-        refs[0][...] = jnp.where(odd, low, high)
-        refs[1][...] = jnp.where(odd, high, low)
-
-
-def start_kernel(count, order, cells, est, u_out, cells_out, first_out, z0, z1, y0, y1, x1, pad):
-    zero = jnp.zeros((2, CELLROWS * 128), F32)
-    pad[...] = zero
+    odds = odd_places(count)
+    for (axis, far), out in zip(slab_kinds(count), outs):
+        low, high = slabs[axis]
+        out[...] = jnp.where(odds[axis], high, low) if far else jnp.where(odds[axis], low, high)
+
+
+def cells_kernel(order, cells, out, got, pad, sems):
+    copies = []
     for update in range(UPDATES):
-        pad[update : update + 1, 0:KS3] = cells[order[update]]
-    wide = pad[...].astype(BF16).astype(F32)
+        copies.append(pltpu.make_async_copy(cells.at[order[update]], got.at[update], sems.at[update]))
+        copies[-1].start()
+    pad[...] = jnp.zeros((1, CELLROWS * 128), F32)
     for update in range(UPDATES):
-        rows = [wide[update : update + 1, 128 * row : 128 * (row + 1)] for row in range(CELLROWS)]
-        block = jnp.concatenate(rows, axis=0).astype(BF16)
+        copies[update].wait()
+        pad[:, 0:KS3] = got[update]
+        wide = pad[...]
+        rows = [wide[:, 128 * row : 128 * (row + 1)] for row in range(CELLROWS)]
         here = slice(CELLROWS * update, CELLROWS * (update + 1))
-        cells_out[here, :] = block
-        first_out[here, :] = block
-    unflatten(lambda row: est[pl.ds(row, 8, stride=3), :], u_out)
-    store_slabs(count, pack_slabs(u_out), ((z0, z1), (y0, y1), (first_out.at[2 * CELLROWS :], x1)))
-
-
-def views_kernel(order, observed, o0, o1, wide):
+        out[here, :] = jnp.concatenate(rows, axis=0).astype(BF16)
+
+
+def start_kernel(count, est, u_out, *refs):
+    outs, (flat, sem) = refs[:-2], refs[-2:]
+    copy = pltpu.make_async_copy(est, flat, sem)
+    copy.start()
+    copy.wait()
+    unflatten(lambda row: flat[pl.ds(row, 8, stride=3), :], u_out)
+    store_slabs(count, pack_slabs(u_out), outs)
+
+
+VIEW_PARTS = 3
+
+
+def views_kernel(order, observed, o0, o1, near, wide, sems):
+    part_lanes = FLAT * 128 // VIEW_PARTS
+    copies = []
+    for part in range(VIEW_PARTS):
+        here = pl.ds(part_lanes * part, part_lanes)
+        copies.append(pltpu.make_async_copy(observed.at[:, :, here], near.at[:, :, here], sems.at[part]))
+        copies[-1].start()
     step_rows = 32
-
-    @pl.loop(0, FLAT // step_rows)
-    def _(step):
-        for row in range(step_rows):
-            at = step * step_rows + row
-            lanes = pl.ds(pl.multiple_of(at * 128, 128), 128)
-            wide[pl.ds(pl.multiple_of(at * 8, 8), VIEWS), :] = observed[0, :, lanes].astype(F32)
+    for part in range(VIEW_PARTS):
+        copies[part].wait()
+
+        @pl.loop(0, FLAT // VIEW_PARTS // step_rows)
+        def _(step):
+            for row in range(step_rows):
+                at = part * (FLAT // VIEW_PARTS) + step * step_rows + row
+                lanes = pl.ds(pl.multiple_of(at * 128, 128), 128)
+                wide[pl.ds(pl.multiple_of(at * 8, 8), VIEWS), :] = near[0, :, lanes].astype(F32)
 
     for update, out in enumerate((o0, o1)):
         view = order[update]
         unflatten(lambda row: wide[pl.ds(8 * row + view, 8, stride=24), :], out)
 
 
-def field_kernel(count, present, u, z0, z1, y0, y1, x0, x1, ea, gy, out, high, low, lines):
-    margins = ((z0[...], z1[...]), (y0[...], y1[...]), (x0[2 * CELLROWS :, :] if x0.shape[0] > 192 else x0[...], x1[...]))
+def field_stage(count, present, u, slabs, ea, gy, out, high, low, lines):
+    found = {kind: slab[...] for kind, slab in zip(slab_kinds(count), slabs)}
+    margins = []
+    for axis in range(3):
+        blank = jnp.zeros(SLABS[axis].shape, BF16)
+        margins.append((found.get((axis, 0), blank), found.get((axis, 1), blank)))
     assemble(present, odd_places(count), u, margins, high, low)
     lines_stage(high, low, ea, lines, SLOTS * PAD, 256)
     y_stage(lines, gy, PAD, out)
 
 
-def update_body(tissue, planes, kernel, u, o, tables, scratch, new_ref):
+def divide(value, by):
+    guess = pl.reciprocal(by, approx=True)
+    guess = guess * (2.0 - by * guess)
+    ratio = value * guess
+    return ratio + guess * (value - ratio * by)
+
+
+def wide_terms(value):
+    high, low = split(value)
+    return jnp.concatenate([high, low, high], axis=1)
+
+
+STEP = 192
+
+
+def update_body(tissue, kernel, u, o, tables, planes, lines, new_ref):
     ea, ei, gh, gb, twiddle = tables
-    planes2, lines = scratch
-    filter_stage(planes, kernel, twiddle, False, planes2)
-    y_back_stage(planes2, gb, lines)
-    rows = SLOTS * E
-    lane = lane_iota((rows, LANES))
+    filter_stage(planes, kernel, twiddle, False, planes)
+    y_back_stage(planes, gb, lines)
+    lane = lane_iota((STEP, LANES))
     valid = (lane % PAD < E) & (lane < 3 * PAD)
-    high, low = split(lines[...])
-    blurred = dot(jnp.concatenate([high, low, high], axis=1), ei[...])
-    quotient = jnp.where(valid, both_halves(o, slice(None)) / blurred, 0.0)
-    high, low = split(quotient)
-    lines[...] = dot(jnp.concatenate([high, low, high], axis=1), ea[...])
-    y_stage(lines, gh, E, planes2)
-    filter_stage(planes2, kernel, twiddle, True, planes2)
-    y_back_stage(planes2, gb, lines)
-    high, low = split(lines[...])
-    correction = dot(jnp.concatenate([high, low, high], axis=1), ei[...])
+    for start in range(0, SLOTS * E, STEP):
+        rows = slice(start, start + STEP)
+        blurred = dot(wide_terms(lines[rows, :]), ei[...])
+        quotient = jnp.where(valid, divide(both_halves(o, rows), blurred), 0.0)
+        lines[rows, :] = dot(wide_terms(quotient), ea[...])
+    y_stage(lines, gh, E, planes)
+    filter_stage(planes, kernel, twiddle, True, planes)
+    y_back_stage(planes, gb, lines)
     alive = tissue[0] > 0
-    for half in range(2):
-        core = u[half]
-        new_ref[half] = jnp.where(alive, core * correction[:, 128 * half : 128 * (half + 1)], core)
-
-
-def first_kernel(count, tissue, planes, kernel, u, o, ea, ei, gh, gb, twiddle, u_out, z0, z1, y0, y1, x0, x1, planes2, lines):
-    update_body(tissue, planes, kernel, u, o, (ea, ei, gh, gb, twiddle), (planes2, lines), u_out)
-    store_slabs(count, pack_slabs(u_out), ((z0, z1), (y0, y1), (x0, x1)))
-
-
-def last_kernel(tissue, planes, kernel, u, o, ea, ei, gh, gb, twiddle, out, planes2, lines, fresh):
-    update_body(tissue, planes, kernel, u, o, (ea, ei, gh, gb, twiddle), (planes2, lines), fresh)
+    for start in range(0, SLOTS * E, STEP):
+        rows = slice(start, start + STEP)
+        correction = dot(wide_terms(lines[rows, :]), ei[...])
+        for half in range(2):
+            core = u[half, rows, :]
+            new_ref[half, rows, :] = jnp.where(alive, core * correction[:, 128 * half : 128 * (half + 1)], core)
+
+
+def first_kernel(count, tissue, present, u, *refs):
+    kinds = len(slab_kinds(count))
+    slabs, (kernel, o, ea, gy, ei, gh, gb, twiddle, u_out), outs = refs[:kinds], refs[kinds : kinds + 9], refs[kinds + 9 : -4]
+    planes, high, low, lines = refs[-4:]
+    field_stage(count, present, u, slabs, ea, gy, planes, high, low, lines)
+    update_body(tissue, kernel, u, o, (ea, ei, gh, gb, twiddle), planes, lines, u_out)
+    store_slabs(count, pack_slabs(u_out), outs)
+
+
+def last_kernel(count, tissue, present, u, *refs):
+    kinds = len(slab_kinds(count))
+    slabs, (kernel, o, ea, gy, ei, gh, gb, twiddle, out) = refs[:kinds], refs[kinds : kinds + 9]
+    planes, high, low, lines, fresh = refs[-5:]
+    field_stage(count, present, u, slabs, ea, gy, planes, high, low, lines)
+    update_body(tissue, kernel, u, o, (ea, ei, gh, gb, twiddle), planes, lines, fresh)
     flatten(fresh, out)
 
 
 VM = pl.BlockSpec(memory_space=pltpu.VMEM)
 SM = pl.BlockSpec(memory_space=pltpu.SMEM)
 ANY = pl.BlockSpec(memory_space=pl.ANY)
+HBM = pl.BlockSpec(memory_space=pltpu.HBM)
 PARAMS = pltpu.CompilerParams(vmem_limit_bytes=48 * 1024 * 1024)
 
 
@@ -593,12 +638,14 @@
 
 SLAB = shape((192, 128), BF16)
 WIDE_SLAB = shape((256, 128), BF16)
+SLABS = [SLAB, WIDE_SLAB, SLAB]
 CELLS = shape((UPDATES * CELLROWS, 128), BF16)
 ROWS = shape((2, SLOTS * E, 128))
 ROWS_V = pltpu.VMEM((2, SLOTS * E, 128), F32)
 PLANES = shape((SLOTS, 128, 128))
 PLANES_V = pltpu.VMEM((SLOTS, 128, 128), F32)
-LINES_V = pltpu.VMEM((SLOTS * E, LANES), F32)
+LINES_V = pltpu.VMEM((SLOTS * PAD, LANES), F32)
+TERMS_V = pltpu.VMEM((SLOTS * PAD, LANES), BF16)
 
 
 def call(body, ins, outs, args, scratch=(), name=None):
@@ -633,14 +680,14 @@
     return lax.ppermute(value, "blk", [(number, number ^ distance) for number in range(count)])
 
 
-def near_swap(value, axis, count):
-    bits = grid_bits(count)[axis]
-    return swap(value, 1 << bits[0], count) if bits else jnp.zeros_like(value)
-
-
-def far_swap(value, axis, count):
-    pairs = far_pairs(count, axis)
-    return lax.ppermute(value, "blk", pairs) if pairs else jnp.zeros_like(value)
+def swap_slabs(slabs, count):
+    margins = []
+    for (axis, far), slab in zip(slab_kinds(count), slabs):
+        if far:
+            margins.append(lax.ppermute(slab, "blk", far_pairs(count, axis)))
+        else:
+            margins.append(swap(slab, 1 << grid_bits(count)[axis][0], count))
+    return margins
 
 
 def local(estimate, observed, psf_cells, tissue, neighbours, psf_list, psf_blend, cell_row, view_order):
@@ -657,98 +704,86 @@
     lists = jnp.swapaxes(psf_list, 1, 2)
     blend = jnp.swapaxes(psf_blend, 1, 2)
 
-    rows, cells, first, z0, z1, y0, y1, x1 = call(
+    cells = call(
+        cells_kernel,
+        [SM, HBM],
+        CELLS,
+        (view_order, jnp.swapaxes(psf_cells, 0, 1)),
+        [
+            pltpu.VMEM((UPDATES, 1, KS3), F32),
+            pltpu.VMEM((1, CELLROWS * 128), F32),
+            pltpu.SemaphoreType.DMA((UPDATES,)),
+        ],
+        name="cells",
+    )
+    slab_shapes = [SLABS[axis] for axis, far in slab_kinds(count)]
+    rows, *slabs = call(
         functools.partial(start_kernel, count),
-        [SM, VM, VM],
-        [ROWS, CELLS, shape((UPDATES * CELLROWS + 192, 128), BF16), SLAB, SLAB, WIDE_SLAB, WIDE_SLAB, SLAB],
-        (view_order, jnp.swapaxes(psf_cells, 0, 1), estimate.reshape(FLAT, 128)),
-        [pltpu.VMEM((UPDATES, CELLROWS * 128), F32)],
+        [HBM],
+        [ROWS] + slab_shapes,
+        (estimate.reshape(FLAT, 128),),
+        [pltpu.VMEM((FLAT, 128), F32), pltpu.SemaphoreType.DMA],
         name="start",
     )
     targets = call(
-        views_kernel, [SM, VM], [ROWS, ROWS], (view_order, observed), [pltpu.VMEM((8 * FLAT, 128), F32)], name="views"
+        views_kernel,
+        [SM, HBM],
+        [ROWS, ROWS],
+        (view_order, observed),
+        [
+            pltpu.VMEM((1, VIEWS, FLAT * 128), BF16),
+            pltpu.VMEM((8 * FLAT, 128), F32),
+            pltpu.SemaphoreType.DMA((VIEW_PARTS,)),
+        ],
+        name="views",
     )
-    pair_bits = [bits[0] if bits else None for bits in grid_bits(count)]
-    near_x, near_y = None, None
     held = cells
-    rounds = gather_rounds(count)
-    for bits in rounds[:-1]:
+    for number, bits in enumerate(gather_rounds(count)[:-1]):
         arrived = [held]
-        size = held.shape[0]
         for part in range(1, 2 ** len(bits)):
             distance = sum(((part >> level) & 1) << bit for level, bit in enumerate(bits))
-            sent = held
-            if distance == 1 << pair_bits[2] and held is cells:
-                near_x = swap(first, distance, count)
-                arrived.append(near_x[:size])
-            elif pair_bits[1] is not None and distance == 1 << pair_bits[1]:
-                both = swap(jnp.concatenate([held, y0], axis=0), distance, count)
-                near_y = both[size:]
-                arrived.append(both[:size])
-            else:
-                arrived.append(swap(held, distance, count))
+            arrived.append(swap(held, distance, count))
+        if number == 0:
+            arrived, rows, slabs = lax.optimization_barrier((arrived, rows, slabs))
+        if number == 1:
+            arrived, targets, slabs = lax.optimization_barrier((arrived, targets, slabs))
         held = jnp.concatenate(arrived, axis=0)
-    if near_x is None:
-        near_x = near_swap(first, 2, count)
-    if near_y is None:
-        near_y = near_swap(y0, 1, count)
-    far_z, far_y, far_x = far_swap(z1, 0, count), far_swap(y1, 1, count), far_swap(x1, 2, count)
-    near_z = near_swap(z0, 0, count)
+    margins = swap_slabs(slabs, count)
     other = swap(held, 1, count)
     near_cells, far_cells = [v.reshape(count // 2, UPDATES * CELLROWS, 128) for v in (held, other)]
 
     def spectrum(update):
         return call(
             functools.partial(spectrum_kernel, update, count),
-            [SM] * 4 + [ANY] * 2 + [VM] * 3,
+            [SM] * 4 + [VM] * 5,
             PLANES,
             (view_order, lists, blend, cell_row, near_cells, far_cells, taps, turns, gt),
             [
-                pltpu.VMEM((2, UPDATES * CELLROWS, 128), BF16),
                 pltpu.VMEM((CELLROWS, 128), F32),
                 pltpu.VMEM((3, TAPS, 128), F32),
                 pltpu.VMEM((TAPS * TAPS, 128), F32),
                 PLANES_V,
-                pltpu.SemaphoreType.DMA((2,)),
             ],
             name="spectrum",
         )
 
-    def field(rows, margins):
+    def update(body, outs, number, kernel, rows, margins, scratch, name):
         return call(
-            functools.partial(field_kernel, count),
-            [SM] + [VM] * 9,
-            PLANES,
-            (neighbours, rows, *margins, ea, gy),
-            [pltpu.VMEM((SLOTS * PAD, LANES), BF16)] * 2 + [pltpu.VMEM((SLOTS * PAD, LANES), F32)],
-            name="field",
+            functools.partial(body, count),
+            [SM] * 2 + [VM] * (9 + len(slab_shapes)),
+            outs,
+            (tissue, neighbours, rows, *margins, kernel, targets[number], ea, gy, ei, gh, gb, twiddle),
+            [PLANES_V, TERMS_V, TERMS_V, LINES_V] + scratch,
+            name=name,
         )
 
-    planes = field(rows, (near_z, far_z, near_y, far_y, near_x, far_x))
     kernel = spectrum(0)
-    first = call(
-        functools.partial(first_kernel, count),
-        [SM] + [VM] * 9,
-        [ROWS, SLAB, SLAB, WIDE_SLAB, WIDE_SLAB, SLAB, SLAB],
-        (tissue, planes, kernel, rows, targets[0], ea, ei, gh, gb, twiddle),
-        [PLANES_V, LINES_V],
-        name="first",
-    )
-    rows, slabs = first[0], first[1:]
-    margins = []
-    for axis in range(3):
-        margins.append(near_swap(slabs[2 * axis], axis, count))
-        margins.append(far_swap(slabs[2 * axis + 1], axis, count))
+    kernel, margins = lax.optimization_barrier((kernel, margins))
+    rows, *slabs = update(first_kernel, [ROWS] + slab_shapes, 0, kernel, rows, margins, [], "first")
+    margins = swap_slabs(slabs, count)
     kernel = spectrum(1)
-    planes = field(rows, margins)
-    out = call(
-        last_kernel,
-        [SM] + [VM] * 9,
-        shape((FLAT, 128)),
-        (tissue, planes, kernel, rows, targets[1], ea, ei, gh, gb, twiddle),
-        [PLANES_V, LINES_V, ROWS_V],
-        name="last",
-    )
+    kernel, margins = lax.optimization_barrier((kernel, margins))
+    out = update(last_kernel, shape((FLAT, 128)), 1, kernel, rows, margins, [ROWS_V], "last")
     return out.reshape(1, FLAT * 128)
 
 

time: 61 us -> 54.8 us (0.90)
  the two profiles are of different devices: /device:TPU:12 before, /device:TPU:6 now
where the time goes in v3:
time: 54.8 us; the launch traced here: 54.5 us
  Pallas kernels  21 us (38%)
  starting transfers between devices  20.7 us (38%)
  waiting for transfers between devices  7 us (13%)
  local copies, waits for them, and re-layouts  4.88 us (9%)
  between operations  0.99 us (2%)
    pallas_call x7, Pallas kernels, call(): pl.pallas_call(body, in_specs=ins, out_specs=[VM] * len(outs) if many els...  21 us
    ppermute x13, starting transfers between devices, swap(): lax.ppermute(value, 'blk', [(number, number ^ distance) for number in ran...  11.6 us
    ppermute x4, starting transfers between devices, swap_slabs(): margins.append(lax.ppermute(slab, 'blk', far_pairs(count, axis)))  9.06 us
    unnamed x42, local copies, waits for them, and re-layouts  4.85 us
    ppermute x4, waiting for transfers between devices, swap_slabs(): margins.append(lax.ppermute(slab, 'blk', far_pairs(count, axis)))  3.69 us
    ppermute x13, waiting for transfers between devices, swap(): lax.ppermute(value, 'blk', [(number, number ^ distance) for number in ran...  3.31 us
  transfers between devices with their start and end apart: 17, of which 4 were waited for; matrix products, arithmetic and copies ran while one was open for 0% of the time, Pallas kernels for 14%

profile of v3, /device:TPU:6, one launch (start us, length us, event | category | flops | bytes accessed | tf_op | source)
XLA Modules:
  0.0 54.5 jit_solution(7612375053151217048)
XLA Ops:
  0.0 0.9 %copy-done.11 = f32[1,6,4913]{2,0,1:T(1,128)S(1)} copy-done((f32[1,6,4913]{2,0,1:T(1,128)S(1)}, f32[1,6,4913]{2,0,1:T(1,128)}, u32[]{:S(2)}) %copy-start.11) | copy-done | bytes 117936
  0.9 0.7 %copy-done.12 = s32[6]{0:T(128)S(1)} copy-done((s32[6]{0:T(128)S(1)}, s32[6]{0:T(128)}, u32[]{:S(2)}) %copy-start.12) | copy-done | bytes 48
  1.6 0.6 %cells.1 = bf16[80,128]{1,0:T(8,128)(2,1)S(1)} custom-call(s32[6]{0:T(128)S(1)} %copy-done.12, f32[6,1,4913]{2,1,0:T(1,128)S(1)} %bitcast.12), custom_call_target="tpu_custom_call" | custom-call | tf_op jit(solution)/shard_map/cells/pallas_call | solution.py:653
  2.2 1.6 %collective-permute-start = (bf16[80,128]{1,0:T(8,128)(2,1)S(1)}, bf16[80,128]{1,0:T(8,128)(2,1)S(1)}, u32[]{:S(2)}, u32[]{:S(2)}) collective-permute-start(bf16[80,128]{1,0:T(8,128)(2,1)S(1)} %cells.1), channel_id=1, source_target_pairs={{0,8},{1,9},{2,10},{3,11},{4,12},{5,13},{6,14},{7,15},{8,0},{9,1},... | collective-permute-start | bytes 61448 | tf_op jit(solution)/shard_map/ppermute | solution.py:680
  3.9 2.6 %collective-permute-start.1 = (bf16[80,128]{1,0:T(8,128)(2,1)S(1)}, bf16[80,128]{1,0:T(8,128)(2,1)S(1)}, u32[]{:S(2)}, u32[]{:S(2)}) collective-permute-start(bf16[80,128]{1,0:T(8,128)(2,1)S(1)} %cells.1), channel_id=1, source_target_pairs={{0,16},{1,17},{2,18},{3,19},{4,20},{5,21},{6,22},{7,23},{8,24},{9,... | collective-permute-start | bytes 61448 | tf_op jit(solution)/shard_map/ppermute | solution.py:680
  6.5 0.2 collective-permute-start.2
  6.7 1.0 %copy-done.5 = f32[1,110592]{1,0:T(1,128)S(1)} copy-done((f32[1,110592]{1,0:T(1,128)S(1)}, f32[1,110592]{1,0:T(1,128)}, u32[]{:S(2)}) %copy-start.5) | copy-done | bytes 442392
  7.7 1.0 %start.1 = (f32[2,768,128]{2,1,0:T(8,128)S(1)}, bf16[192,128]{1,0:T(8,128)(2,1)S(1)}, bf16[256,128]{1,0:T(8,128)(2,1)S(1)}, bf16[192,128]{1,0:T(8,128)(2,1)S(1)}...) custom-call(f32[864,128]{1,0:T(8,128)S(1)} %bitcast.11), custom_call_target="tpu_custom_call" | custom-call | tf_op jit(solution)/shard_map/start/pallas_call | solution.py:653
  8.8 0.1 collective-permute-done.1
  8.9 3.2 %collective-permute-done.2 = bf16[80,128]{1,0:T(8,128)(2,1)S(1)} collective-permute-done((bf16[80,128]{1,0:T(8,128)(2,1)S(1)}, bf16[80,128]{1,0:T(8,128)(2,1)S(1)}, u32[]{:S(2)}, u32[]{:S(2)}) %collective-permute-start.2) | collective-permute-done | bytes 20512 | tf_op jit(solution)/shard_map/ppermute | solution.py:680
  12.1 0.6 %collective-permute-start.3 = (bf16[320,128]{1,0:T(8,128)(2,1)S(1)}, bf16[320,128]{1,0:T(8,128)(2,1)S(1)}, u32[]{:S(2)}, u32[]{:S(2)}) collective-permute-start(bf16[320,128]{1,0:T(8,128)(2,1)S(1)} %constant_dynamic-update-slice_fusion), channel_id=1, source_target_pairs={{0,2},{1,3},{2,0},{3,1},{4,6},{5,7},{6,4},{7,5},{8,10},{9,11},{10,... | collective-permute-start | bytes 245768 | tf_op jit(solution)/shard_map/ppermute | solution.py:680
  12.7 0.5 collective-permute-start.4
  13.2 2.4 %collective-permute-start.5 = (bf16[320,128]{1,0:T(8,128)(2,1)S(1)}, bf16[320,128]{1,0:T(8,128)(2,1)S(1)}, u32[]{:S(2)}, u32[]{:S(2)}) collective-permute-start(bf16[320,128]{1,0:T(8,128)(2,1)S(1)} %constant_dynamic-update-slice_fusion), channel_id=1, source_target_pairs={{0,6},{1,7},{2,4},{3,5},{4,2},{5,3},{6,0},{7,1},{8,14},{9,15},{10,... | collective-permute-start | bytes 245768 | tf_op jit(solution)/shard_map/ppermute | solution.py:680
  15.7 1.5 %copy-done = bf16[1,6,110592]{2,1,0:T(8,128)(2,1)S(1)} copy-done((bf16[1,6,110592]{2,1,0:T(8,128)(2,1)S(1)}, bf16[1,6,110592]{2,1,0:T(8,128)(2,1)}, u32[]{:S(2)}) %copy-start) | copy-done | bytes 1327128
  17.2 0.7 %copy-done.13 = s32[6]{0:T(128)S(1)} copy-done((s32[6]{0:T(128)S(1)}, s32[6]{0:T(128)}, u32[]{:S(2)}) %copy-start.13) | copy-done | bytes 48
  17.8 0.0 copy-start.7
  17.8 2.7 %views.1 = (f32[2,768,128]{2,1,0:T(8,128)S(1)}, f32[2,768,128]{2,1,0:T(8,128)S(1)}) custom-call(s32[6]{0:T(128)S(1)} %copy-done.13, bf16[1,6,110592]{2,1,0:T(8,128)(2,1)S(1)} %copy-done), custom_call_target="tpu_custom_call" | custom-call | tf_op jit(solution)/shard_map/views/pallas_call | solution.py:653
  20.7 0.1 collective-permute-start.6
  20.8 0.6 %collective-permute-start.8 = (bf16[256,128]{1,0:T(8,128)(2,1)S(1)}, bf16[256,128]{1,0:T(8,128)(2,1)S(1)}, u32[]{:S(2)}, u32[]{:S(2)}) collective-permute-start(bf16[256,128]{1,0:T(8,128)(2,1)S(1)} %get-tuple-element.75), channel_id=1, source_target_pairs={{0,2},{1,3},{2,0},{3,1},{4,6},{5,7},{6,4},{7,5},{8,10},{9,11},{10,... | collective-permute-start | bytes 196616 | tf_op jit(solution)/shard_map/ppermute | solution.py:680
  21.4 0.2 collective-permute-start.9
  21.5 4.6 %collective-permute-start.10 = (bf16[192,128]{1,0:T(8,128)(2,1)S(1)}, bf16[192,128]{1,0:T(8,128)(2,1)S(1)}, u32[]{:S(2)}, u32[]{:S(2)}) collective-permute-start(bf16[192,128]{1,0:T(8,128)(2,1)S(1)} %get-tuple-element.77), channel_id=1, source_target_pairs={{4,16},{5,17},{6,18},{7,19},{12,24},{13,25},{14,26},{15,27},{16,4}... | collective-permute-start | bytes 147464 | tf_op jit(solution)/shard_map/ppermute | solution.py:687
  26.2 0.7 %collective-permute-start.11 = (bf16[192,128]{1,0:T(8,128)(2,1)S(1)}, bf16[192,128]{1,0:T(8,128)(2,1)S(1)}, u32[]{:S(2)}, u32[]{:S(2)}) collective-permute-start(bf16[192,128]{1,0:T(8,128)(2,1)S(1)} %get-tuple-element.78), channel_id=1, source_target_pairs={{1,8},{3,10},{5,12},{7,14},{8,1},{10,3},{12,5},{14,7},{17,24},{19,... | collective-permute-start | bytes 147464 | tf_op jit(solution)/shard_map/ppermute | solution.py:687
  27.5 2.0 %spectrum.2.refs_5_ = f32[16,128,128]{2,1,0:T(8,128)S(1)} custom-call(s32[6]{0:T(128)S(1)} %copy-done.13, s32[1,2,6]{2,1,0:T(2,128)S(1)} %bitcast.13, f32[1,2,6]{2,1,0:T(2,128)S(1)} %bitcast.15, s32[32]{0:T(128)S(1)} %copy-done.17, bf16[16,80,128]{2,1,0:T(8,128)(2,1)S(1)} %bitcast.7, bf16[16,80,128]{2,1,0:T(8,128)(2,1)S(1)} %bitcast.9, ...), custom_call_target="tpu_custom_call" | custom-call | tf_op jit(solution)/shard_map/spectrum/pallas_call | solution.py:653
  29.6 0.7 %collective-permute-done.10.refs_3_ = bf16[192,128]{1,0:T(8,128)(2,1)S(1)} collective-permute-done((bf16[192,128]{1,0:T(8,128)(2,1)S(1)}, bf16[192,128]{1,0:T(8,128)(2,1)S(1)}, u32[]{:S(2)}, u32[]{:S(2)}) %collective-permute-start.10) | collective-permute-done | bytes 49184 | tf_op jit(solution)/shard_map/ppermute | solution.py:687
  30.3 5.9 %first.1 = (f32[2,768,128]{2,1,0:T(8,128)S(1)}, bf16[192,128]{1,0:T(8,128)(2,1)S(1)}, bf16[256,128]{1,0:T(8,128)(2,1)S(1)}, bf16[192,128]{1,0:T(8,128)(2,1)S(1)}...) custom-call(s32[1]{0:T(128)S(6)} %copy.25.tissue, s32[1,6]{1,0:T(1,128)S(1)} %copy-done.16, ...), custom_call_target="tpu_custom_call" | custom-call | tf_op jit(solution)/shard_map/first/pallas_call | solution.py:653
  36.3 1.6 %collective-permute-start.13 = (bf16[256,128]{1,0:T(8,128)(2,1)S(1)}, bf16[256,128]{1,0:T(8,128)(2,1)S(1)}, u32[]{:S(2)}, u32[]{:S(2)}) collective-permute-start(bf16[256,128]{1,0:T(8,128)(2,1)S(1)} %get-tuple-element.88), channel_id=1, source_target_pairs={{0,2},{1,3},{2,0},{3,1},{4,6},{5,7},{6,4},{7,5},{8,10},{9,11},{10,... | collective-permute-start | bytes 196616 | tf_op jit(solution)/shard_map/ppermute | solution.py:680
  37.8 1.2 %collective-permute-start.14 = (bf16[192,128]{1,0:T(8,128)(2,1)S(1)}, bf16[192,128]{1,0:T(8,128)(2,1)S(1)}, u32[]{:S(2)}, u32[]{:S(2)}) collective-permute-start(bf16[192,128]{1,0:T(8,128)(2,1)S(1)} %get-tuple-element.89), channel_id=1, source_target_pairs={{0,1},{1,0},{2,3},{3,2},{4,5},{5,4},{6,7},{7,6},{8,9},{9,8},{10,11... | collective-permute-start | bytes 147464 | tf_op jit(solution)/shard_map/ppermute | solution.py:680
  39.1 2.9 %collective-permute-start.15 = (bf16[192,128]{1,0:T(8,128)(2,1)S(1)}, bf16[192,128]{1,0:T(8,128)(2,1)S(1)}, u32[]{:S(2)}, u32[]{:S(2)}) collective-permute-start(bf16[192,128]{1,0:T(8,128)(2,1)S(1)} %get-tuple-element.90), channel_id=1, source_target_pairs={{4,16},{5,17},{6,18},{7,19},{12,24},{13,25},{14,26},{15,27},{16,4}... | collective-permute-start | bytes 147464 | tf_op jit(solution)/shard_map/ppermute | solution.py:687
  42.0 0.8 %collective-permute-start.16 = (bf16[192,128]{1,0:T(8,128)(2,1)S(1)}, bf16[192,128]{1,0:T(8,128)(2,1)S(1)}, u32[]{:S(2)}, u32[]{:S(2)}) collective-permute-start(bf16[192,128]{1,0:T(8,128)(2,1)S(1)} %get-tuple-element.91), channel_id=1, source_target_pairs={{1,8},{3,10},{5,12},{7,14},{8,1},{10,3},{12,5},{14,7},{17,24},{19,... | collective-permute-start | bytes 147464 | tf_op jit(solution)/shard_map/ppermute | solution.py:687
  42.9 2.0 %spectrum.3.refs_5_ = f32[16,128,128]{2,1,0:T(8,128)S(1)} custom-call(s32[6]{0:T(128)S(1)} %copy-done.13, s32[1,2,6]{2,1,0:T(2,128)S(1)} %bitcast.14, f32[1,2,6]{2,1,0:T(2,128)S(1)} %bitcast.16, s32[32]{0:T(128)S(1)} %copy-done.17, bf16[16,80,128]{2,1,0:T(8,128)(2,1)S(1)} %bitcast.8, bf16[16,80,128]{2,1,0:T(8,128)(2,1)S(1)} %bitcast.10, ...), custom_call_target="tpu_custom_call" | custom-call | tf_op jit(solution)/shard_map/spectrum/pallas_call | solution.py:653
  44.9 3.0 %collective-permute-done.15.refs_3_ = bf16[192,128]{1,0:T(8,128)(2,1)S(1)} collective-permute-done((bf16[192,128]{1,0:T(8,128)(2,1)S(1)}, bf16[192,128]{1,0:T(8,128)(2,1)S(1)}, u32[]{:S(2)}, u32[]{:S(2)}) %collective-permute-start.15) | collective-permute-done | bytes 49184 | tf_op jit(solution)/shard_map/ppermute | solution.py:687
  47.9 6.6 %last.1 = f32[864,128]{1,0:T(8,128)} custom-call(s32[1]{0:T(128)S(6)} %copy.25.tissue, s32[1,6]{1,0:T(1,128)S(1)} %copy-done.16, f32[2,768,128]{2,1,0:T(8,128)S(1)} %get-tuple-element.86.u, bf16[192,128]{1,0:T(8,128)(2,1)S(1)} %collective-permute-done.12.refs_0_, bf16[256,128]{1,0:T(8,128)(2,1)S(1)} %collective-permute-done.13.refs_1_, ...), custom_call_target="tpu_custom_call" | custom-call | tf_op jit(solution)/shard_map/last/pallas_call | solution.py:653
  (53 shorter events, 0.2 us)
Async XLA Ops:
  0.0 27.5 %copy-start.3 = (f32[2,17,8,128]{3,2,1,0:T(8,128)S(1)}, f32[2,17,8,128]{3,2,1,0:T(8,128)}, u32[]{:S(2)}) copy-start(f32[2,17,8,128]{3,2,1,0:T(8,128)} %constant.25.clone.turns) | copy-start | bytes 417796
  1.6 25.9 %copy-start.14 = (s32[1,6,2]{1,2,0:T(2,128)S(1)}, s32[1,6,2]{1,2,0:T(2,128)}, u32[]{:S(2)}) copy-start(s32[1,6,2]{1,2,0:T(2,128)} %param.23) | copy-start | bytes 148
  1.6 25.9 %copy-start.15 = (f32[1,6,2]{1,2,0:T(2,128)S(1)}, f32[1,6,2]{1,2,0:T(2,128)}, u32[]{:S(2)}) copy-start(f32[1,6,2]{1,2,0:T(2,128)} %param.24) | copy-start | bytes 148
  1.6 25.9 %copy-start.17 = (s32[32]{0:T(128)S(1)}, s32[32]{0:T(128)}, u32[]{:S(2)}) copy-start(s32[32]{0:T(128)} %cell_row.3) | copy-start | bytes 388
  2.2 6.5 %collective-permute-start = (bf16[80,128]{1,0:T(8,128)(2,1)S(1)}, bf16[80,128]{1,0:T(8,128)(2,1)S(1)}, u32[]{:S(2)}, u32[]{:S(2)}) collective-permute-start(bf16[80,128]{1,0:T(8,128)(2,1)S(1)} %cells.1), channel_id=1, source_target_pairs={{0,8},{1,9},{2,10},{3,11},{4,12},{5,13},{6,14},{7,15},{8,0},{9,1},... | collective-permute-start | bytes 61448 | tf_op jit(solution)/shard_map/ppermute | solution.py:680
  3.9 5.0 %collective-permute-start.1 = (bf16[80,128]{1,0:T(8,128)(2,1)S(1)}, bf16[80,128]{1,0:T(8,128)(2,1)S(1)}, u32[]{:S(2)}, u32[]{:S(2)}) collective-permute-start(bf16[80,128]{1,0:T(8,128)(2,1)S(1)} %cells.1), channel_id=1, source_target_pairs={{0,16},{1,17},{2,18},{3,19},{4,20},{5,21},{6,22},{7,23},{8,24},{9,... | collective-permute-start | bytes 61448 | tf_op jit(solution)/shard_map/ppermute | solution.py:680
  6.5 5.6 %collective-permute-start.2 = (bf16[80,128]{1,0:T(8,128)(2,1)S(1)}, bf16[80,128]{1,0:T(8,128)(2,1)S(1)}, u32[]{:S(2)}, u32[]{:S(2)}) collective-permute-start(bf16[80,128]{1,0:T(8,128)(2,1)S(1)} %cells.1), channel_id=1, source_target_pairs={{0,24},{1,25},{2,26},{3,27},{4,28},{5,29},{6,30},{7,31},{8,16},{9,... | collective-permute-start | bytes 61448 | tf_op jit(solution)/shard_map/ppermute | solution.py:680
  6.7 1.0 %copy-start.5 = (f32[1,110592]{1,0:T(1,128)S(1)}, f32[1,110592]{1,0:T(1,128)}, u32[]{:S(2)}) copy-start(f32[1,110592]{1,0:T(1,128)} %param.18) | copy-start | bytes 1327108
  7.7 19.8 %copy-start.9 = (bf16[128,256]{1,0:T(8,128)(2,1)S(1)}, bf16[128,256]{1,0:T(8,128)(2,1)}, u32[]{:S(2)}) copy-start(bf16[128,256]{1,0:T(8,128)(2,1)} %constant.24.clone.table) | copy-start | bytes 196612
  7.7 19.8 %copy-start.10 = (bf16[128,144]{1,0:T(8,128)(2,1)S(1)}, bf16[128,144]{1,0:T(8,128)(2,1)}, u32[]{:S(2)}) copy-start(bf16[128,144]{1,0:T(8,128)(2,1)} %constant.23.clone.table_y_ref) | copy-start | bytes 110596
  12.1 18.2 %copy-start.8 = (bf16[96,384]{1,0:T(8,128)(2,1)S(1)}, bf16[96,384]{1,0:T(8,128)(2,1)}, u32[]{:S(2)}) copy-start(bf16[96,384]{1,0:T(8,128)(2,1)} %constant.22.clone.refs_11_) | copy-start | bytes 221188
  12.1 18.2 %copy-start.16 = (s32[1,6]{1,0:T(1,128)S(1)}, s32[1,6]{1,0:T(1,128)}, u32[]{:S(2)}) copy-start(s32[1,6]{1,0:T(1,128)} %present.3) | copy-start | bytes 76
  12.1 8.5 %collective-permute-start.3 = (bf16[320,128]{1,0:T(8,128)(2,1)S(1)}, bf16[320,128]{1,0:T(8,128)(2,1)S(1)}, u32[]{:S(2)}, u32[]{:S(2)}) collective-permute-start(bf16[320,128]{1,0:T(8,128)(2,1)S(1)} %constant_dynamic-update-slice_fusion), channel_id=1, source_target_pairs={{0,2},{1,3},{2,0},{3,1},{4,6},{5,7},{6,4},{7,5},{8,10},{9,11},{10,... | collective-permute-start | bytes 245768 | tf_op jit(solution)/shard_map/ppermute | solution.py:680
  12.7 7.9 %collective-permute-start.4 = (bf16[320,128]{1,0:T(8,128)(2,1)S(1)}, bf16[320,128]{1,0:T(8,128)(2,1)S(1)}, u32[]{:S(2)}, u32[]{:S(2)}) collective-permute-start(bf16[320,128]{1,0:T(8,128)(2,1)S(1)} %constant_dynamic-update-slice_fusion), channel_id=1, source_target_pairs={{0,4},{1,5},{2,6},{3,7},{4,0},{5,1},{6,2},{7,3},{8,12},{9,13},{10,... | collective-permute-start | bytes 245768 | tf_op jit(solution)/shard_map/ppermute | solution.py:680
  13.2 7.4 %collective-permute-start.5 = (bf16[320,128]{1,0:T(8,128)(2,1)S(1)}, bf16[320,128]{1,0:T(8,128)(2,1)S(1)}, u32[]{:S(2)}, u32[]{:S(2)}) collective-permute-start(bf16[320,128]{1,0:T(8,128)(2,1)S(1)} %constant_dynamic-update-slice_fusion), channel_id=1, source_target_pairs={{0,6},{1,7},{2,4},{3,5},{4,2},{5,3},{6,0},{7,1},{8,14},{9,15},{10,... | collective-permute-start | bytes 245768 | tf_op jit(solution)/shard_map/ppermute | solution.py:680
  15.7 1.5 %copy-start = (bf16[1,6,110592]{2,1,0:T(8,128)(2,1)S(1)}, bf16[1,6,110592]{2,1,0:T(8,128)(2,1)}, u32[]{:S(2)}) copy-start(bf16[1,6,110592]{2,1,0:T(8,128)(2,1)} %observed.1) | copy-start | bytes 3981316
  17.8 12.5 %copy-start.1 = (bf16[768,256]{1,0:T(8,128)(2,1)S(1)}, bf16[768,256]{1,0:T(8,128)(2,1)}, u32[]{:S(2)}) copy-start(bf16[768,256]{1,0:T(8,128)(2,1)} %constant.18.clone.refs_7_) | copy-start | bytes 1179652
  17.8 12.5 %copy-start.2 = (bf16[768,256]{1,0:T(8,128)(2,1)S(1)}, bf16[768,256]{1,0:T(8,128)(2,1)}, u32[]{:S(2)}) copy-start(bf16[768,256]{1,0:T(8,128)(2,1)} %constant.19.clone.refs_9_) | copy-start | bytes 1179652
  17.8 12.5 %copy-start.4 = (f32[2,16,8,128]{3,2,1,0:T(8,128)S(1)}, f32[2,16,8,128]{3,2,1,0:T(8,128)}, u32[]{:S(2)}) copy-start(f32[2,16,8,128]{3,2,1,0:T(8,128)} %constant.26.clone.refs_12_) | copy-start | bytes 393220
  17.8 12.5 %copy-start.6 = (bf16[128,384]{1,0:T(8,128)(2,1)S(1)}, bf16[128,384]{1,0:T(8,128)(2,1)}, u32[]{:S(2)}) copy-start(bf16[128,384]{1,0:T(8,128)(2,1)} %constant.20.clone.refs_8_) | copy-start | bytes 294916
  17.8 12.5 %copy-start.7 = (bf16[128,288]{1,0:T(8,128)(2,1)S(1)}, bf16[128,288]{1,0:T(8,128)(2,1)}, u32[]{:S(2)}) copy-start(bf16[128,288]{1,0:T(8,128)(2,1)} %constant.21.clone.refs_10_) | copy-start | bytes 221188
  20.7 5.5 %collective-permute-start.6 = (bf16[1280,128]{1,0:T(8,128)(2,1)S(1)}, bf16[1280,128]{1,0:T(8,128)(2,1)S(1)}, u32[]{:S(2)}, u32[]{:S(2)}) collective-permute-start(bf16[1280,128]{1,0:T(8,128)(2,1)S(1)} %constant_dynamic-update-slice_fusion.4), channel_id=1, source_target_pairs={{0,1},{1,0},{2,3},{3,2},{4,5},{5,4},{6,7},{7,6},{8,9},{9,8},{10,11... | collective-permute-start | bytes 983048 | tf_op jit(solution)/shard_map/ppermute | solution.py:680
  20.8 9.5 %collective-permute-start.8 = (bf16[256,128]{1,0:T(8,128)(2,1)S(1)}, bf16[256,128]{1,0:T(8,128)(2,1)S(1)}, u32[]{:S(2)}, u32[]{:S(2)}) collective-permute-start(bf16[256,128]{1,0:T(8,128)(2,1)S(1)} %get-tuple-element.75), channel_id=1, source_target_pairs={{0,2},{1,3},{2,0},{3,1},{4,6},{5,7},{6,4},{7,5},{8,10},{9,11},{10,... | collective-permute-start | bytes 196616 | tf_op jit(solution)/shard_map/ppermute | solution.py:680
  21.4 8.2 %collective-permute-start.7 = (bf16[192,128]{1,0:T(8,128)(2,1)S(1)}, bf16[192,128]{1,0:T(8,128)(2,1)S(1)}, u32[]{:S(2)}, u32[]{:S(2)}) collective-permute-start(bf16[192,128]{1,0:T(8,128)(2,1)S(1)} %get-tuple-element.74), channel_id=1, source_target_pairs={{0,16},{1,17},{2,18},{3,19},{4,20},{5,21},{6,22},{7,23},{8,24},{9,... | collective-permute-start | bytes 147464 | tf_op jit(solution)/shard_map/ppermute | solution.py:680
  21.4 8.2 %collective-permute-start.9 = (bf16[192,128]{1,0:T(8,128)(2,1)S(1)}, bf16[192,128]{1,0:T(8,128)(2,1)S(1)}, u32[]{:S(2)}, u32[]{:S(2)}) collective-permute-start(bf16[192,128]{1,0:T(8,128)(2,1)S(1)} %get-tuple-element.76), channel_id=1, source_target_pairs={{0,1},{1,0},{2,3},{3,2},{4,5},{5,4},{6,7},{7,6},{8,9},{9,8},{10,11... | collective-permute-start | bytes 147464 | tf_op jit(solution)/shard_map/ppermute | solution.py:680
  21.5 8.7 %collective-permute-start.10 = (bf16[192,128]{1,0:T(8,128)(2,1)S(1)}, bf16[192,128]{1,0:T(8,128)(2,1)S(1)}, u32[]{:S(2)}, u32[]{:S(2)}) collective-permute-start(bf16[192,128]{1,0:T(8,128)(2,1)S(1)} %get-tuple-element.77), channel_id=1, source_target_pairs={{4,16},{5,17},{6,18},{7,19},{12,24},{13,25},{14,26},{15,27},{16,4}... | collective-permute-start | bytes 147464 | tf_op jit(solution)/shard_map/ppermute | solution.py:687
  26.2 4.1 %collective-permute-start.11 = (bf16[192,128]{1,0:T(8,128)(2,1)S(1)}, bf16[192,128]{1,0:T(8,128)(2,1)S(1)}, u32[]{:S(2)}, u32[]{:S(2)}) collective-permute-start(bf16[192,128]{1,0:T(8,128)(2,1)S(1)} %get-tuple-element.78), channel_id=1, source_target_pairs={{1,8},{3,10},{5,12},{7,14},{8,1},{10,3},{12,5},{14,7},{17,24},{19,... | collective-permute-start | bytes 147464 | tf_op jit(solution)/shard_map/ppermute | solution.py:687
  36.3 11.6 %collective-permute-start.13 = (bf16[256,128]{1,0:T(8,128)(2,1)S(1)}, bf16[256,128]{1,0:T(8,128)(2,1)S(1)}, u32[]{:S(2)}, u32[]{:S(2)}) collective-permute-start(bf16[256,128]{1,0:T(8,128)(2,1)S(1)} %get-tuple-element.88), channel_id=1, source_target_pairs={{0,2},{1,3},{2,0},{3,1},{4,6},{5,7},{6,4},{7,5},{8,10},{9,11},{10,... | collective-permute-start | bytes 196616 | tf_op jit(solution)/shard_map/ppermute | solution.py:680
  37.8 7.1 %collective-permute-start.12 = (bf16[192,128]{1,0:T(8,128)(2,1)S(1)}, bf16[192,128]{1,0:T(8,128)(2,1)S(1)}, u32[]{:S(2)}, u32[]{:S(2)}) collective-permute-start(bf16[192,128]{1,0:T(8,128)(2,1)S(1)} %get-tuple-element.87), channel_id=1, source_target_pairs={{0,16},{1,17},{2,18},{3,19},{4,20},{5,21},{6,22},{7,23},{8,24},{9,... | collective-permute-start | bytes 147464 | tf_op jit(solution)/shard_map/ppermute | solution.py:680
  37.8 7.1 %collective-permute-start.14 = (bf16[192,128]{1,0:T(8,128)(2,1)S(1)}, bf16[192,128]{1,0:T(8,128)(2,1)S(1)}, u32[]{:S(2)}, u32[]{:S(2)}) collective-permute-start(bf16[192,128]{1,0:T(8,128)(2,1)S(1)} %get-tuple-element.89), channel_id=1, source_target_pairs={{0,1},{1,0},{2,3},{3,2},{4,5},{5,4},{6,7},{7,6},{8,9},{9,8},{10,11... | collective-permute-start | bytes 147464 | tf_op jit(solution)/shard_map/ppermute | solution.py:680
  39.1 8.8 %collective-permute-start.15 = (bf16[192,128]{1,0:T(8,128)(2,1)S(1)}, bf16[192,128]{1,0:T(8,128)(2,1)S(1)}, u32[]{:S(2)}, u32[]{:S(2)}) collective-permute-start(bf16[192,128]{1,0:T(8,128)(2,1)S(1)} %get-tuple-element.90), channel_id=1, source_target_pairs={{4,16},{5,17},{6,18},{7,19},{12,24},{13,25},{14,26},{15,27},{16,4}... | collective-permute-start | bytes 147464 | tf_op jit(solution)/shard_map/ppermute | solution.py:687
  42.0 5.9 %collective-permute-start.16 = (bf16[192,128]{1,0:T(8,128)(2,1)S(1)}, bf16[192,128]{1,0:T(8,128)(2,1)S(1)}, u32[]{:S(2)}, u32[]{:S(2)}) collective-permute-start(bf16[192,128]{1,0:T(8,128)(2,1)S(1)} %get-tuple-element.91), channel_id=1, source_target_pairs={{1,8},{3,10},{5,12},{7,14},{8,1},{10,3},{12,5},{14,7},{17,24},{19,... | collective-permute-start | bytes 147464 | tf_op jit(solution)/shard_map/ppermute | solution.py:687
  (3 other events, 2.2 us)

commit v4 on v3

--- a/solution.py
+++ b/solution.py
@@ -532,26 +532,29 @@
     store_slabs(count, pack_slabs(u_out), outs)
 
 
-VIEW_PARTS = 3
+VIEW_PARTS = 9
 
 
 def views_kernel(order, observed, o0, o1, near, wide, sems):
-    part_lanes = FLAT * 128 // VIEW_PARTS
+    part_rows = FLAT // VIEW_PARTS
     copies = []
     for part in range(VIEW_PARTS):
-        here = pl.ds(part_lanes * part, part_lanes)
+        here = pl.ds(part_rows * 128 * part, part_rows * 128)
         copies.append(pltpu.make_async_copy(observed.at[:, :, here], near.at[:, :, here], sems.at[part]))
         copies[-1].start()
     step_rows = 32
     for part in range(VIEW_PARTS):
         copies[part].wait()
 
-        @pl.loop(0, FLAT // VIEW_PARTS // step_rows)
+        @pl.loop(0, part_rows // step_rows)
         def _(step):
+            first = part * part_rows + step * step_rows
+            lanes = pl.ds(pl.multiple_of(first * 128, 128), step_rows * 128)
+            value = near[0, :, lanes].astype(F32)
+            value = jnp.concatenate([value, value[0 : 8 - VIEWS]], axis=0)
             for row in range(step_rows):
-                at = part * (FLAT // VIEW_PARTS) + step * step_rows + row
-                lanes = pl.ds(pl.multiple_of(at * 128, 128), 128)
-                wide[pl.ds(pl.multiple_of(at * 8, 8), VIEWS), :] = near[0, :, lanes].astype(F32)
+                rows = pl.ds(pl.multiple_of((first + row) * 8, 8), 8)
+                wide[rows, :] = value[:, 128 * row : 128 * (row + 1)]
 
     for update, out in enumerate((o0, o1)):
         view = order[update]
@@ -569,13 +572,6 @@
     y_stage(lines, gy, PAD, out)
 
 
-def divide(value, by):
-    guess = pl.reciprocal(by, approx=True)
-    guess = guess * (2.0 - by * guess)
-    ratio = value * guess
-    return ratio + guess * (value - ratio * by)
-
-
 def wide_terms(value):
     high, low = split(value)
     return jnp.concatenate([high, low, high], axis=1)
@@ -593,7 +589,7 @@
     for start in range(0, SLOTS * E, STEP):
         rows = slice(start, start + STEP)
         blurred = dot(wide_terms(lines[rows, :]), ei[...])
-        quotient = jnp.where(valid, divide(both_halves(o, rows), blurred), 0.0)
+        quotient = jnp.where(valid, both_halves(o, rows) / blurred, 0.0)
         lines[rows, :] = dot(wide_terms(quotient), ea[...])
     y_stage(lines, gh, E, planes)
     filter_stage(planes, kernel, twiddle, True, planes)
@@ -667,12 +663,11 @@
     pairs = []
     for number in range(count):
         at = sum(((number >> bit) & 1) << level for level, bit in enumerate(bits))
-        moved = at + 1 if at % 2 else at - 1
-        if 0 <= moved < extent:
-            other = number
-            for level, bit in enumerate(bits):
-                other = other & ~(1 << bit) | ((moved >> level) & 1) << bit
-            pairs.append((number, other))
+        moved = (at + 1 if at % 2 else at - 1) % extent
+        other = number
+        for level, bit in enumerate(bits):
+            other = other & ~(1 << bit) | ((moved >> level) & 1) << bit
+        pairs.append((number, other))
     return pairs
 
 
@@ -680,14 +675,15 @@
     return lax.ppermute(value, "blk", [(number, number ^ distance) for number in range(count)])
 
 
+def swap_slab(kind, slab, count):
+    axis, far = kind
+    if far:
+        return lax.ppermute(slab, "blk", far_pairs(count, axis))
+    return swap(slab, 1 << grid_bits(count)[axis][0], count)
+
+
 def swap_slabs(slabs, count):
-    margins = []
-    for (axis, far), slab in zip(slab_kinds(count), slabs):
-        if far:
-            margins.append(lax.ppermute(slab, "blk", far_pairs(count, axis)))
-        else:
-            margins.append(swap(slab, 1 << grid_bits(count)[axis][0], count))
-    return margins
+    return [swap_slab(kind, slab, count) for kind, slab in zip(slab_kinds(count), slabs)]
 
 
 def local(estimate, observed, psf_cells, tissue, neighbours, psf_list, psf_blend, cell_row, view_order):
@@ -708,7 +704,7 @@
         cells_kernel,
         [SM, HBM],
         CELLS,
-        (view_order, jnp.swapaxes(psf_cells, 0, 1)),
+        (view_order, pltpu.with_memory_space_constraint(jnp.swapaxes(psf_cells, 0, 1), pltpu.HBM)),
         [
             pltpu.VMEM((UPDATES, 1, KS3), F32),
             pltpu.VMEM((1, CELLROWS * 128), F32),
@@ -721,7 +717,7 @@
         functools.partial(start_kernel, count),
         [HBM],
         [ROWS] + slab_shapes,
-        (estimate.reshape(FLAT, 128),),
+        (pltpu.with_memory_space_constraint(estimate.reshape(FLAT, 128), pltpu.HBM),),
         [pltpu.VMEM((FLAT, 128), F32), pltpu.SemaphoreType.DMA],
         name="start",
     )
@@ -729,7 +725,7 @@
         views_kernel,
         [SM, HBM],
         [ROWS, ROWS],
-        (view_order, observed),
+        (view_order, pltpu.with_memory_space_constraint(observed, pltpu.HBM)),
         [
             pltpu.VMEM((1, VIEWS, FLAT * 128), BF16),
             pltpu.VMEM((8 * FLAT, 128), F32),
@@ -746,9 +742,11 @@
         if number == 0:
             arrived, rows, slabs = lax.optimization_barrier((arrived, rows, slabs))
         if number == 1:
-            arrived, targets, slabs = lax.optimization_barrier((arrived, targets, slabs))
+            kinds = slab_kinds(count)
+            far = [swap_slab(kind, slab, count) if kind[1] else None for kind, slab in zip(kinds, slabs)]
+            arrived, far, targets = lax.optimization_barrier((arrived, far, targets))
         held = jnp.concatenate(arrived, axis=0)
-    margins = swap_slabs(slabs, count)
+    margins = [swap_slab(kind, slab, count) if done is None else done for kind, slab, done in zip(kinds, slabs, far)]
     other = swap(held, 1, count)
     near_cells, far_cells = [v.reshape(count // 2, UPDATES * CELLROWS, 128) for v in (held, other)]
 

time: 54.8 us -> 50.5 us (0.922)
  the two profiles are of different devices: /device:TPU:6 before, /device:TPU:0 now
where the time goes in v4:
time: 50.5 us; the launch traced here: 50.3 us
  Pallas kernels  22.4 us (44%)
  starting transfers between devices  16.7 us (33%)
  waiting for transfers between devices  9.36 us (19%)
  between operations  0.96 us (2%)
  local copies, waits for them, and re-layouts  0.85 us (2%)
    pallas_call x7, Pallas kernels, call(): pl.pallas_call(body, in_specs=ins, out_specs=[VM] * len(outs) if many els...  22.4 us
    ppermute x13, starting transfers between devices, swap(): lax.ppermute(value, 'blk', [(number, number ^ distance) for number in ran...  14.2 us
    ppermute x13, waiting for transfers between devices, swap(): lax.ppermute(value, 'blk', [(number, number ^ distance) for number in ran...  4.78 us
    ppermute x4, waiting for transfers between devices, swap_slab(): return lax.ppermute(slab, 'blk', far_pairs(count, axis))  4.58 us
    ppermute x4, starting transfers between devices, swap_slab(): return lax.ppermute(slab, 'blk', far_pairs(count, axis))  2.45 us
  transfers between devices with their start and end apart: 17, of which 6 were waited for; matrix products, arithmetic and copies ran while one was open for 0% of the time, Pallas kernels for 17%

profile of v4, /device:TPU:0, one launch (start us, length us, event | category | flops | bytes accessed | tf_op | source)
XLA Modules:
  0.0 50.3 jit_solution(353788507653156626)
XLA Ops:
  0.0 0.7 %copy-done.9 = s32[6]{0:T(128)S(1)} copy-done((s32[6]{0:T(128)S(1)}, s32[6]{0:T(128)}, u32[]{:S(2)}) %copy-start.9) | copy-done | bytes 48
  0.7 1.3 %cells.1 = bf16[80,128]{1,0:T(8,128)(2,1)S(1)} custom-call(s32[6]{0:T(128)S(1)} %copy-done.9, f32[6,1,4913]{2,1,0:T(1,128)} %bitcast.16), custom_call_target="tpu_custom_call" | custom-call | tf_op jit(solution)/shard_map/cells/pallas_call | solution.py:649
  2.0 3.1 %collective-permute-start = (bf16[80,128]{1,0:T(8,128)(2,1)S(1)}, bf16[80,128]{1,0:T(8,128)(2,1)S(1)}, u32[]{:S(2)}, u32[]{:S(2)}) collective-permute-start(bf16[80,128]{1,0:T(8,128)(2,1)S(1)} %cells.1), channel_id=1, source_target_pairs={{0,8},{1,9},{2,10},{3,11},{4,12},{5,13},{6,14},{7,15},{8,0},{9,1},... | collective-permute-start | bytes 61448 | tf_op jit(solution)/shard_map/ppermute | solution.py:675
  5.1 2.6 %collective-permute-start.1 = (bf16[80,128]{1,0:T(8,128)(2,1)S(1)}, bf16[80,128]{1,0:T(8,128)(2,1)S(1)}, u32[]{:S(2)}, u32[]{:S(2)}) collective-permute-start(bf16[80,128]{1,0:T(8,128)(2,1)S(1)} %cells.1), channel_id=1, source_target_pairs={{0,16},{1,17},{2,18},{3,19},{4,20},{5,21},{6,22},{7,23},{8,24},{9,... | collective-permute-start | bytes 61448 | tf_op jit(solution)/shard_map/ppermute | solution.py:675
  7.7 1.8 %start.1 = (f32[2,768,128]{2,1,0:T(8,128)S(1)}, bf16[192,128]{1,0:T(8,128)(2,1)S(1)}, bf16[256,128]{1,0:T(8,128)(2,1)S(1)}, bf16[192,128]{1,0:T(8,128)(2,1)S(1)}...) custom-call(f32[864,128]{1,0:T(8,128)} %bitcast.15), custom_call_target="tpu_custom_call" | custom-call | tf_op jit(solution)/shard_map/start/pallas_call | solution.py:649
  9.6 0.5 collective-permute-done.1
  10.0 3.3 %collective-permute-done.2 = bf16[80,128]{1,0:T(8,128)(2,1)S(1)} collective-permute-done((bf16[80,128]{1,0:T(8,128)(2,1)S(1)}, bf16[80,128]{1,0:T(8,128)(2,1)S(1)}, u32[]{:S(2)}, u32[]{:S(2)}) %collective-permute-start.2) | collective-permute-done | bytes 20512 | tf_op jit(solution)/shard_map/ppermute | solution.py:675
  13.3 0.0 copy-start
  13.4 0.0 copy-start.1
  13.4 0.0 copy-start.3
  13.4 0.0 copy-start.4
  13.4 0.0 copy-start.5
  13.4 0.0 copy-start.6
  13.4 1.6 %collective-permute-start.3 = (bf16[320,128]{1,0:T(8,128)(2,1)S(1)}, bf16[320,128]{1,0:T(8,128)(2,1)S(1)}, u32[]{:S(2)}, u32[]{:S(2)}) collective-permute-start(bf16[320,128]{1,0:T(8,128)(2,1)S(1)} %constant_dynamic-update-slice_fusion), channel_id=1, source_target_pairs={{0,2},{1,3},{2,0},{3,1},{4,6},{5,7},{6,4},{7,5},{8,10},{9,11},{10,... | collective-permute-start | bytes 245768 | tf_op jit(solution)/shard_map/ppermute | solution.py:675
  15.0 1.5 %collective-permute-start.4 = (bf16[320,128]{1,0:T(8,128)(2,1)S(1)}, bf16[320,128]{1,0:T(8,128)(2,1)S(1)}, u32[]{:S(2)}, u32[]{:S(2)}) collective-permute-start(bf16[320,128]{1,0:T(8,128)(2,1)S(1)} %constant_dynamic-update-slice_fusion), channel_id=1, source_target_pairs={{0,4},{1,5},{2,6},{3,7},{4,0},{5,1},{6,2},{7,3},{8,12},{9,13},{10,... | collective-permute-start | bytes 245768 | tf_op jit(solution)/shard_map/ppermute | solution.py:675
  16.5 0.5 collective-permute-start.5
  17.0 0.1 collective-permute-start.6
  17.0 2.9 %views.1 = (f32[2,768,128]{2,1,0:T(8,128)S(1)}, f32[2,768,128]{2,1,0:T(8,128)S(1)}) custom-call(s32[6]{0:T(128)S(1)} %copy-done.9, bf16[1,6,110592]{2,1,0:T(8,128)(2,1)} %observed.1), custom_call_target="tpu_custom_call" | custom-call | tf_op jit(solution)/shard_map/views/pallas_call | solution.py:649
  20.0 2.9 %collective-permute-done.6.refs_3_ = bf16[192,128]{1,0:T(8,128)(2,1)S(1)} collective-permute-done((bf16[192,128]{1,0:T(8,128)(2,1)S(1)}, bf16[192,128]{1,0:T(8,128)(2,1)S(1)}, u32[]{:S(2)}, u32[]{:S(2)}) %collective-permute-start.6) | collective-permute-done | bytes 49184 | tf_op jit(solution)/shard_map/ppermute | solution.py:681
  23.0 0.1 collective-permute-start.8
  23.1 1.6 %collective-permute-start.10 = (bf16[256,128]{1,0:T(8,128)(2,1)S(1)}, bf16[256,128]{1,0:T(8,128)(2,1)S(1)}, u32[]{:S(2)}, u32[]{:S(2)}) collective-permute-start(bf16[256,128]{1,0:T(8,128)(2,1)S(1)} %get-tuple-element.69), channel_id=1, source_target_pairs={{0,2},{1,3},{2,0},{3,1},{4,6},{5,7},{6,4},{7,5},{8,10},{9,11},{10,... | collective-permute-start | bytes 196616 | tf_op jit(solution)/shard_map/ppermute | solution.py:675
  24.6 1.5 %collective-permute-start.9 = (bf16[192,128]{1,0:T(8,128)(2,1)S(1)}, bf16[192,128]{1,0:T(8,128)(2,1)S(1)}, u32[]{:S(2)}, u32[]{:S(2)}) collective-permute-start(bf16[192,128]{1,0:T(8,128)(2,1)S(1)} %get-tuple-element.68), channel_id=1, source_target_pairs={{0,16},{1,17},{2,18},{3,19},{4,20},{5,21},{6,22},{7,23},{8,24},{9,... | collective-permute-start | bytes 147464 | tf_op jit(solution)/shard_map/ppermute | solution.py:675
  26.8 2.0 %spectrum.2.refs_5_ = f32[16,128,128]{2,1,0:T(8,128)S(1)} custom-call(s32[6]{0:T(128)S(1)} %copy-done.9, s32[1,2,6]{2,1,0:T(2,128)S(1)} %bitcast.11, f32[1,2,6]{2,1,0:T(2,128)S(1)} %bitcast.13, s32[32]{0:T(128)S(1)} %copy-done.13, bf16[16,80,128]{2,1,0:T(8,128)(2,1)S(1)} %bitcast.7, bf16[16,80,128]{2,1,0:T(8,128)(2,1)S(1)} %bitcast.9, ...), custom_call_target="tpu_custom_call" | custom-call | tf_op jit(solution)/shard_map/spectrum/pallas_call | solution.py:649
  28.8 1.0 %collective-permute-done.9.refs_0_ = bf16[192,128]{1,0:T(8,128)(2,1)S(1)} collective-permute-done((bf16[192,128]{1,0:T(8,128)(2,1)S(1)}, bf16[192,128]{1,0:T(8,128)(2,1)S(1)}, u32[]{:S(2)}, u32[]{:S(2)}) %collective-permute-start.9) | collective-permute-done | bytes 49184 | tf_op jit(solution)/shard_map/ppermute | solution.py:675
  29.9 5.8 %first.1 = (f32[2,768,128]{2,1,0:T(8,128)S(1)}, bf16[192,128]{1,0:T(8,128)(2,1)S(1)}, bf16[256,128]{1,0:T(8,128)(2,1)S(1)}, bf16[192,128]{1,0:T(8,128)(2,1)S(1)}...) custom-call(s32[1]{0:T(128)S(6)} %copy.25.tissue, s32[1,6]{1,0:T(1,128)S(1)} %copy-done.12, ...), custom_call_target="tpu_custom_call" | custom-call | tf_op jit(solution)/shard_map/first/pallas_call | solution.py:649
  35.8 0.6 %collective-permute-start.13 = (bf16[256,128]{1,0:T(8,128)(2,1)S(1)}, bf16[256,128]{1,0:T(8,128)(2,1)S(1)}, u32[]{:S(2)}, u32[]{:S(2)}) collective-permute-start(bf16[256,128]{1,0:T(8,128)(2,1)S(1)} %get-tuple-element.82), channel_id=1, source_target_pairs={{0,2},{1,3},{2,0},{3,1},{4,6},{5,7},{6,4},{7,5},{8,10},{9,11},{10,... | collective-permute-start | bytes 196616 | tf_op jit(solution)/shard_map/ppermute | solution.py:675
  36.4 1.3 %collective-permute-start.12 = (bf16[192,128]{1,0:T(8,128)(2,1)S(1)}, bf16[192,128]{1,0:T(8,128)(2,1)S(1)}, u32[]{:S(2)}, u32[]{:S(2)}) collective-permute-start(bf16[192,128]{1,0:T(8,128)(2,1)S(1)} %get-tuple-element.81), channel_id=1, source_target_pairs={{0,16},{1,17},{2,18},{3,19},{4,20},{5,21},{6,22},{7,23},{8,24},{9,... | collective-permute-start | bytes 147464 | tf_op jit(solution)/shard_map/ppermute | solution.py:675
  37.6 2.4 %collective-permute-start.15 = (bf16[192,128]{1,0:T(8,128)(2,1)S(1)}, bf16[192,128]{1,0:T(8,128)(2,1)S(1)}, u32[]{:S(2)}, u32[]{:S(2)}) collective-permute-start(bf16[192,128]{1,0:T(8,128)(2,1)S(1)} %get-tuple-element.84), channel_id=1, source_target_pairs={{0,20},{1,21},{2,22},{3,23},{4,16},{5,17},{6,18},{7,19},{8,28},{9,... | collective-permute-start | bytes 147464 | tf_op jit(solution)/shard_map/ppermute | solution.py:681
  40.0 2.0 %spectrum.3.refs_5_ = f32[16,128,128]{2,1,0:T(8,128)S(1)} custom-call(s32[6]{0:T(128)S(1)} %copy-done.9, s32[1,2,6]{2,1,0:T(2,128)S(1)} %bitcast.12, f32[1,2,6]{2,1,0:T(2,128)S(1)} %bitcast.14, s32[32]{0:T(128)S(1)} %copy-done.13, bf16[16,80,128]{2,1,0:T(8,128)(2,1)S(1)} %bitcast.8, bf16[16,80,128]{2,1,0:T(8,128)(2,1)S(1)} %bitcast.10, ...), custom_call_target="tpu_custom_call" | custom-call | tf_op jit(solution)/shard_map/spectrum/pallas_call | solution.py:649
  42.0 1.6 %collective-permute-done.15.refs_3_ = bf16[192,128]{1,0:T(8,128)(2,1)S(1)} collective-permute-done((bf16[192,128]{1,0:T(8,128)(2,1)S(1)}, bf16[192,128]{1,0:T(8,128)(2,1)S(1)}, u32[]{:S(2)}, u32[]{:S(2)}) %collective-permute-start.15) | collective-permute-done | bytes 49184 | tf_op jit(solution)/shard_map/ppermute | solution.py:681
  43.6 0.1 collective-permute-done.16.refs_4_
  43.7 6.5 %last.1 = f32[864,128]{1,0:T(8,128)} custom-call(s32[1]{0:T(128)S(6)} %copy.25.tissue, s32[1,6]{1,0:T(1,128)S(1)} %copy-done.12, f32[2,768,128]{2,1,0:T(8,128)S(1)} %get-tuple-element.80.u, bf16[192,128]{1,0:T(8,128)(2,1)S(1)} %collective-permute-done.12.refs_0_, bf16[256,128]{1,0:T(8,128)(2,1)S(1)} %collective-permute-done.13.refs_1_, ...), custom_call_target="tpu_custom_call" | custom-call | tf_op jit(solution)/shard_map/last/pallas_call | solution.py:649
  (45 shorter events, 0.2 us)
Async XLA Ops:
  0.0 26.8 %copy-start.7 = (bf16[128,256]{1,0:T(8,128)(2,1)S(1)}, bf16[128,256]{1,0:T(8,128)(2,1)}, u32[]{:S(2)}) copy-start(bf16[128,256]{1,0:T(8,128)(2,1)} %constant.24.clone.table) | copy-start | bytes 196612
  0.0 26.8 %copy-start.2 = (f32[2,17,8,128]{3,2,1,0:T(8,128)S(1)}, f32[2,17,8,128]{3,2,1,0:T(8,128)}, u32[]{:S(2)}) copy-start(f32[2,17,8,128]{3,2,1,0:T(8,128)} %constant.25.clone.turns) | copy-start | bytes 417796
  0.0 26.8 %copy-start.8 = (bf16[128,144]{1,0:T(8,128)(2,1)S(1)}, bf16[128,144]{1,0:T(8,128)(2,1)}, u32[]{:S(2)}) copy-start(bf16[128,144]{1,0:T(8,128)(2,1)} %constant.23.clone.table_y_ref) | copy-start | bytes 110596
  0.0 0.7 %copy-start.9 = (s32[6]{0:T(128)S(1)}, s32[6]{0:T(128)}, u32[]{:S(2)}) copy-start(s32[6]{0:T(128)} %order.7) | copy-start | bytes 76
  0.7 26.1 %copy-start.10 = (s32[1,6,2]{1,2,0:T(2,128)S(1)}, s32[1,6,2]{1,2,0:T(2,128)}, u32[]{:S(2)}) copy-start(s32[1,6,2]{1,2,0:T(2,128)} %param.23) | copy-start | bytes 148
  0.7 26.1 %copy-start.11 = (f32[1,6,2]{1,2,0:T(2,128)S(1)}, f32[1,6,2]{1,2,0:T(2,128)}, u32[]{:S(2)}) copy-start(f32[1,6,2]{1,2,0:T(2,128)} %param.24) | copy-start | bytes 148
  0.7 26.1 %copy-start.13 = (s32[32]{0:T(128)S(1)}, s32[32]{0:T(128)}, u32[]{:S(2)}) copy-start(s32[32]{0:T(128)} %cell_row.3) | copy-start | bytes 388
  2.0 7.5 %collective-permute-start = (bf16[80,128]{1,0:T(8,128)(2,1)S(1)}, bf16[80,128]{1,0:T(8,128)(2,1)S(1)}, u32[]{:S(2)}, u32[]{:S(2)}) collective-permute-start(bf16[80,128]{1,0:T(8,128)(2,1)S(1)} %cells.1), channel_id=1, source_target_pairs={{0,8},{1,9},{2,10},{3,11},{4,12},{5,13},{6,14},{7,15},{8,0},{9,1},... | collective-permute-start | bytes 61448 | tf_op jit(solution)/shard_map/ppermute | solution.py:675
  5.1 4.9 %collective-permute-start.1 = (bf16[80,128]{1,0:T(8,128)(2,1)S(1)}, bf16[80,128]{1,0:T(8,128)(2,1)S(1)}, u32[]{:S(2)}, u32[]{:S(2)}) collective-permute-start(bf16[80,128]{1,0:T(8,128)(2,1)S(1)} %cells.1), channel_id=1, source_target_pairs={{0,16},{1,17},{2,18},{3,19},{4,20},{5,21},{6,22},{7,23},{8,24},{9,... | collective-permute-start | bytes 61448 | tf_op jit(solution)/shard_map/ppermute | solution.py:675
  7.7 5.6 %collective-permute-start.2 = (bf16[80,128]{1,0:T(8,128)(2,1)S(1)}, bf16[80,128]{1,0:T(8,128)(2,1)S(1)}, u32[]{:S(2)}, u32[]{:S(2)}) collective-permute-start(bf16[80,128]{1,0:T(8,128)(2,1)S(1)} %cells.1), channel_id=1, source_target_pairs={{0,24},{1,25},{2,26},{3,27},{4,28},{5,29},{6,30},{7,31},{8,16},{9,... | collective-permute-start | bytes 61448 | tf_op jit(solution)/shard_map/ppermute | solution.py:675
  13.3 16.5 %copy-start = (bf16[768,256]{1,0:T(8,128)(2,1)S(1)}, bf16[768,256]{1,0:T(8,128)(2,1)}, u32[]{:S(2)}) copy-start(bf16[768,256]{1,0:T(8,128)(2,1)} %constant.18.clone.refs_7_) | copy-start | bytes 1179652
  13.4 16.5 %copy-start.1 = (bf16[768,256]{1,0:T(8,128)(2,1)S(1)}, bf16[768,256]{1,0:T(8,128)(2,1)}, u32[]{:S(2)}) copy-start(bf16[768,256]{1,0:T(8,128)(2,1)} %constant.19.clone.refs_9_) | copy-start | bytes 1179652
  13.4 16.5 %copy-start.3 = (f32[2,16,8,128]{3,2,1,0:T(8,128)S(1)}, f32[2,16,8,128]{3,2,1,0:T(8,128)}, u32[]{:S(2)}) copy-start(f32[2,16,8,128]{3,2,1,0:T(8,128)} %constant.26.clone.refs_12_) | copy-start | bytes 393220
  13.4 16.5 %copy-start.4 = (bf16[128,384]{1,0:T(8,128)(2,1)S(1)}, bf16[128,384]{1,0:T(8,128)(2,1)}, u32[]{:S(2)}) copy-start(bf16[128,384]{1,0:T(8,128)(2,1)} %constant.20.clone.refs_8_) | copy-start | bytes 294916
  13.4 16.5 %copy-start.5 = (bf16[128,288]{1,0:T(8,128)(2,1)S(1)}, bf16[128,288]{1,0:T(8,128)(2,1)}, u32[]{:S(2)}) copy-start(bf16[128,288]{1,0:T(8,128)(2,1)} %constant.21.clone.refs_10_) | copy-start | bytes 221188
  13.4 16.5 %copy-start.6 = (bf16[96,384]{1,0:T(8,128)(2,1)S(1)}, bf16[96,384]{1,0:T(8,128)(2,1)}, u32[]{:S(2)}) copy-start(bf16[96,384]{1,0:T(8,128)(2,1)} %constant.22.clone.refs_11_) | copy-start | bytes 221188
  13.4 16.5 %copy-start.12 = (s32[1,6]{1,0:T(1,128)S(1)}, s32[1,6]{1,0:T(1,128)}, u32[]{:S(2)}) copy-start(s32[1,6]{1,0:T(1,128)} %present.3) | copy-start | bytes 76
  13.4 9.4 %collective-permute-start.3 = (bf16[320,128]{1,0:T(8,128)(2,1)S(1)}, bf16[320,128]{1,0:T(8,128)(2,1)S(1)}, u32[]{:S(2)}, u32[]{:S(2)}) collective-permute-start(bf16[320,128]{1,0:T(8,128)(2,1)S(1)} %constant_dynamic-update-slice_fusion), channel_id=1, source_target_pairs={{0,2},{1,3},{2,0},{3,1},{4,6},{5,7},{6,4},{7,5},{8,10},{9,11},{10,... | collective-permute-start | bytes 245768 | tf_op jit(solution)/shard_map/ppermute | solution.py:675
  15.0 7.9 %collective-permute-start.4 = (bf16[320,128]{1,0:T(8,128)(2,1)S(1)}, bf16[320,128]{1,0:T(8,128)(2,1)S(1)}, u32[]{:S(2)}, u32[]{:S(2)}) collective-permute-start(bf16[320,128]{1,0:T(8,128)(2,1)S(1)} %constant_dynamic-update-slice_fusion), channel_id=1, source_target_pairs={{0,4},{1,5},{2,6},{3,7},{4,0},{5,1},{6,2},{7,3},{8,12},{9,13},{10,... | collective-permute-start | bytes 245768 | tf_op jit(solution)/shard_map/ppermute | solution.py:675
  16.5 6.4 %collective-permute-start.5 = (bf16[320,128]{1,0:T(8,128)(2,1)S(1)}, bf16[320,128]{1,0:T(8,128)(2,1)S(1)}, u32[]{:S(2)}, u32[]{:S(2)}) collective-permute-start(bf16[320,128]{1,0:T(8,128)(2,1)S(1)} %constant_dynamic-update-slice_fusion), channel_id=1, source_target_pairs={{0,6},{1,7},{2,4},{3,5},{4,2},{5,3},{6,0},{7,1},{8,14},{9,15},{10,... | collective-permute-start | bytes 245768 | tf_op jit(solution)/shard_map/ppermute | solution.py:675
  17.0 5.9 %collective-permute-start.6 = (bf16[192,128]{1,0:T(8,128)(2,1)S(1)}, bf16[192,128]{1,0:T(8,128)(2,1)S(1)}, u32[]{:S(2)}, u32[]{:S(2)}) collective-permute-start(bf16[192,128]{1,0:T(8,128)(2,1)S(1)} %get-tuple-element.60), channel_id=1, source_target_pairs={{0,20},{1,21},{2,22},{3,23},{4,16},{5,17},{6,18},{7,19},{8,28},{9,... | collective-permute-start | bytes 147464 | tf_op jit(solution)/shard_map/ppermute | solution.py:681
  17.0 5.8 %collective-permute-start.7 = (bf16[192,128]{1,0:T(8,128)(2,1)S(1)}, bf16[192,128]{1,0:T(8,128)(2,1)S(1)}, u32[]{:S(2)}, u32[]{:S(2)}) collective-permute-start(bf16[192,128]{1,0:T(8,128)(2,1)S(1)} %get-tuple-element.61), channel_id=1, source_target_pairs={{0,9},{1,8},{2,11},{3,10},{4,13},{5,12},{6,15},{7,14},{8,1},{9,0},... | collective-permute-start | bytes 147464 | tf_op jit(solution)/shard_map/ppermute | solution.py:681
  23.0 3.8 %collective-permute-start.8 = (bf16[1280,128]{1,0:T(8,128)(2,1)S(1)}, bf16[1280,128]{1,0:T(8,128)(2,1)S(1)}, u32[]{:S(2)}, u32[]{:S(2)}) collective-permute-start(bf16[1280,128]{1,0:T(8,128)(2,1)S(1)} %constant_dynamic-update-slice_fusion.4), channel_id=1, source_target_pairs={{0,1},{1,0},{2,3},{3,2},{4,5},{5,4},{6,7},{7,6},{8,9},{9,8},{10,11... | collective-permute-start | bytes 983048 | tf_op jit(solution)/shard_map/ppermute | solution.py:675
  23.1 6.8 %collective-permute-start.10 = (bf16[256,128]{1,0:T(8,128)(2,1)S(1)}, bf16[256,128]{1,0:T(8,128)(2,1)S(1)}, u32[]{:S(2)}, u32[]{:S(2)}) collective-permute-start(bf16[256,128]{1,0:T(8,128)(2,1)S(1)} %get-tuple-element.69), channel_id=1, source_target_pairs={{0,2},{1,3},{2,0},{3,1},{4,6},{5,7},{6,4},{7,5},{8,10},{9,11},{10,... | collective-permute-start | bytes 196616 | tf_op jit(solution)/shard_map/ppermute | solution.py:675
  24.6 5.2 %collective-permute-start.9 = (bf16[192,128]{1,0:T(8,128)(2,1)S(1)}, bf16[192,128]{1,0:T(8,128)(2,1)S(1)}, u32[]{:S(2)}, u32[]{:S(2)}) collective-permute-start(bf16[192,128]{1,0:T(8,128)(2,1)S(1)} %get-tuple-element.68), channel_id=1, source_target_pairs={{0,16},{1,17},{2,18},{3,19},{4,20},{5,21},{6,22},{7,23},{8,24},{9,... | collective-permute-start | bytes 147464 | tf_op jit(solution)/shard_map/ppermute | solution.py:675
  26.1 3.7 %collective-permute-start.11 = (bf16[192,128]{1,0:T(8,128)(2,1)S(1)}, bf16[192,128]{1,0:T(8,128)(2,1)S(1)}, u32[]{:S(2)}, u32[]{:S(2)}) collective-permute-start(bf16[192,128]{1,0:T(8,128)(2,1)S(1)} %get-tuple-element.70), channel_id=1, source_target_pairs={{0,1},{1,0},{2,3},{3,2},{4,5},{5,4},{6,7},{7,6},{8,9},{9,8},{10,11... | collective-permute-start | bytes 147464 | tf_op jit(solution)/shard_map/ppermute | solution.py:675
  35.8 8.0 %collective-permute-start.13 = (bf16[256,128]{1,0:T(8,128)(2,1)S(1)}, bf16[256,128]{1,0:T(8,128)(2,1)S(1)}, u32[]{:S(2)}, u32[]{:S(2)}) collective-permute-start(bf16[256,128]{1,0:T(8,128)(2,1)S(1)} %get-tuple-element.82), channel_id=1, source_target_pairs={{0,2},{1,3},{2,0},{3,1},{4,6},{5,7},{6,4},{7,5},{8,10},{9,11},{10,... | collective-permute-start | bytes 196616 | tf_op jit(solution)/shard_map/ppermute | solution.py:675
  36.4 5.7 %collective-permute-start.12 = (bf16[192,128]{1,0:T(8,128)(2,1)S(1)}, bf16[192,128]{1,0:T(8,128)(2,1)S(1)}, u32[]{:S(2)}, u32[]{:S(2)}) collective-permute-start(bf16[192,128]{1,0:T(8,128)(2,1)S(1)} %get-tuple-element.81), channel_id=1, source_target_pairs={{0,16},{1,17},{2,18},{3,19},{4,20},{5,21},{6,22},{7,23},{8,24},{9,... | collective-permute-start | bytes 147464 | tf_op jit(solution)/shard_map/ppermute | solution.py:675
  37.6 4.4 %collective-permute-start.14 = (bf16[192,128]{1,0:T(8,128)(2,1)S(1)}, bf16[192,128]{1,0:T(8,128)(2,1)S(1)}, u32[]{:S(2)}, u32[]{:S(2)}) collective-permute-start(bf16[192,128]{1,0:T(8,128)(2,1)S(1)} %get-tuple-element.83), channel_id=1, source_target_pairs={{0,1},{1,0},{2,3},{3,2},{4,5},{5,4},{6,7},{7,6},{8,9},{9,8},{10,11... | collective-permute-start | bytes 147464 | tf_op jit(solution)/shard_map/ppermute | solution.py:675
  37.6 6.0 %collective-permute-start.15 = (bf16[192,128]{1,0:T(8,128)(2,1)S(1)}, bf16[192,128]{1,0:T(8,128)(2,1)S(1)}, u32[]{:S(2)}, u32[]{:S(2)}) collective-permute-start(bf16[192,128]{1,0:T(8,128)(2,1)S(1)} %get-tuple-element.84), channel_id=1, source_target_pairs={{0,20},{1,21},{2,22},{3,23},{4,16},{5,17},{6,18},{7,19},{8,28},{9,... | collective-permute-start | bytes 147464 | tf_op jit(solution)/shard_map/ppermute | solution.py:681
  40.0 3.7 %collective-permute-start.16 = (bf16[192,128]{1,0:T(8,128)(2,1)S(1)}, bf16[192,128]{1,0:T(8,128)(2,1)S(1)}, u32[]{:S(2)}, u32[]{:S(2)}) collective-permute-start(bf16[192,128]{1,0:T(8,128)(2,1)S(1)} %get-tuple-element.85), channel_id=1, source_target_pairs={{0,9},{1,8},{2,11},{3,10},{4,13},{5,12},{6,15},{7,14},{8,1},{9,0},... | collective-permute-start | bytes 147464 | tf_op jit(solution)/shard_map/ppermute | solution.py:681

commit v5 on v4

--- a/solution.py
+++ b/solution.py
@@ -187,6 +187,48 @@
                 flat_ref[pl.ds(first + m, 8, stride=3), :] = out[m]
 
 
+def squeeze(pieces):
+    out = [None, None, None]
+    for piece, value in enumerate(pieces):
+        spot, start = E * piece // 128, E * piece % 128
+        moved = pltpu.roll(value, start, 1) if start else value
+        out[spot] = moved if out[spot] is None else jnp.where(lane_iota(moved.shape) < start, out[spot], moved)
+        if start + E > 128:
+            out[spot + 1] = moved
+    return out
+
+
+def stretch(full):
+    return [cut(full, piece, 0) for piece in range(8)]
+
+
+def pack_x_side(value):
+    last = value[144:192]
+    lane = lane_iota(last.shape)
+    out = []
+    for part in range(3):
+        moved = pltpu.roll(last, (96 - 32 * part) % 128, 1)
+        out.append(jnp.where(lane < 96, value[48 * part : 48 * (part + 1)], moved))
+    return jnp.concatenate(out, axis=0)
+
+
+def unpack_x_side(value):
+    parts = [value[48 * part : 48 * (part + 1)] for part in range(3)]
+    lane = lane_iota(parts[0].shape)
+    last = pltpu.roll(parts[0], 32, 1)
+    for part in range(1, 3):
+        last = jnp.where(lane < 32 * part, last, pltpu.roll(parts[part], (32 + 32 * part) % 128, 1))
+    return jnp.concatenate(parts + [last], axis=0)
+
+
+def pack_z_side(blocks):
+    return jnp.concatenate(squeeze(blocks), axis=0)
+
+
+def unpack_z_side(value):
+    return stretch([value[48 * part : 48 * (part + 1)] for part in range(3)])
+
+
 def x_picks(wide, packed, low_start, high_start):
     place = packed % 128
     start = jnp.where(packed >= 128, high_start, low_start)
@@ -208,8 +250,8 @@
         value = found[0:192, 128 * face : 128 * (face + 1)]
         for group in range(1, 4):
             part = found[192 * group : 192 * (group + 1), 128 * face : 128 * (face + 1)]
-            value = value + pltpu.roll(part, 32 * group, 1)
-        faces.append(value.astype(BF16))
+            value = value + pltpu.roll(part, 3 * MARGIN * group, 1)
+        faces.append(pack_x_side(value).astype(BF16))
     x0, x1 = faces
     low_rows, high_rows = [], []
     for slot in range(SLOTS):
@@ -217,13 +259,8 @@
         high_rows.append(both_halves(rows_ref, slice(E * slot + E - MARGIN, E * (slot + 1))))
     y0, y1 = jnp.concatenate(low_rows, axis=0), jnp.concatenate(high_rows, axis=0)
     y0, y1 = [jnp.concatenate([v[:, 0:128], v[:, 128:256]], axis=0).astype(BF16) for v in (y0, y1)]
-    lane = lane_iota((192, 128))
-    first = rows_ref[0, 0:192, :]
-    second = pltpu.roll(rows_ref[0, 192:384, :], 64, 1)
-    z0 = jnp.where(lane < 64, first, second).astype(BF16)
-    first = rows_ref[1, 384:576, :]
-    second = pltpu.roll(rows_ref[1, 576:768, :], 64, 1)
-    z1 = jnp.where(lane < 64, first, second).astype(BF16)
+    z0 = pack_z_side([rows_ref[0, E * slot : E * (slot + 1), :] for slot in range(MARGIN)]).astype(BF16)
+    z1 = pack_z_side([rows_ref[1, E * slot : E * (slot + 1), :] for slot in range(MARGIN, SLOTS)]).astype(BF16)
     return (z0, z1), (y0, y1), (x0, x1)
 
 
@@ -242,25 +279,21 @@
     ]
     rows, columns = both_iotas()
     picks = x_picks(columns, rows, PAD - MARGIN, E)
+    sides = [unpack_x_side(v) for v in (xm, xp)]
     parts = []
     for group in range(4):
-        pair = [pltpu.roll(v, 128 - 32 * group, 1) if group else v for v in (xm, xp)]
+        pair = [pltpu.roll(v, 128 - 3 * MARGIN * group, 1) if group else v for v in sides]
         parts.append(jnp.concatenate(pair, axis=1))
     side = dot(jnp.concatenate(parts, axis=0).astype(BF16), picks)
     ym_rows, yp_rows = [jnp.concatenate([v[0:128], v[128:256]], axis=1) for v in (ym, yp)]
-    z_sides = []
-    for value in (zp, zm):
-        z_sides.append(pltpu.roll(value, 64, 1))
-        z_sides.append(value)
+    z_sides = [pltpu.roll(v, 64, 1) for value in (zp, zm) for v in unpack_z_side(value)]
     lane = lane_iota((E, 128))
     for slot in range(SLOTS):
-        group, inner = slot // 4, slot % 4
         core = both_halves(rows_ref, slice(E * slot, E * (slot + 1)))
         high, low = split(core)
         added = side[E * slot : E * (slot + 1)]
         full = high.astype(F32) + added
-        z_side = z_sides[group][E * inner : E * (inner + 1), :]
-        right = jnp.where(lane < 64, full[:, 128:256], z_side)
+        right = jnp.where(lane < 64, full[:, 128:256], jnp.where(lane < 64 + E, z_sides[slot], 0.0))
         high_ref[PAD * slot : PAD * slot + E, 0:128] = full[:, 0:128].astype(BF16)
         high_ref[PAD * slot : PAD * slot + E, 128:256] = right.astype(BF16)
         rows = slice(MARGIN * slot, MARGIN * (slot + 1))
@@ -478,13 +511,28 @@
 
 
 def gather_rounds(count):
-    bits = list(range(count.bit_length() - 1))
-    rounds = [bits[:1]]
-    bits = bits[1:]
+    axes = grid_bits(count)
+    bits = axes[2][:2] + axes[1][:1] + axes[0][1:2]
+    bits += [bit for bit in range(1, count.bit_length() - 1) if bit not in bits]
+    rounds = []
     while bits:
         rounds.append(bits[:2])
         bits = bits[2:]
-    return rounds[::-1]
+    return rounds + [[0]]
+
+
+def riders(count):
+    axes = grid_bits(count)
+    found = {1: (0, 0)}
+    if axes[1]:
+        found[1 << axes[1][0]] = (1, 0)
+    found[1 << axes[2][0]] = (2, 0)
+    for axis in (1, 2):
+        if len(axes[axis]) == 2:
+            found[1 << axes[axis][0] | 1 << axes[axis][1]] = (axis, 1)
+    if len(axes[0]) == 2:
+        found[1 << axes[0][1]] = (0, 1)
+    return found
 
 
 def odd_places(count):
@@ -493,12 +541,8 @@
 
 
 def slab_kinds(count):
-    return [
-        (axis, far)
-        for far in (0, 1)
-        for axis in (2, 1, 0)
-        if len(grid_bits(count)[axis]) > far
-    ]
+    kinds = [(1, 0), (2, 0), (2, 1), (0, 1), (0, 0), (1, 1)]
+    return [kind for kind in kinds if len(grid_bits(count)[kind[0]]) > kind[1]]
 
 
 def store_slabs(count, slabs, outs):
@@ -508,7 +552,10 @@
         out[...] = jnp.where(odds[axis], high, low) if far else jnp.where(odds[axis], low, high)
 
 
-def cells_kernel(order, cells, out, got, pad, sems):
+def start_kernel(count, order, cells, est, u_out, cells_out, *refs):
+    outs, (got, pad, flat, sems) = refs[:-4], refs[-4:]
+    loading = pltpu.make_async_copy(est, flat, sems.at[UPDATES])
+    loading.start()
     copies = []
     for update in range(UPDATES):
         copies.append(pltpu.make_async_copy(cells.at[order[update]], got.at[update], sems.at[update]))
@@ -520,14 +567,8 @@
         wide = pad[...]
         rows = [wide[:, 128 * row : 128 * (row + 1)] for row in range(CELLROWS)]
         here = slice(CELLROWS * update, CELLROWS * (update + 1))
-        out[here, :] = jnp.concatenate(rows, axis=0).astype(BF16)
-
-
-def start_kernel(count, est, u_out, *refs):
-    outs, (flat, sem) = refs[:-2], refs[-2:]
-    copy = pltpu.make_async_copy(est, flat, sem)
-    copy.start()
-    copy.wait()
+        cells_out[here, :] = jnp.concatenate(rows, axis=0).astype(BF16)
+    loading.wait()
     unflatten(lambda row: flat[pl.ds(row, 8, stride=3), :], u_out)
     store_slabs(count, pack_slabs(u_out), outs)
 
@@ -632,7 +673,7 @@
     return jax.ShapeDtypeStruct(dims, kind)
 
 
-SLAB = shape((192, 128), BF16)
+SLAB = shape((144, 128), BF16)
 WIDE_SLAB = shape((256, 128), BF16)
 SLABS = [SLAB, WIDE_SLAB, SLAB]
 CELLS = shape((UPDATES * CELLROWS, 128), BF16)
@@ -663,10 +704,13 @@
     pairs = []
     for number in range(count):
         at = sum(((number >> bit) & 1) << level for level, bit in enumerate(bits))
-        moved = (at + 1 if at % 2 else at - 1) % extent
+        moved = at + 1 if at % 2 else at - 1
         other = number
-        for level, bit in enumerate(bits):
-            other = other & ~(1 << bit) | ((moved >> level) & 1) << bit
+        if 0 <= moved < extent:
+            for level, bit in enumerate(bits):
+                other = other & ~(1 << bit) | ((moved >> level) & 1) << bit
+        else:
+            other = number ^ (1 if axis else 2)
         pairs.append((number, other))
     return pairs
 
@@ -700,25 +744,22 @@
     lists = jnp.swapaxes(psf_list, 1, 2)
     blend = jnp.swapaxes(psf_blend, 1, 2)
 
-    cells = call(
-        cells_kernel,
-        [SM, HBM],
-        CELLS,
-        (view_order, pltpu.with_memory_space_constraint(jnp.swapaxes(psf_cells, 0, 1), pltpu.HBM)),
+    slab_shapes = [SLABS[axis] for axis, far in slab_kinds(count)]
+    rows, cells, *slabs = call(
+        functools.partial(start_kernel, count),
+        [SM, HBM, HBM],
+        [ROWS, CELLS] + slab_shapes,
+        (
+            view_order,
+            pltpu.with_memory_space_constraint(jnp.swapaxes(psf_cells, 0, 1), pltpu.HBM),
+            pltpu.with_memory_space_constraint(estimate.reshape(FLAT, 128), pltpu.HBM),
+        ),
         [
             pltpu.VMEM((UPDATES, 1, KS3), F32),
             pltpu.VMEM((1, CELLROWS * 128), F32),
-            pltpu.SemaphoreType.DMA((UPDATES,)),
+            pltpu.VMEM((FLAT, 128), F32),
+            pltpu.SemaphoreType.DMA((UPDATES + 1,)),
         ],
-        name="cells",
-    )
-    slab_shapes = [SLABS[axis] for axis, far in slab_kinds(count)]
-    rows, *slabs = call(
-        functools.partial(start_kernel, count),
-        [HBM],
-        [ROWS] + slab_shapes,
-        (pltpu.with_memory_space_constraint(estimate.reshape(FLAT, 128), pltpu.HBM),),
-        [pltpu.VMEM((FLAT, 128), F32), pltpu.SemaphoreType.DMA],
         name="start",
     )
     targets = call(
@@ -733,21 +774,36 @@
         ],
         name="views",
     )
+    slabs = dict(zip(slab_kinds(count), slabs))
+    riding = riders(count)
+    margins = {}
     held = cells
-    for number, bits in enumerate(gather_rounds(count)[:-1]):
+    for number, bits in enumerate(gather_rounds(count)):
         arrived = [held]
+        size = held.shape[0]
         for part in range(1, 2 ** len(bits)):
             distance = sum(((part >> level) & 1) << bit for level, bit in enumerate(bits))
-            arrived.append(swap(held, distance, count))
+            load = [held]
+            kind = riding.get(distance)
+            if kind is not None:
+                load.append(slabs[kind])
+            if distance == 1 and (0, 1) in margins:
+                load.append(margins[0, 1])
+            got = swap(jnp.concatenate(load, axis=0) if len(load) > 1 else held, distance, count)
+            arrived.append(got[:size])
+            if kind is not None:
+                margins[kind] = got[size : size + slabs[kind].shape[0]]
+            if distance == 1 and (0, 1) in margins:
+                margins[0, 1] = got[got.shape[0] - SLAB.shape[0] :]
         if number == 0:
-            arrived, rows, slabs = lax.optimization_barrier((arrived, rows, slabs))
-        if number == 1:
-            kinds = slab_kinds(count)
-            far = [swap_slab(kind, slab, count) if kind[1] else None for kind, slab in zip(kinds, slabs)]
-            arrived, far, targets = lax.optimization_barrier((arrived, far, targets))
-        held = jnp.concatenate(arrived, axis=0)
-    margins = [swap_slab(kind, slab, count) if done is None else done for kind, slab, done in zip(kinds, slabs, far)]
-    other = swap(held, 1, count)
+            arrived, targets = lax.optimization_barrier((arrived, targets))
+        if bits != [0]:
+            held = jnp.concatenate(arrived, axis=0)
+    other = arrived[1]
+    for kind in slab_kinds(count):
+        if kind not in margins:
+            margins[kind] = swap_slab(kind, slabs[kind], count)
+    margins = [margins[kind] for kind in slab_kinds(count)]
     near_cells, far_cells = [v.reshape(count // 2, UPDATES * CELLROWS, 128) for v in (held, other)]
 
     def spectrum(update):

time: 50.5 us -> 46.9 us (0.929)
  waiting for transfers between devices: 9.36 us -> 7.31 us
  starting transfers between devices: 16.7 us -> 15.3 us
    ppermute x4 -> x2, waiting for transfers between devices: 4.58 us -> 0.08 us  [swap_slab(): return lax.ppermute(slab, 'blk', far_pairs(count, axis))]
    ppermute x13 -> x10, waiting for transfers between devices: 4.78 us -> 7.23 us  [swap(): lax.ppermute(value, 'blk', [(number, number ^ distance) for number in ran...]
    ppermute x4 -> x2, starting transfers between devices: 2.45 us -> 1.02 us  [swap_slab(): return lax.ppermute(slab, 'blk', far_pairs(count, axis))]
    pallas_call x7 -> x6, Pallas kernels: 22.4 us -> 22 us  [call(): pl.pallas_call(body, in_specs=ins, out_specs=[VM] * len(outs) if many els...]
    ppermute x13 -> x10, starting transfers between devices: 14.2 us -> 14.3 us  [swap(): lax.ppermute(value, 'blk', [(number, number ^ distance) for number in ran...]
  transfers between devices with their start and end apart: 17 -> 12, of which waited for: 6 -> 6; matrix products, arithmetic and copies ran while one was open for 0% -> 0% of each run, Pallas kernels for 17% -> 11%
where the time goes in v5:
time: 46.9 us; the launch traced here: 46.7 us
  Pallas kernels  22 us (47%)
  starting transfers between devices  15.3 us (33%)
  waiting for transfers between devices  7.31 us (16%)
  between operations  1.03 us (2%)
  local copies, waits for them, and re-layouts  1.01 us (2%)
    pallas_call x6, Pallas kernels, call(): pl.pallas_call(body, in_specs=ins, out_specs=[VM] * len(outs) if many els...  22 us
    ppermute x10, starting transfers between devices, swap(): lax.ppermute(value, 'blk', [(number, number ^ distance) for number in ran...  14.3 us
    ppermute x10, waiting for transfers between devices, swap(): lax.ppermute(value, 'blk', [(number, number ^ distance) for number in ran...  7.23 us
    ppermute x2, starting transfers between devices, swap_slab(): return lax.ppermute(slab, 'blk', far_pairs(count, axis))  1.02 us
  transfers between devices with their start and end apart: 12, of which 6 were waited for; matrix products, arithmetic and copies ran while one was open for 0% of the time, Pallas kernels for 11%

profile of v5, /device:TPU:0, one launch (start us, length us, event | category | flops | bytes accessed | tf_op | source)
XLA Modules:
  0.0 46.7 jit_solution(15118557438717060789)
XLA Ops:
  0.0 0.7 %copy-done.9 = s32[6]{0:T(128)S(1)} copy-done((s32[6]{0:T(128)S(1)}, s32[6]{0:T(128)}, u32[]{:S(2)}) %copy-start.9) | copy-done | bytes 48
  0.7 2.5 %start.1 = (f32[2,768,128]{2,1,0:T(8,128)S(1)}, bf16[80,128]{1,0:T(8,128)(2,1)S(1)}, bf16[256,128]{1,0:T(8,128)(2,1)S(1)}, bf16[144,128]{1,0:T(8,128)(2,1)S(1)},...) custom-call(s32[6]{0:T(128)S(1)} %copy-done.9, f32[6,1,4913]{2,1,0:T(1,128)} %bitcast.16, ...), custom_call_target="tpu_custom_call" | custom-call | tf_op jit(solution)/shard_map/start/pallas_call | solution.py:690
  3.2 4.1 %collective-permute-start = (bf16[224,128]{1,0:T(8,128)(2,1)S(1)}, bf16[224,128]{1,0:T(8,128)(2,1)S(1)}, u32[]{:S(2)}, u32[]{:S(2)}) collective-permute-start(bf16[224,128]{1,0:T(8,128)(2,1)S(1)} %get-tuple-element.96), channel_id=1, source_target_pairs={{0,16},{1,17},{2,18},{3,19},{4,20},{5,21},{6,22},{7,23},{8,24},{9,... | collective-permute-start | bytes 172040 | tf_op jit(solution)/shard_map/ppermute | solution.py:719
  7.3 1.3 %collective-permute-start.2 = (bf16[224,128]{1,0:T(8,128)(2,1)S(1)}, bf16[224,128]{1,0:T(8,128)(2,1)S(1)}, u32[]{:S(2)}, u32[]{:S(2)}) collective-permute-start(bf16[224,128]{1,0:T(8,128)(2,1)S(1)} %get-tuple-element.95), channel_id=1, source_target_pairs={{0,20},{1,21},{2,22},{3,23},{4,16},{5,17},{6,18},{7,19},{8,28},{9,... | collective-permute-start | bytes 172040 | tf_op jit(solution)/shard_map/ppermute | solution.py:719
  8.6 0.3 collective-permute-start.1
  8.9 2.9 %views.1 = (f32[2,768,128]{2,1,0:T(8,128)S(1)}, f32[2,768,128]{2,1,0:T(8,128)S(1)}) custom-call(s32[6]{0:T(128)S(1)} %copy-done.9, bf16[1,6,110592]{2,1,0:T(8,128)(2,1)} %observed.1), custom_call_target="tpu_custom_call" | custom-call | tf_op jit(solution)/shard_map/views/pallas_call | solution.py:690
  11.8 0.0 copy-start.2
  11.8 0.0 copy-start.7
  11.8 0.0 copy-start.8
  11.9 1.8 %collective-permute-done.2 = bf16[224,128]{1,0:T(8,128)(2,1)S(1)} collective-permute-done((bf16[224,128]{1,0:T(8,128)(2,1)S(1)}, bf16[224,128]{1,0:T(8,128)(2,1)S(1)}, u32[]{:S(2)}, u32[]{:S(2)}) %collective-permute-start.2) | collective-permute-done | bytes 57376 | tf_op jit(solution)/shard_map/ppermute | solution.py:719
  13.8 1.6 %collective-permute-start.3 = (bf16[576,128]{1,0:T(8,128)(2,1)S(1)}, bf16[576,128]{1,0:T(8,128)(2,1)S(1)}, u32[]{:S(2)}, u32[]{:S(2)}) collective-permute-start(bf16[576,128]{1,0:T(8,128)(2,1)S(1)} %constant_dynamic-update-slice_fusion), channel_id=1, source_target_pairs={{0,2},{1,3},{2,0},{3,1},{4,6},{5,7},{6,4},{7,5},{8,10},{9,11},{10,... | collective-permute-start | bytes 442376 | tf_op jit(solution)/shard_map/ppermute | solution.py:719
  15.4 1.2 %collective-permute-start.4 = (bf16[464,128]{1,0:T(8,128)(2,1)S(1)}, bf16[464,128]{1,0:T(8,128)(2,1)S(1)}, u32[]{:S(2)}, u32[]{:S(2)}) collective-permute-start(bf16[464,128]{1,0:T(8,128)(2,1)S(1)} %constant_dynamic-update-slice_fusion.5), channel_id=1, source_target_pairs={{0,8},{1,9},{2,10},{3,11},{4,12},{5,13},{6,14},{7,15},{8,0},{9,1},... | collective-permute-start | bytes 356360 | tf_op jit(solution)/shard_map/ppermute | solution.py:719
  16.6 0.8 %collective-permute-start.5 = (bf16[320,128]{1,0:T(8,128)(2,1)S(1)}, bf16[320,128]{1,0:T(8,128)(2,1)S(1)}, u32[]{:S(2)}, u32[]{:S(2)}) collective-permute-start(bf16[320,128]{1,0:T(8,128)(2,1)S(1)} %pad_maximum_fusion), channel_id=1, source_target_pairs={{0,10},{1,11},{2,8},{3,9},{4,14},{5,15},{6,12},{7,13},{8,2},{9,3},... | collective-permute-start | bytes 245768 | tf_op jit(solution)/shard_map/ppermute | solution.py:719
  17.4 2.8 %collective-permute-done.3 = bf16[576,128]{1,0:T(8,128)(2,1)S(1)} collective-permute-done((bf16[576,128]{1,0:T(8,128)(2,1)S(1)}, bf16[576,128]{1,0:T(8,128)(2,1)S(1)}, u32[]{:S(2)}, u32[]{:S(2)}) %collective-permute-start.3) | collective-permute-done | bytes 147488 | tf_op jit(solution)/shard_map/ppermute | solution.py:719
  20.2 0.6 %collective-permute-done.4 = bf16[464,128]{1,0:T(8,128)(2,1)S(1)} collective-permute-done((bf16[464,128]{1,0:T(8,128)(2,1)S(1)}, bf16[464,128]{1,0:T(8,128)(2,1)S(1)}, u32[]{:S(2)}, u32[]{:S(2)}) %collective-permute-start.4) | collective-permute-done | bytes 118816 | tf_op jit(solution)/shard_map/ppermute | solution.py:719
  20.8 0.0 copy-start
  20.8 0.0 copy-start.1
  20.8 0.0 copy-start.3
  20.9 0.0 copy-start.5
  20.9 0.0 copy-start.6
  20.9 1.0 %collective-permute-done.5 = bf16[320,128]{1,0:T(8,128)(2,1)S(1)} collective-permute-done((bf16[320,128]{1,0:T(8,128)(2,1)S(1)}, bf16[320,128]{1,0:T(8,128)(2,1)S(1)}, u32[]{:S(2)}, u32[]{:S(2)}) %collective-permute-start.5) | collective-permute-done | bytes 81952 | tf_op jit(solution)/shard_map/ppermute | solution.py:719
  22.0 0.1 collective-permute-start.6
  22.8 1.0 %collective-permute-done.6 = bf16[1568,128]{1,0:T(8,128)(2,1)S(1)} collective-permute-done((bf16[1568,128]{1,0:T(8,128)(2,1)S(1)}, bf16[1568,128]{1,0:T(8,128)(2,1)S(1)}, u32[]{:S(2)}, u32[]{:S(2)}) %collective-permute-start.6) | collective-permute-done | bytes 401440 | tf_op jit(solution)/shard_map/ppermute | solution.py:719
  23.9 2.0 %spectrum.2.refs_5_ = f32[16,128,128]{2,1,0:T(8,128)S(1)} custom-call(s32[6]{0:T(128)S(1)} %copy-done.9, s32[1,2,6]{2,1,0:T(2,128)S(1)} %bitcast.11, f32[1,2,6]{2,1,0:T(2,128)S(1)} %bitcast.13, s32[32]{0:T(128)S(1)} %copy-done.13, bf16[16,80,128]{2,1,0:T(8,128)(2,1)S(1)} %bitcast.9, bf16[16,80,128]{2,1,0:T(8,128)(2,1)S(1)} %bitcast.7, ...), custom_call_target="tpu_custom_call" | custom-call | tf_op jit(solution)/shard_map/spectrum/pallas_call | solution.py:690
  26.0 6.0 %first.1 = (f32[2,768,128]{2,1,0:T(8,128)S(1)}, bf16[256,128]{1,0:T(8,128)(2,1)S(1)}, bf16[144,128]{1,0:T(8,128)(2,1)S(1)}, bf16[144,128]{1,0:T(8,128)(2,1)S(1)}...) custom-call(s32[1]{0:T(128)S(6)} %copy.41.tissue, s32[1,6]{1,0:T(1,128)S(1)} %copy-done.12, ...), custom_call_target="tpu_custom_call" | custom-call | tf_op jit(solution)/shard_map/first/pallas_call | solution.py:690
  32.0 1.3 %collective-permute-start.7 = (bf16[256,128]{1,0:T(8,128)(2,1)S(1)}, bf16[256,128]{1,0:T(8,128)(2,1)S(1)}, u32[]{:S(2)}, u32[]{:S(2)}) collective-permute-start(bf16[256,128]{1,0:T(8,128)(2,1)S(1)} %get-tuple-element.59), channel_id=1, source_target_pairs={{0,2},{1,3},{2,0},{3,1},{4,6},{5,7},{6,4},{7,5},{8,10},{9,11},{10,... | collective-permute-start | bytes 196616 | tf_op jit(solution)/shard_map/ppermute | solution.py:719
  33.2 2.9 %collective-permute-start.8 = (bf16[144,128]{1,0:T(8,128)(2,1)S(1)}, bf16[144,128]{1,0:T(8,128)(2,1)S(1)}, u32[]{:S(2)}, u32[]{:S(2)}) collective-permute-start(bf16[144,128]{1,0:T(8,128)(2,1)S(1)} %get-tuple-element.60), channel_id=1, source_target_pairs={{0,16},{1,17},{2,18},{3,19},{4,20},{5,21},{6,22},{7,23},{8,24},{9,... | collective-permute-start | bytes 110600 | tf_op jit(solution)/shard_map/ppermute | solution.py:719
  36.1 1.0 %collective-permute-start.10 = (bf16[144,128]{1,0:T(8,128)(2,1)S(1)}, bf16[144,128]{1,0:T(8,128)(2,1)S(1)}, u32[]{:S(2)}, u32[]{:S(2)}) collective-permute-start(bf16[144,128]{1,0:T(8,128)(2,1)S(1)} %get-tuple-element.62), channel_id=1, source_target_pairs={{0,2},{1,8},{2,0},{3,10},{4,6},{5,12},{6,4},{7,14},{8,1},{9,11},{1... | collective-permute-start | bytes 110600 | tf_op jit(solution)/shard_map/ppermute | solution.py:725
  37.2 0.8 %collective-permute-start.11 = (bf16[144,128]{1,0:T(8,128)(2,1)S(1)}, bf16[144,128]{1,0:T(8,128)(2,1)S(1)}, u32[]{:S(2)}, u32[]{:S(2)}) collective-permute-start(bf16[144,128]{1,0:T(8,128)(2,1)S(1)} %get-tuple-element.63), channel_id=1, source_target_pairs={{0,1},{1,0},{2,3},{3,2},{4,5},{5,4},{6,7},{7,6},{8,9},{9,8},{10,11... | collective-permute-start | bytes 110600 | tf_op jit(solution)/shard_map/ppermute | solution.py:719
  38.0 2.0 %spectrum.3.refs_5_ = f32[16,128,128]{2,1,0:T(8,128)S(1)} custom-call(s32[6]{0:T(128)S(1)} %copy-done.9, s32[1,2,6]{2,1,0:T(2,128)S(1)} %bitcast.12, f32[1,2,6]{2,1,0:T(2,128)S(1)} %bitcast.14, s32[32]{0:T(128)S(1)} %copy-done.13, bf16[16,80,128]{2,1,0:T(8,128)(2,1)S(1)} %bitcast.10, bf16[16,80,128]{2,1,0:T(8,128)(2,1)S(1)} %bitcast.8, ...), custom_call_target="tpu_custom_call" | custom-call | tf_op jit(solution)/shard_map/spectrum/pallas_call | solution.py:690
  40.0 0.1 collective-permute-done.10.refs_3_
  40.1 6.6 %last.1 = f32[864,128]{1,0:T(8,128)} custom-call(s32[1]{0:T(128)S(6)} %copy.41.tissue, s32[1,6]{1,0:T(1,128)S(1)} %copy-done.12, f32[2,768,128]{2,1,0:T(8,128)S(1)} %get-tuple-element.58.u, bf16[256,128]{1,0:T(8,128)(2,1)S(1)} %collective-permute-done.7.refs_0_, bf16[144,128]{1,0:T(8,128)(2,1)S(1)} %collective-permute-done.8.refs_1_, ...), custom_call_target="tpu_custom_call" | custom-call | tf_op jit(solution)/shard_map/last/pallas_call | solution.py:690
  (46 shorter events, 0.4 us)
Async XLA Ops:
  0.0 0.7 %copy-start.9 = (s32[6]{0:T(128)S(1)}, s32[6]{0:T(128)}, u32[]{:S(2)}) copy-start(s32[6]{0:T(128)} %order.7) | copy-start | bytes 76
  3.2 8.7 %collective-permute-start = (bf16[224,128]{1,0:T(8,128)(2,1)S(1)}, bf16[224,128]{1,0:T(8,128)(2,1)S(1)}, u32[]{:S(2)}, u32[]{:S(2)}) collective-permute-start(bf16[224,128]{1,0:T(8,128)(2,1)S(1)} %get-tuple-element.96), channel_id=1, source_target_pairs={{0,16},{1,17},{2,18},{3,19},{4,20},{5,21},{6,22},{7,23},{8,24},{9,... | collective-permute-start | bytes 172040 | tf_op jit(solution)/shard_map/ppermute | solution.py:719
  7.3 6.4 %collective-permute-start.2 = (bf16[224,128]{1,0:T(8,128)(2,1)S(1)}, bf16[224,128]{1,0:T(8,128)(2,1)S(1)}, u32[]{:S(2)}, u32[]{:S(2)}) collective-permute-start(bf16[224,128]{1,0:T(8,128)(2,1)S(1)} %get-tuple-element.95), channel_id=1, source_target_pairs={{0,20},{1,21},{2,22},{3,23},{4,16},{5,17},{6,18},{7,19},{8,28},{9,... | collective-permute-start | bytes 172040 | tf_op jit(solution)/shard_map/ppermute | solution.py:719
  8.6 5.1 %collective-permute-start.1 = (bf16[80,128]{1,0:T(8,128)(2,1)S(1)}, bf16[80,128]{1,0:T(8,128)(2,1)S(1)}, u32[]{:S(2)}, u32[]{:S(2)}) collective-permute-start(bf16[80,128]{1,0:T(8,128)(2,1)S(1)} %get-tuple-element.44), channel_id=1, source_target_pairs={{0,4},{1,5},{2,6},{3,7},{4,0},{5,1},{6,2},{7,3},{8,12},{9,13},{10,... | collective-permute-start | bytes 61448 | tf_op jit(solution)/shard_map/ppermute | solution.py:719
  11.8 12.0 %copy-start.2 = (f32[2,17,8,128]{3,2,1,0:T(8,128)S(1)}, f32[2,17,8,128]{3,2,1,0:T(8,128)}, u32[]{:S(2)}) copy-start(f32[2,17,8,128]{3,2,1,0:T(8,128)} %constant.25.clone.turns) | copy-start | bytes 417796
  11.8 12.0 %copy-start.7 = (bf16[128,256]{1,0:T(8,128)(2,1)S(1)}, bf16[128,256]{1,0:T(8,128)(2,1)}, u32[]{:S(2)}) copy-start(bf16[128,256]{1,0:T(8,128)(2,1)} %constant.24.clone.table) | copy-start | bytes 196612
  11.8 12.0 %copy-start.8 = (bf16[128,144]{1,0:T(8,128)(2,1)S(1)}, bf16[128,144]{1,0:T(8,128)(2,1)}, u32[]{:S(2)}) copy-start(bf16[128,144]{1,0:T(8,128)(2,1)} %constant.23.clone.table_y_ref) | copy-start | bytes 110596
  11.8 12.0 %copy-start.10 = (s32[1,6,2]{1,2,0:T(2,128)S(1)}, s32[1,6,2]{1,2,0:T(2,128)}, u32[]{:S(2)}) copy-start(s32[1,6,2]{1,2,0:T(2,128)} %param.23) | copy-start | bytes 148
  11.8 12.0 %copy-start.11 = (f32[1,6,2]{1,2,0:T(2,128)S(1)}, f32[1,6,2]{1,2,0:T(2,128)}, u32[]{:S(2)}) copy-start(f32[1,6,2]{1,2,0:T(2,128)} %param.24) | copy-start | bytes 148
  11.9 12.0 %copy-start.13 = (s32[32]{0:T(128)S(1)}, s32[32]{0:T(128)}, u32[]{:S(2)}) copy-start(s32[32]{0:T(128)} %cell_row.3) | copy-start | bytes 388
  13.8 6.3 %collective-permute-start.3 = (bf16[576,128]{1,0:T(8,128)(2,1)S(1)}, bf16[576,128]{1,0:T(8,128)(2,1)S(1)}, u32[]{:S(2)}, u32[]{:S(2)}) collective-permute-start(bf16[576,128]{1,0:T(8,128)(2,1)S(1)} %constant_dynamic-update-slice_fusion), channel_id=1, source_target_pairs={{0,2},{1,3},{2,0},{3,1},{4,6},{5,7},{6,4},{7,5},{8,10},{9,11},{10,... | collective-permute-start | bytes 442376 | tf_op jit(solution)/shard_map/ppermute | solution.py:719
  15.4 5.4 %collective-permute-start.4 = (bf16[464,128]{1,0:T(8,128)(2,1)S(1)}, bf16[464,128]{1,0:T(8,128)(2,1)S(1)}, u32[]{:S(2)}, u32[]{:S(2)}) collective-permute-start(bf16[464,128]{1,0:T(8,128)(2,1)S(1)} %constant_dynamic-update-slice_fusion.5), channel_id=1, source_target_pairs={{0,8},{1,9},{2,10},{3,11},{4,12},{5,13},{6,14},{7,15},{8,0},{9,1},... | collective-permute-start | bytes 356360 | tf_op jit(solution)/shard_map/ppermute | solution.py:719
  16.6 5.3 %collective-permute-start.5 = (bf16[320,128]{1,0:T(8,128)(2,1)S(1)}, bf16[320,128]{1,0:T(8,128)(2,1)S(1)}, u32[]{:S(2)}, u32[]{:S(2)}) collective-permute-start(bf16[320,128]{1,0:T(8,128)(2,1)S(1)} %pad_maximum_fusion), channel_id=1, source_target_pairs={{0,10},{1,11},{2,8},{3,9},{4,14},{5,15},{6,12},{7,13},{8,2},{9,3},... | collective-permute-start | bytes 245768 | tf_op jit(solution)/shard_map/ppermute | solution.py:719
  20.8 5.1 %copy-start = (bf16[768,256]{1,0:T(8,128)(2,1)S(1)}, bf16[768,256]{1,0:T(8,128)(2,1)}, u32[]{:S(2)}) copy-start(bf16[768,256]{1,0:T(8,128)(2,1)} %constant.18.clone.refs_7_) | copy-start | bytes 1179652
  20.8 5.1 %copy-start.1 = (bf16[768,256]{1,0:T(8,128)(2,1)S(1)}, bf16[768,256]{1,0:T(8,128)(2,1)}, u32[]{:S(2)}) copy-start(bf16[768,256]{1,0:T(8,128)(2,1)} %constant.19.clone.refs_9_) | copy-start | bytes 1179652
  20.8 5.1 %copy-start.3 = (f32[2,16,8,128]{3,2,1,0:T(8,128)S(1)}, f32[2,16,8,128]{3,2,1,0:T(8,128)}, u32[]{:S(2)}) copy-start(f32[2,16,8,128]{3,2,1,0:T(8,128)} %constant.26.clone.refs_12_) | copy-start | bytes 393220
  20.8 5.1 %copy-start.4 = (bf16[128,384]{1,0:T(8,128)(2,1)S(1)}, bf16[128,384]{1,0:T(8,128)(2,1)}, u32[]{:S(2)}) copy-start(bf16[128,384]{1,0:T(8,128)(2,1)} %constant.20.clone.refs_8_) | copy-start | bytes 294916
  20.9 5.1 %copy-start.5 = (bf16[128,288]{1,0:T(8,128)(2,1)S(1)}, bf16[128,288]{1,0:T(8,128)(2,1)}, u32[]{:S(2)}) copy-start(bf16[128,288]{1,0:T(8,128)(2,1)} %constant.21.clone.refs_10_) | copy-start | bytes 221188
  20.9 5.1 %copy-start.6 = (bf16[96,384]{1,0:T(8,128)(2,1)S(1)}, bf16[96,384]{1,0:T(8,128)(2,1)}, u32[]{:S(2)}) copy-start(bf16[96,384]{1,0:T(8,128)(2,1)} %constant.22.clone.refs_11_) | copy-start | bytes 221188
  20.9 5.1 %copy-start.12 = (s32[1,6]{1,0:T(1,128)S(1)}, s32[1,6]{1,0:T(1,128)}, u32[]{:S(2)}) copy-start(s32[1,6]{1,0:T(1,128)} %present.3) | copy-start | bytes 76
  22.0 1.8 %collective-permute-start.6 = (bf16[1568,128]{1,0:T(8,128)(2,1)S(1)}, bf16[1568,128]{1,0:T(8,128)(2,1)S(1)}, u32[]{:S(2)}, u32[]{:S(2)}) collective-permute-start(bf16[1568,128]{1,0:T(8,128)(2,1)S(1)} %constant_dynamic-update-slice_fusion.15), channel_id=1, source_target_pairs={{0,1},{1,0},{2,3},{3,2},{4,5},{5,4},{6,7},{7,6},{8,9},{9,8},{10,11... | collective-permute-start | bytes 1204232 | tf_op jit(solution)/shard_map/ppermute | solution.py:719
  32.0 8.1 %collective-permute-start.7 = (bf16[256,128]{1,0:T(8,128)(2,1)S(1)}, bf16[256,128]{1,0:T(8,128)(2,1)S(1)}, u32[]{:S(2)}, u32[]{:S(2)}) collective-permute-start(bf16[256,128]{1,0:T(8,128)(2,1)S(1)} %get-tuple-element.59), channel_id=1, source_target_pairs={{0,2},{1,3},{2,0},{3,1},{4,6},{5,7},{6,4},{7,5},{8,10},{9,11},{10,... | collective-permute-start | bytes 196616 | tf_op jit(solution)/shard_map/ppermute | solution.py:719
  33.2 6.8 %collective-permute-start.8 = (bf16[144,128]{1,0:T(8,128)(2,1)S(1)}, bf16[144,128]{1,0:T(8,128)(2,1)S(1)}, u32[]{:S(2)}, u32[]{:S(2)}) collective-permute-start(bf16[144,128]{1,0:T(8,128)(2,1)S(1)} %get-tuple-element.60), channel_id=1, source_target_pairs={{0,16},{1,17},{2,18},{3,19},{4,20},{5,21},{6,22},{7,23},{8,24},{9,... | collective-permute-start | bytes 110600 | tf_op jit(solution)/shard_map/ppermute | solution.py:719
  36.1 3.9 %collective-permute-start.9 = (bf16[144,128]{1,0:T(8,128)(2,1)S(1)}, bf16[144,128]{1,0:T(8,128)(2,1)S(1)}, u32[]{:S(2)}, u32[]{:S(2)}) collective-permute-start(bf16[144,128]{1,0:T(8,128)(2,1)S(1)} %get-tuple-element.61), channel_id=1, source_target_pairs={{0,1},{1,0},{2,3},{3,2},{4,16},{5,17},{6,18},{7,19},{8,9},{9,8},{1... | collective-permute-start | bytes 110600 | tf_op jit(solution)/shard_map/ppermute | solution.py:725
  36.1 4.0 %collective-permute-start.10 = (bf16[144,128]{1,0:T(8,128)(2,1)S(1)}, bf16[144,128]{1,0:T(8,128)(2,1)S(1)}, u32[]{:S(2)}, u32[]{:S(2)}) collective-permute-start(bf16[144,128]{1,0:T(8,128)(2,1)S(1)} %get-tuple-element.62), channel_id=1, source_target_pairs={{0,2},{1,8},{2,0},{3,10},{4,6},{5,12},{6,4},{7,14},{8,1},{9,11},{1... | collective-permute-start | bytes 110600 | tf_op jit(solution)/shard_map/ppermute | solution.py:725
  37.2 2.9 %collective-permute-start.11 = (bf16[144,128]{1,0:T(8,128)(2,1)S(1)}, bf16[144,128]{1,0:T(8,128)(2,1)S(1)}, u32[]{:S(2)}, u32[]{:S(2)}) collective-permute-start(bf16[144,128]{1,0:T(8,128)(2,1)S(1)} %get-tuple-element.63), channel_id=1, source_target_pairs={{0,1},{1,0},{2,3},{3,2},{4,5},{5,4},{6,7},{7,6},{8,9},{9,8},{10,11... | collective-permute-start | bytes 110600 | tf_op jit(solution)/shard_map/ppermute | solution.py:719

commit v6 on v5

--- a/solution.py
+++ b/solution.py
@@ -265,12 +265,11 @@
 
 
 def sort_margins(present, odd, axis, pair):
-    on = [present[0, 2 * axis + side] >= 0 for side in range(2)]
+    on = jnp.where(present[...] >= 0, 1.0, 0.0)
     pair = [value.astype(F32) for value in pair]
     low = jnp.where(odd, pair[0], pair[1])
     high = jnp.where(odd, pair[1], pair[0])
-    zero = jnp.zeros_like(low)
-    return jnp.where(on[0], low, zero), jnp.where(on[1], high, zero)
+    return low * on[:, 2 * axis : 2 * axis + 1], high * on[:, 2 * axis + 1 : 2 * axis + 2]
 
 
 def assemble(present, odds, rows_ref, margins, high_ref, low_ref):
@@ -484,22 +483,27 @@
     return place
 
 
-def spectrum_kernel(update, count, order, lists, blend, cell_row, near, far, table, turns, table_y_ref, out_ref, flat, lines, spread, planes):
-    view = order[update]
+def spectrum_kernel(update, count, order, lists, blend, cell_row, near, far, table, turns, table_y_ref, out_ref, flat, tap_lines, spread, planes):
     own = lax.axis_index("blk")
     half = count // 2
-    total = blend[0, 0, view] + blend[0, 1, view]
-    value = None
+    view = order[:, update : update + 1]
+    chosen = jnp.where(lax.broadcasted_iota(jnp.int32, (1, VIEWS), 1) == view, 1.0, 0.0)
+    numbers = lax.broadcasted_iota(jnp.int32, (1, count), 1)
     rows = slice(CELLROWS * update, CELLROWS * (update + 1))
+    lines, weights = [], []
     for k in range(2):
-        place = gathered_place(count, cell_row[lists[0, k, view]] ^ own)
+        listed = jnp.sum(lists[0, k : k + 1, :].astype(F32) * chosen, axis=1, keepdims=True)
+        owners = jnp.where(numbers == listed.astype(jnp.int32), cell_row[...].astype(F32), 0.0)
+        place = gathered_place(count, jnp.sum(owners).astype(jnp.int32) ^ own)
         inner = lax.rem(place, half)
         line = jnp.where(place < half, near[inner].astype(F32), far[inner].astype(F32))[rows]
-        weight = blend[0, k, view] / total * (2.0 / float(PAD**3))
-        part = line * (weight / jnp.sum(line))
-        value = part if value is None else value + part
+        lines.append(line)
+        weights.append(jnp.sum(blend[0, k : k + 1, :] * chosen, axis=1, keepdims=True))
+    total = (weights[0] + weights[1]) * (float(PAD**3) / 2.0)
+    value = lines[0] * (weights[0] / (total * jnp.sum(lines[0], keepdims=True)))
+    value = value + lines[1] * (weights[1] / (total * jnp.sum(lines[1], keepdims=True)))
     flat[...] = value
-    tap_stage(flat, lines, spread, table, turns, table_y_ref, planes)
+    tap_stage(flat, tap_lines, spread, table, turns, table_y_ref, planes)
     z_stage(planes, out_ref)
 
 
@@ -527,9 +531,6 @@
     if axes[1]:
         found[1 << axes[1][0]] = (1, 0)
     found[1 << axes[2][0]] = (2, 0)
-    for axis in (1, 2):
-        if len(axes[axis]) == 2:
-            found[1 << axes[axis][0] | 1 << axes[axis][1]] = (axis, 1)
     if len(axes[0]) == 2:
         found[1 << axes[0][1]] = (0, 1)
     return found
@@ -553,30 +554,36 @@
 
 
 def start_kernel(count, order, cells, est, u_out, cells_out, *refs):
-    outs, (got, pad, flat, sems) = refs[:-4], refs[-4:]
-    loading = pltpu.make_async_copy(est, flat, sems.at[UPDATES])
-    loading.start()
+    outs, (view, got, pad, flat, sems) = refs[:-5], refs[-5:]
     copies = []
-    for update in range(UPDATES):
-        copies.append(pltpu.make_async_copy(cells.at[order[update]], got.at[update], sems.at[update]))
+    for number, (source, target) in enumerate(((est, flat), (cells, got), (order, view))):
+        copies.append(pltpu.make_async_copy(source, target, sems.at[number]))
         copies[-1].start()
+    copies[0].wait()
+    unflatten(lambda row: flat[pl.ds(row, 8, stride=3), :], u_out)
+    store_slabs(count, pack_slabs(u_out), outs)
+    copies[1].wait()
+    copies[2].wait()
     pad[...] = jnp.zeros((1, CELLROWS * 128), F32)
     for update in range(UPDATES):
-        copies[update].wait()
-        pad[:, 0:KS3] = got[update]
+        now = view[:, update : update + 1]
+        value = None
+        for number in range(VIEWS):
+            part = got[number] * jnp.where(now == number, 1.0, 0.0)
+            value = part if value is None else value + part
+        pad[:, 0:KS3] = value
         wide = pad[...]
         rows = [wide[:, 128 * row : 128 * (row + 1)] for row in range(CELLROWS)]
         here = slice(CELLROWS * update, CELLROWS * (update + 1))
         cells_out[here, :] = jnp.concatenate(rows, axis=0).astype(BF16)
-    loading.wait()
-    unflatten(lambda row: flat[pl.ds(row, 8, stride=3), :], u_out)
-    store_slabs(count, pack_slabs(u_out), outs)
 
 
 VIEW_PARTS = 9
 
 
-def views_kernel(order, observed, o0, o1, near, wide, sems):
+def views_kernel(order, observed, o0, o1, held, near, wide, sems):
+    asked = pltpu.make_async_copy(order, held, sems.at[VIEW_PARTS])
+    asked.start()
     part_rows = FLAT // VIEW_PARTS
     copies = []
     for part in range(VIEW_PARTS):
@@ -597,8 +604,9 @@
                 rows = pl.ds(pl.multiple_of((first + row) * 8, 8), 8)
                 wide[rows, :] = value[:, 128 * row : 128 * (row + 1)]
 
+    asked.wait()
     for update, out in enumerate((o0, o1)):
-        view = order[update]
+        view = jnp.sum(held[:, update : update + 1].astype(F32)).astype(jnp.int32)
         unflatten(lambda row: wide[pl.ds(8 * row + view, 8, stride=24), :], out)
 
 
@@ -635,7 +643,7 @@
     y_stage(lines, gh, E, planes)
     filter_stage(planes, kernel, twiddle, True, planes)
     y_back_stage(planes, gb, lines)
-    alive = tissue[0] > 0
+    alive = jnp.broadcast_to(tissue[...], (STEP, 128)) > 0
     for start in range(0, SLOTS * E, STEP):
         rows = slice(start, start + STEP)
         correction = dot(wide_terms(lines[rows, :]), ei[...])
@@ -747,30 +755,35 @@
     slab_shapes = [SLABS[axis] for axis, far in slab_kinds(count)]
     rows, cells, *slabs = call(
         functools.partial(start_kernel, count),
-        [SM, HBM, HBM],
+        [HBM, HBM, HBM],
         [ROWS, CELLS] + slab_shapes,
         (
-            view_order,
+            pltpu.with_memory_space_constraint(view_order.reshape(1, VIEWS), pltpu.HBM),
             pltpu.with_memory_space_constraint(jnp.swapaxes(psf_cells, 0, 1), pltpu.HBM),
             pltpu.with_memory_space_constraint(estimate.reshape(FLAT, 128), pltpu.HBM),
         ),
         [
-            pltpu.VMEM((UPDATES, 1, KS3), F32),
+            pltpu.VMEM((1, VIEWS), jnp.int32),
+            pltpu.VMEM((VIEWS, 1, KS3), F32),
             pltpu.VMEM((1, CELLROWS * 128), F32),
             pltpu.VMEM((FLAT, 128), F32),
-            pltpu.SemaphoreType.DMA((UPDATES + 1,)),
+            pltpu.SemaphoreType.DMA((3,)),
         ],
         name="start",
     )
     targets = call(
         views_kernel,
-        [SM, HBM],
+        [HBM, HBM],
         [ROWS, ROWS],
-        (view_order, pltpu.with_memory_space_constraint(observed, pltpu.HBM)),
+        (
+            pltpu.with_memory_space_constraint(view_order.reshape(1, VIEWS), pltpu.HBM),
+            pltpu.with_memory_space_constraint(observed, pltpu.HBM),
+        ),
         [
+            pltpu.VMEM((1, VIEWS), jnp.int32),
             pltpu.VMEM((1, VIEWS, FLAT * 128), BF16),
             pltpu.VMEM((8 * FLAT, 128), F32),
-            pltpu.SemaphoreType.DMA((VIEW_PARTS,)),
+            pltpu.SemaphoreType.DMA((VIEW_PARTS + 1,)),
         ],
         name="views",
     )
@@ -796,22 +809,24 @@
             if distance == 1 and (0, 1) in margins:
                 margins[0, 1] = got[got.shape[0] - SLAB.shape[0] :]
         if number == 0:
-            arrived, targets = lax.optimization_barrier((arrived, targets))
+            sides = {kind: slab for kind, slab in slabs.items() if kind not in riding.values()}
+            arrived, targets, sides = lax.optimization_barrier((arrived, targets, sides))
+        if number == 1:
+            sides = {kind: swap_slab(kind, slab, count) for kind, slab in sides.items()}
+            arrived, sides = lax.optimization_barrier((arrived, sides))
+            margins.update(sides)
         if bits != [0]:
             held = jnp.concatenate(arrived, axis=0)
     other = arrived[1]
-    for kind in slab_kinds(count):
-        if kind not in margins:
-            margins[kind] = swap_slab(kind, slabs[kind], count)
     margins = [margins[kind] for kind in slab_kinds(count)]
     near_cells, far_cells = [v.reshape(count // 2, UPDATES * CELLROWS, 128) for v in (held, other)]
 
     def spectrum(update):
         return call(
             functools.partial(spectrum_kernel, update, count),
-            [SM] * 4 + [VM] * 5,
+            [VM] * 9,
             PLANES,
-            (view_order, lists, blend, cell_row, near_cells, far_cells, taps, turns, gt),
+            (view_order.reshape(1, VIEWS), lists, blend, cell_row.reshape(1, count), near_cells, far_cells, taps, turns, gt),
             [
                 pltpu.VMEM((CELLROWS, 128), F32),
                 pltpu.VMEM((3, TAPS, 128), F32),
@@ -824,9 +839,9 @@
     def update(body, outs, number, kernel, rows, margins, scratch, name):
         return call(
             functools.partial(body, count),
-            [SM] * 2 + [VM] * (9 + len(slab_shapes)),
+            [VM] * (11 + len(slab_shapes)),
             outs,
-            (tissue, neighbours, rows, *margins, kernel, targets[number], ea, gy, ei, gh, gb, twiddle),
+            (tissue.reshape(1, 1), neighbours, rows, *margins, kernel, targets[number], ea, gy, ei, gh, gb, twiddle),
             [PLANES_V, TERMS_V, TERMS_V, LINES_V] + scratch,
             name=name,
         )

time: 46.9 us -> 44.3 us (0.945)
  Pallas kernels: 22 us -> 19.7 us
  waiting for transfers between devices: 7.31 us -> 9.06 us
  starting transfers between devices: 15.3 us -> 14 us
  local copies, waits for them, and re-layouts: 1.01 us -> 0.3 us
    pallas_call x6, Pallas kernels: 22 us -> 19.7 us  [call(): pl.pallas_call(body, in_specs=ins, out_specs=[VM] * len(outs) if many els...]
    ppermute x10, waiting for transfers between devices: 7.23 us -> 8.69 us  [swap(): lax.ppermute(value, 'blk', [(number, number ^ distance) for number in ran...]
    ppermute x10, starting transfers between devices: 14.3 us -> 12.9 us  [swap(): lax.ppermute(value, 'blk', [(number, number ^ distance) for number in ran...]
    unnamed x36 -> x37, local copies, waits for them, and re-layouts: 0.92 us -> 0.21 us
    ppermute x2 -> x3, starting transfers between devices: 1.02 us -> 1.06 us  [swap_slab(): return lax.ppermute(slab, 'blk', far_pairs(count, axis))]
  transfers between devices with their start and end apart: 12 -> 13, of which waited for: 6 -> 5; matrix products, arithmetic and copies ran while one was open for 0% -> 0% of each run, Pallas kernels for 11% -> 9%
where the time goes in v6:
time: 44.3 us; the launch traced here: 44.2 us
  Pallas kernels  19.7 us (44%)
  starting transfers between devices  14 us (32%)
  waiting for transfers between devices  9.06 us (20%)
  between operations  1.07 us (2%)
    pallas_call x6, Pallas kernels, call(): pl.pallas_call(body, in_specs=ins, out_specs=[VM] * len(outs) if many els...  19.7 us
    ppermute x10, starting transfers between devices, swap(): lax.ppermute(value, 'blk', [(number, number ^ distance) for number in ran...  12.9 us
    ppermute x10, waiting for transfers between devices, swap(): lax.ppermute(value, 'blk', [(number, number ^ distance) for number in ran...  8.69 us
    ppermute x3, starting transfers between devices, swap_slab(): return lax.ppermute(slab, 'blk', far_pairs(count, axis))  1.06 us
  transfers between devices with their start and end apart: 13, of which 5 were waited for; matrix products, arithmetic and copies ran while one was open for 0% of the time, Pallas kernels for 9%

profile of v6, /device:TPU:0, one launch (start us, length us, event | category | flops | bytes accessed | tf_op | source)
XLA Modules:
  0.0 44.2 jit_solution(4306597468363151900)
XLA Ops:
  0.0 2.1 %start.1 = (f32[2,768,128]{2,1,0:T(8,128)S(1)}, bf16[80,128]{1,0:T(8,128)(2,1)S(1)}, bf16[256,128]{1,0:T(8,128)(2,1)S(1)}, bf16[144,128]{1,0:T(8,128)(2,1)S(1)},...) custom-call(s32[1,6]{1,0:T(1,128)} %bitcast.16, f32[6,1,4913]{2,1,0:T(1,128)} %bitcast.27, ...), custom_call_target="tpu_custom_call" | custom-call | tf_op jit(solution)/shard_map/start/pallas_call | solution.py:698
  2.1 4.1 %collective-permute-start = (bf16[224,128]{1,0:T(8,128)(2,1)S(1)}, bf16[224,128]{1,0:T(8,128)(2,1)S(1)}, u32[]{:S(2)}, u32[]{:S(2)}) collective-permute-start(bf16[224,128]{1,0:T(8,128)(2,1)S(1)} %pad_maximum_fusion.1), channel_id=1, source_target_pairs={{0,16},{1,17},{2,18},{3,19},{4,20},{5,21},{6,22},{7,23},{8,24},{9,... | collective-permute-start | bytes 172040 | tf_op jit(solution)/shard_map/ppermute | solution.py:727
  6.2 1.5 %collective-permute-start.1 = (bf16[80,128]{1,0:T(8,128)(2,1)S(1)}, bf16[80,128]{1,0:T(8,128)(2,1)S(1)}, u32[]{:S(2)}, u32[]{:S(2)}) collective-permute-start(bf16[80,128]{1,0:T(8,128)(2,1)S(1)} %get-tuple-element.50), channel_id=1, source_target_pairs={{0,4},{1,5},{2,6},{3,7},{4,0},{5,1},{6,2},{7,3},{8,12},{9,13},{10,... | collective-permute-start | bytes 61448 | tf_op jit(solution)/shard_map/ppermute | solution.py:727
  7.8 0.0 collective-permute-start.2
  7.8 2.6 %views.1 = (f32[2,768,128]{2,1,0:T(8,128)S(1)}, f32[2,768,128]{2,1,0:T(8,128)S(1)}) custom-call(s32[1,6]{1,0:T(1,128)} %bitcast.17, bf16[1,6,110592]{2,1,0:T(8,128)(2,1)} %observed.1), custom_call_target="tpu_custom_call" | custom-call | tf_op jit(solution)/shard_map/views/pallas_call | solution.py:698
  10.3 0.0 copy-start.2
  10.3 0.0 copy-start.7
  10.4 0.0 copy-start.8
  10.4 0.0 copy-start.11
  10.5 2.9 %collective-permute-done.2 = bf16[80,128]{1,0:T(8,128)(2,1)S(1)} collective-permute-done((bf16[80,128]{1,0:T(8,128)(2,1)S(1)}, bf16[80,128]{1,0:T(8,128)(2,1)S(1)}, u32[]{:S(2)}, u32[]{:S(2)}) %collective-permute-start.2) | collective-permute-done | bytes 20512 | tf_op jit(solution)/shard_map/ppermute | solution.py:727
  13.4 1.6 %collective-permute-start.3 = (bf16[576,128]{1,0:T(8,128)(2,1)S(1)}, bf16[576,128]{1,0:T(8,128)(2,1)S(1)}, u32[]{:S(2)}, u32[]{:S(2)}) collective-permute-start(bf16[576,128]{1,0:T(8,128)(2,1)S(1)} %constant_dynamic-update-slice_fusion.4), channel_id=1, source_target_pairs={{0,2},{1,3},{2,0},{3,1},{4,6},{5,7},{6,4},{7,5},{8,10},{9,11},{10,... | collective-permute-start | bytes 442376 | tf_op jit(solution)/shard_map/ppermute | solution.py:727
  15.0 1.6 %collective-permute-start.4 = (bf16[464,128]{1,0:T(8,128)(2,1)S(1)}, bf16[464,128]{1,0:T(8,128)(2,1)S(1)}, u32[]{:S(2)}, u32[]{:S(2)}) collective-permute-start(bf16[464,128]{1,0:T(8,128)(2,1)S(1)} %constant_dynamic-update-slice_fusion.9), channel_id=1, source_target_pairs={{0,8},{1,9},{2,10},{3,11},{4,12},{5,13},{6,14},{7,15},{8,0},{9,1},... | collective-permute-start | bytes 356360 | tf_op jit(solution)/shard_map/ppermute | solution.py:727
  16.6 0.4 collective-permute-start.5
  17.0 2.8 %collective-permute-done.4 = bf16[464,128]{1,0:T(8,128)(2,1)S(1)} collective-permute-done((bf16[464,128]{1,0:T(8,128)(2,1)S(1)}, bf16[464,128]{1,0:T(8,128)(2,1)S(1)}, u32[]{:S(2)}, u32[]{:S(2)}) %collective-permute-start.4) | collective-permute-done | bytes 118816 | tf_op jit(solution)/shard_map/ppermute | solution.py:727
  19.9 2.0 %collective-permute-done.5 = bf16[320,128]{1,0:T(8,128)(2,1)S(1)} collective-permute-done((bf16[320,128]{1,0:T(8,128)(2,1)S(1)}, bf16[320,128]{1,0:T(8,128)(2,1)S(1)}, u32[]{:S(2)}, u32[]{:S(2)}) %collective-permute-start.5) | collective-permute-done | bytes 81952 | tf_op jit(solution)/shard_map/ppermute | solution.py:727
  22.0 0.1 collective-permute-start.7
  22.7 0.0 copy-start
  22.7 0.0 copy-start.1
  22.8 0.0 copy-start.3
  22.8 0.0 copy-start.4
  22.8 0.0 copy-start.5
  22.8 0.0 copy-start.6
  22.9 0.9 %collective-permute-done.7 = bf16[1568,128]{1,0:T(8,128)(2,1)S(1)} collective-permute-done((bf16[1568,128]{1,0:T(8,128)(2,1)S(1)}, bf16[1568,128]{1,0:T(8,128)(2,1)S(1)}, u32[]{:S(2)}, u32[]{:S(2)}) %collective-permute-start.7) | collective-permute-done | bytes 401440 | tf_op jit(solution)/shard_map/ppermute | solution.py:727
  23.9 1.6 %spectrum.2.refs_5_ = f32[16,128,128]{2,1,0:T(8,128)S(1)} custom-call(s32[1,6]{1,0:T(1,128)S(1)} %bitcast.18, s32[1,2,6]{2,1,0:T(2,128)S(1)} %bitcast.20, f32[1,2,6]{2,1,0:T(2,128)S(1)} %bitcast.22, s32[1,32]{1,0:T(1,128)S(1)} %bitcast.24, bf16[16,80,128]{2,1,0:T(8,128)(2,1)S(1)} %bitcast.12, bf16[16,80,128]{2,1,0:T(8,128)(2,1)S(1)} %bitcast.14, ...), custom_call_target="tpu_custom_call" | custom-call | tf_op jit(solution)/shard_map/spectrum/pallas_call | solution.py:698
  25.6 5.7 %first.1 = (f32[2,768,128]{2,1,0:T(8,128)S(1)}, bf16[256,128]{1,0:T(8,128)(2,1)S(1)}, bf16[144,128]{1,0:T(8,128)(2,1)S(1)}, bf16[144,128]{1,0:T(8,128)(2,1)S(1)}...) custom-call(s32[1,1]{1,0:T(1,128)} %bitcast.10.tissue, s32[1,6]{1,0:T(1,128)S(1)} %copy-done.12, ...), custom_call_target="tpu_custom_call" | custom-call | tf_op jit(solution)/shard_map/first/pallas_call | solution.py:698
  31.3 0.6 %collective-permute-start.8 = (bf16[256,128]{1,0:T(8,128)(2,1)S(1)}, bf16[256,128]{1,0:T(8,128)(2,1)S(1)}, u32[]{:S(2)}, u32[]{:S(2)}) collective-permute-start(bf16[256,128]{1,0:T(8,128)(2,1)S(1)} %get-tuple-element.71), channel_id=1, source_target_pairs={{0,2},{1,3},{2,0},{3,1},{4,6},{5,7},{6,4},{7,5},{8,10},{9,11},{10,... | collective-permute-start | bytes 196616 | tf_op jit(solution)/shard_map/ppermute | solution.py:727
  31.9 2.2 %collective-permute-start.9 = (bf16[144,128]{1,0:T(8,128)(2,1)S(1)}, bf16[144,128]{1,0:T(8,128)(2,1)S(1)}, u32[]{:S(2)}, u32[]{:S(2)}) collective-permute-start(bf16[144,128]{1,0:T(8,128)(2,1)S(1)} %get-tuple-element.72), channel_id=1, source_target_pairs={{0,16},{1,17},{2,18},{3,19},{4,20},{5,21},{6,22},{7,23},{8,24},{9,... | collective-permute-start | bytes 110600 | tf_op jit(solution)/shard_map/ppermute | solution.py:727
  34.0 1.1 %collective-permute-start.11 = (bf16[144,128]{1,0:T(8,128)(2,1)S(1)}, bf16[144,128]{1,0:T(8,128)(2,1)S(1)}, u32[]{:S(2)}, u32[]{:S(2)}) collective-permute-start(bf16[144,128]{1,0:T(8,128)(2,1)S(1)} %get-tuple-element.74), channel_id=1, source_target_pairs={{0,2},{1,8},{2,0},{3,10},{4,6},{5,12},{6,4},{7,14},{8,1},{9,11},{1... | collective-permute-start | bytes 110600 | tf_op jit(solution)/shard_map/ppermute | solution.py:733
  35.1 0.9 %collective-permute-start.12 = (bf16[144,128]{1,0:T(8,128)(2,1)S(1)}, bf16[144,128]{1,0:T(8,128)(2,1)S(1)}, u32[]{:S(2)}, u32[]{:S(2)}) collective-permute-start(bf16[144,128]{1,0:T(8,128)(2,1)S(1)} %get-tuple-element.75), channel_id=1, source_target_pairs={{0,1},{1,0},{2,3},{3,2},{4,5},{5,4},{6,7},{7,6},{8,9},{9,8},{10,11... | collective-permute-start | bytes 110600 | tf_op jit(solution)/shard_map/ppermute | solution.py:727
  36.0 1.6 %spectrum.3.refs_5_ = f32[16,128,128]{2,1,0:T(8,128)S(1)} custom-call(s32[1,6]{1,0:T(1,128)S(1)} %bitcast.19, s32[1,2,6]{2,1,0:T(2,128)S(1)} %bitcast.21, f32[1,2,6]{2,1,0:T(2,128)S(1)} %bitcast.23, s32[1,32]{1,0:T(1,128)S(1)} %bitcast.25, bf16[16,80,128]{2,1,0:T(8,128)(2,1)S(1)} %bitcast.13, bf16[16,80,128]{2,1,0:T(8,128)(2,1)S(1)} %bitcast.15, ...), custom_call_target="tpu_custom_call" | custom-call | tf_op jit(solution)/shard_map/spectrum/pallas_call | solution.py:698
  37.6 0.4 collective-permute-done.11.refs_3_
  38.0 6.2 %last.1 = f32[864,128]{1,0:T(8,128)} custom-call(s32[1,1]{1,0:T(1,128)} %bitcast.11.tissue, s32[1,6]{1,0:T(1,128)S(1)} %copy-done.12, f32[2,768,128]{2,1,0:T(8,128)S(1)} %get-tuple-element.70.u, bf16[256,128]{1,0:T(8,128)(2,1)S(1)} %collective-permute-done.8.refs_0_, bf16[144,128]{1,0:T(8,128)(2,1)S(1)} %collective-permute-done.9.refs_1_, ...), custom_call_target="tpu_custom_call" | custom-call | tf_op jit(solution)/shard_map/last/pallas_call | solution.py:698
  (49 shorter events, 0.3 us)
Async XLA Ops:
  2.1 8.3 %collective-permute-start = (bf16[224,128]{1,0:T(8,128)(2,1)S(1)}, bf16[224,128]{1,0:T(8,128)(2,1)S(1)}, u32[]{:S(2)}, u32[]{:S(2)}) collective-permute-start(bf16[224,128]{1,0:T(8,128)(2,1)S(1)} %pad_maximum_fusion.1), channel_id=1, source_target_pairs={{0,16},{1,17},{2,18},{3,19},{4,20},{5,21},{6,22},{7,23},{8,24},{9,... | collective-permute-start | bytes 172040 | tf_op jit(solution)/shard_map/ppermute | solution.py:727
  6.2 4.2 %collective-permute-start.1 = (bf16[80,128]{1,0:T(8,128)(2,1)S(1)}, bf16[80,128]{1,0:T(8,128)(2,1)S(1)}, u32[]{:S(2)}, u32[]{:S(2)}) collective-permute-start(bf16[80,128]{1,0:T(8,128)(2,1)S(1)} %get-tuple-element.50), channel_id=1, source_target_pairs={{0,4},{1,5},{2,6},{3,7},{4,0},{5,1},{6,2},{7,3},{8,12},{9,13},{10,... | collective-permute-start | bytes 61448 | tf_op jit(solution)/shard_map/ppermute | solution.py:727
  7.8 5.6 %collective-permute-start.2 = (bf16[80,128]{1,0:T(8,128)(2,1)S(1)}, bf16[80,128]{1,0:T(8,128)(2,1)S(1)}, u32[]{:S(2)}, u32[]{:S(2)}) collective-permute-start(bf16[80,128]{1,0:T(8,128)(2,1)S(1)} %get-tuple-element.50), channel_id=1, source_target_pairs={{0,20},{1,21},{2,22},{3,23},{4,16},{5,17},{6,18},{7,19},{8,28},{9,... | collective-permute-start | bytes 61448 | tf_op jit(solution)/shard_map/ppermute | solution.py:727
  10.3 13.5 %copy-start.2 = (f32[2,17,8,128]{3,2,1,0:T(8,128)S(1)}, f32[2,17,8,128]{3,2,1,0:T(8,128)}, u32[]{:S(2)}) copy-start(f32[2,17,8,128]{3,2,1,0:T(8,128)} %constant.25.clone.turns) | copy-start | bytes 417796
  10.3 13.5 %copy-start.7 = (bf16[128,256]{1,0:T(8,128)(2,1)S(1)}, bf16[128,256]{1,0:T(8,128)(2,1)}, u32[]{:S(2)}) copy-start(bf16[128,256]{1,0:T(8,128)(2,1)} %constant.24.clone.table) | copy-start | bytes 196612
  10.4 13.5 %copy-start.8 = (bf16[128,144]{1,0:T(8,128)(2,1)S(1)}, bf16[128,144]{1,0:T(8,128)(2,1)}, u32[]{:S(2)}) copy-start(bf16[128,144]{1,0:T(8,128)(2,1)} %constant.23.clone.table_y_ref) | copy-start | bytes 110596
  10.4 13.5 %copy-start.9 = (s32[6]{0:T(128)S(1)}, s32[6]{0:T(128)}, u32[]{:S(2)}) copy-start(s32[6]{0:T(128)} %param.26) | copy-start | bytes 76
  10.4 13.5 %copy-start.10 = (s32[1,6,2]{1,2,0:T(2,128)S(1)}, s32[1,6,2]{1,2,0:T(2,128)}, u32[]{:S(2)}) copy-start(s32[1,6,2]{1,2,0:T(2,128)} %param.23) | copy-start | bytes 148
  10.4 13.5 %copy-start.11 = (f32[1,6,2]{1,2,0:T(2,128)S(1)}, f32[1,6,2]{1,2,0:T(2,128)}, u32[]{:S(2)}) copy-start(f32[1,6,2]{1,2,0:T(2,128)} %param.24) | copy-start | bytes 148
  10.4 13.5 %copy-start.13 = (s32[32]{0:T(128)S(1)}, s32[32]{0:T(128)}, u32[]{:S(2)}) copy-start(s32[32]{0:T(128)} %param.25) | copy-start | bytes 388
  13.4 6.4 %collective-permute-start.3 = (bf16[576,128]{1,0:T(8,128)(2,1)S(1)}, bf16[576,128]{1,0:T(8,128)(2,1)S(1)}, u32[]{:S(2)}, u32[]{:S(2)}) collective-permute-start(bf16[576,128]{1,0:T(8,128)(2,1)S(1)} %constant_dynamic-update-slice_fusion.4), channel_id=1, source_target_pairs={{0,2},{1,3},{2,0},{3,1},{4,6},{5,7},{6,4},{7,5},{8,10},{9,11},{10,... | collective-permute-start | bytes 442376 | tf_op jit(solution)/shard_map/ppermute | solution.py:727
  15.0 4.8 %collective-permute-start.4 = (bf16[464,128]{1,0:T(8,128)(2,1)S(1)}, bf16[464,128]{1,0:T(8,128)(2,1)S(1)}, u32[]{:S(2)}, u32[]{:S(2)}) collective-permute-start(bf16[464,128]{1,0:T(8,128)(2,1)S(1)} %constant_dynamic-update-slice_fusion.9), channel_id=1, source_target_pairs={{0,8},{1,9},{2,10},{3,11},{4,12},{5,13},{6,14},{7,15},{8,0},{9,1},... | collective-permute-start | bytes 356360 | tf_op jit(solution)/shard_map/ppermute | solution.py:727
  16.6 5.3 %collective-permute-start.5 = (bf16[320,128]{1,0:T(8,128)(2,1)S(1)}, bf16[320,128]{1,0:T(8,128)(2,1)S(1)}, u32[]{:S(2)}, u32[]{:S(2)}) collective-permute-start(bf16[320,128]{1,0:T(8,128)(2,1)S(1)} %get-tuple-element.57), channel_id=1, source_target_pairs={{0,10},{1,11},{2,8},{3,9},{4,14},{5,15},{6,12},{7,13},{8,2},{9,3},... | collective-permute-start | bytes 245768 | tf_op jit(solution)/shard_map/ppermute | solution.py:727
  17.0 2.9 %collective-permute-start.6 = (bf16[144,128]{1,0:T(8,128)(2,1)S(1)}, bf16[144,128]{1,0:T(8,128)(2,1)S(1)}, u32[]{:S(2)}, u32[]{:S(2)}) collective-permute-start(bf16[144,128]{1,0:T(8,128)(2,1)S(1)} %get-tuple-element.56), channel_id=1, source_target_pairs={{0,1},{1,0},{2,3},{3,2},{4,16},{5,17},{6,18},{7,19},{8,9},{9,8},{1... | collective-permute-start | bytes 110600 | tf_op jit(solution)/shard_map/ppermute | solution.py:733
  22.0 1.8 %collective-permute-start.7 = (bf16[1568,128]{1,0:T(8,128)(2,1)S(1)}, bf16[1568,128]{1,0:T(8,128)(2,1)S(1)}, u32[]{:S(2)}, u32[]{:S(2)}) collective-permute-start(bf16[1568,128]{1,0:T(8,128)(2,1)S(1)} %constant_dynamic-update-slice_fusion.14), channel_id=1, source_target_pairs={{0,1},{1,0},{2,3},{3,2},{4,5},{5,4},{6,7},{7,6},{8,9},{9,8},{10,11... | collective-permute-start | bytes 1204232 | tf_op jit(solution)/shard_map/ppermute | solution.py:727
  22.7 2.8 %copy-start = (bf16[768,256]{1,0:T(8,128)(2,1)S(1)}, bf16[768,256]{1,0:T(8,128)(2,1)}, u32[]{:S(2)}) copy-start(bf16[768,256]{1,0:T(8,128)(2,1)} %constant.18.clone.refs_7_) | copy-start | bytes 1179652
  22.7 2.8 %copy-start.1 = (bf16[768,256]{1,0:T(8,128)(2,1)S(1)}, bf16[768,256]{1,0:T(8,128)(2,1)}, u32[]{:S(2)}) copy-start(bf16[768,256]{1,0:T(8,128)(2,1)} %constant.19.clone.refs_9_) | copy-start | bytes 1179652
  22.8 2.8 %copy-start.3 = (f32[2,16,8,128]{3,2,1,0:T(8,128)S(1)}, f32[2,16,8,128]{3,2,1,0:T(8,128)}, u32[]{:S(2)}) copy-start(f32[2,16,8,128]{3,2,1,0:T(8,128)} %constant.26.clone.refs_12_) | copy-start | bytes 393220
  22.8 2.8 %copy-start.4 = (bf16[128,384]{1,0:T(8,128)(2,1)S(1)}, bf16[128,384]{1,0:T(8,128)(2,1)}, u32[]{:S(2)}) copy-start(bf16[128,384]{1,0:T(8,128)(2,1)} %constant.20.clone.refs_8_) | copy-start | bytes 294916
  22.8 2.8 %copy-start.5 = (bf16[128,288]{1,0:T(8,128)(2,1)S(1)}, bf16[128,288]{1,0:T(8,128)(2,1)}, u32[]{:S(2)}) copy-start(bf16[128,288]{1,0:T(8,128)(2,1)} %constant.21.clone.refs_10_) | copy-start | bytes 221188
  22.8 2.8 %copy-start.6 = (bf16[96,384]{1,0:T(8,128)(2,1)S(1)}, bf16[96,384]{1,0:T(8,128)(2,1)}, u32[]{:S(2)}) copy-start(bf16[96,384]{1,0:T(8,128)(2,1)} %constant.22.clone.refs_11_) | copy-start | bytes 221188
  22.8 2.8 %copy-start.12 = (s32[1,6]{1,0:T(1,128)S(1)}, s32[1,6]{1,0:T(1,128)}, u32[]{:S(2)}) copy-start(s32[1,6]{1,0:T(1,128)} %present.3) | copy-start | bytes 76
  31.3 6.7 %collective-permute-start.8 = (bf16[256,128]{1,0:T(8,128)(2,1)S(1)}, bf16[256,128]{1,0:T(8,128)(2,1)S(1)}, u32[]{:S(2)}, u32[]{:S(2)}) collective-permute-start(bf16[256,128]{1,0:T(8,128)(2,1)S(1)} %get-tuple-element.71), channel_id=1, source_target_pairs={{0,2},{1,3},{2,0},{3,1},{4,6},{5,7},{6,4},{7,5},{8,10},{9,11},{10,... | collective-permute-start | bytes 196616 | tf_op jit(solution)/shard_map/ppermute | solution.py:727
  31.9 5.7 %collective-permute-start.9 = (bf16[144,128]{1,0:T(8,128)(2,1)S(1)}, bf16[144,128]{1,0:T(8,128)(2,1)S(1)}, u32[]{:S(2)}, u32[]{:S(2)}) collective-permute-start(bf16[144,128]{1,0:T(8,128)(2,1)S(1)} %get-tuple-element.72), channel_id=1, source_target_pairs={{0,16},{1,17},{2,18},{3,19},{4,20},{5,21},{6,22},{7,23},{8,24},{9,... | collective-permute-start | bytes 110600 | tf_op jit(solution)/shard_map/ppermute | solution.py:727
  34.0 3.6 %collective-permute-start.10 = (bf16[144,128]{1,0:T(8,128)(2,1)S(1)}, bf16[144,128]{1,0:T(8,128)(2,1)S(1)}, u32[]{:S(2)}, u32[]{:S(2)}) collective-permute-start(bf16[144,128]{1,0:T(8,128)(2,1)S(1)} %get-tuple-element.73), channel_id=1, source_target_pairs={{0,1},{1,0},{2,3},{3,2},{4,16},{5,17},{6,18},{7,19},{8,9},{9,8},{1... | collective-permute-start | bytes 110600 | tf_op jit(solution)/shard_map/ppermute | solution.py:733
  34.0 4.0 %collective-permute-start.11 = (bf16[144,128]{1,0:T(8,128)(2,1)S(1)}, bf16[144,128]{1,0:T(8,128)(2,1)S(1)}, u32[]{:S(2)}, u32[]{:S(2)}) collective-permute-start(bf16[144,128]{1,0:T(8,128)(2,1)S(1)} %get-tuple-element.74), channel_id=1, source_target_pairs={{0,2},{1,8},{2,0},{3,10},{4,6},{5,12},{6,4},{7,14},{8,1},{9,11},{1... | collective-permute-start | bytes 110600 | tf_op jit(solution)/shard_map/ppermute | solution.py:733
  35.1 2.9 %collective-permute-start.12 = (bf16[144,128]{1,0:T(8,128)(2,1)S(1)}, bf16[144,128]{1,0:T(8,128)(2,1)S(1)}, u32[]{:S(2)}, u32[]{:S(2)}) collective-permute-start(bf16[144,128]{1,0:T(8,128)(2,1)S(1)} %get-tuple-element.75), channel_id=1, source_target_pairs={{0,1},{1,0},{2,3},{3,2},{4,5},{5,4},{6,7},{7,6},{8,9},{9,8},{10,11... | collective-permute-start | bytes 110600 | tf_op jit(solution)/shard_map/ppermute | solution.py:727

commit v7 on v6

--- a/solution.py
+++ b/solution.py
@@ -565,6 +565,7 @@
     copies[1].wait()
     copies[2].wait()
     pad[...] = jnp.zeros((1, CELLROWS * 128), F32)
+    rows = []
     for update in range(UPDATES):
         now = view[:, update : update + 1]
         value = None
@@ -573,9 +574,8 @@
             value = part if value is None else value + part
         pad[:, 0:KS3] = value
         wide = pad[...]
-        rows = [wide[:, 128 * row : 128 * (row + 1)] for row in range(CELLROWS)]
-        here = slice(CELLROWS * update, CELLROWS * (update + 1))
-        cells_out[here, :] = jnp.concatenate(rows, axis=0).astype(BF16)
+        rows += [wide[:, 128 * row : 128 * (row + 1)] for row in range(CELLROWS)]
+    cells_out[...] = jnp.concatenate(rows, axis=0).astype(BF16)
 
 
 VIEW_PARTS = 9

time: 44.3 us -> 44.4 us (level)
  no operation moved by 1% of the time
where the time goes in v7:
time: 44.4 us; the launch traced here: 44.2 us
  Pallas kernels  19.7 us (44%)
  starting transfers between devices  14 us (32%)
  waiting for transfers between devices  9.07 us (20%)
  between operations  1.07 us (2%)
    pallas_call x6, Pallas kernels, call(): pl.pallas_call(body, in_specs=ins, out_specs=[VM] * len(outs) if many els...  19.7 us
    ppermute x10, starting transfers between devices, swap(): lax.ppermute(value, 'blk', [(number, number ^ distance) for number in ran...  12.9 us
    ppermute x10, waiting for transfers between devices, swap(): lax.ppermute(value, 'blk', [(number, number ^ distance) for number in ran...  8.69 us
    ppermute x3, starting transfers between devices, swap_slab(): return lax.ppermute(slab, 'blk', far_pairs(count, axis))  1.06 us
  transfers between devices with their start and end apart: 13, of which 5 were waited for; matrix products, arithmetic and copies ran while one was open for 0% of the time, Pallas kernels for 9%

profile of v7, /device:TPU:0, one launch (start us, length us, event | category | flops | bytes accessed | tf_op | source)
XLA Modules:
  0.0 44.2 jit_solution(12450234418696226317)
XLA Ops:
  0.0 2.1 %start.1 = (f32[2,768,128]{2,1,0:T(8,128)S(1)}, bf16[80,128]{1,0:T(8,128)(2,1)S(1)}, bf16[256,128]{1,0:T(8,128)(2,1)S(1)}, bf16[144,128]{1,0:T(8,128)(2,1)S(1)},...) custom-call(s32[1,6]{1,0:T(1,128)} %bitcast.16, f32[6,1,4913]{2,1,0:T(1,128)} %bitcast.27, ...), custom_call_target="tpu_custom_call" | custom-call | tf_op jit(solution)/shard_map/start/pallas_call | solution.py:698
  2.1 4.1 %collective-permute-start = (bf16[224,128]{1,0:T(8,128)(2,1)S(1)}, bf16[224,128]{1,0:T(8,128)(2,1)S(1)}, u32[]{:S(2)}, u32[]{:S(2)}) collective-permute-start(bf16[224,128]{1,0:T(8,128)(2,1)S(1)} %pad_maximum_fusion.1), channel_id=1, source_target_pairs={{0,16},{1,17},{2,18},{3,19},{4,20},{5,21},{6,22},{7,23},{8,24},{9,... | collective-permute-start | bytes 172040 | tf_op jit(solution)/shard_map/ppermute | solution.py:727
  6.2 1.5 %collective-permute-start.1 = (bf16[80,128]{1,0:T(8,128)(2,1)S(1)}, bf16[80,128]{1,0:T(8,128)(2,1)S(1)}, u32[]{:S(2)}, u32[]{:S(2)}) collective-permute-start(bf16[80,128]{1,0:T(8,128)(2,1)S(1)} %get-tuple-element.50), channel_id=1, source_target_pairs={{0,4},{1,5},{2,6},{3,7},{4,0},{5,1},{6,2},{7,3},{8,12},{9,13},{10,... | collective-permute-start | bytes 61448 | tf_op jit(solution)/shard_map/ppermute | solution.py:727
  7.7 0.0 collective-permute-start.2
  7.8 2.6 %views.1 = (f32[2,768,128]{2,1,0:T(8,128)S(1)}, f32[2,768,128]{2,1,0:T(8,128)S(1)}) custom-call(s32[1,6]{1,0:T(1,128)} %bitcast.17, bf16[1,6,110592]{2,1,0:T(8,128)(2,1)} %observed.1), custom_call_target="tpu_custom_call" | custom-call | tf_op jit(solution)/shard_map/views/pallas_call | solution.py:698
  10.3 0.0 copy-start.2
  10.3 0.0 copy-start.7
  10.4 0.0 copy-start.8
  10.4 0.0 copy-start.9
  10.5 2.9 %collective-permute-done.2 = bf16[80,128]{1,0:T(8,128)(2,1)S(1)} collective-permute-done((bf16[80,128]{1,0:T(8,128)(2,1)S(1)}, bf16[80,128]{1,0:T(8,128)(2,1)S(1)}, u32[]{:S(2)}, u32[]{:S(2)}) %collective-permute-start.2) | collective-permute-done | bytes 20512 | tf_op jit(solution)/shard_map/ppermute | solution.py:727
  13.4 1.6 %collective-permute-start.3 = (bf16[576,128]{1,0:T(8,128)(2,1)S(1)}, bf16[576,128]{1,0:T(8,128)(2,1)S(1)}, u32[]{:S(2)}, u32[]{:S(2)}) collective-permute-start(bf16[576,128]{1,0:T(8,128)(2,1)S(1)} %constant_dynamic-update-slice_fusion.4), channel_id=1, source_target_pairs={{0,2},{1,3},{2,0},{3,1},{4,6},{5,7},{6,4},{7,5},{8,10},{9,11},{10,... | collective-permute-start | bytes 442376 | tf_op jit(solution)/shard_map/ppermute | solution.py:727
  15.0 1.6 %collective-permute-start.4 = (bf16[464,128]{1,0:T(8,128)(2,1)S(1)}, bf16[464,128]{1,0:T(8,128)(2,1)S(1)}, u32[]{:S(2)}, u32[]{:S(2)}) collective-permute-start(bf16[464,128]{1,0:T(8,128)(2,1)S(1)} %constant_dynamic-update-slice_fusion.9), channel_id=1, source_target_pairs={{0,8},{1,9},{2,10},{3,11},{4,12},{5,13},{6,14},{7,15},{8,0},{9,1},... | collective-permute-start | bytes 356360 | tf_op jit(solution)/shard_map/ppermute | solution.py:727
  16.6 0.4 collective-permute-start.5
  17.0 2.8 %collective-permute-done.4 = bf16[464,128]{1,0:T(8,128)(2,1)S(1)} collective-permute-done((bf16[464,128]{1,0:T(8,128)(2,1)S(1)}, bf16[464,128]{1,0:T(8,128)(2,1)S(1)}, u32[]{:S(2)}, u32[]{:S(2)}) %collective-permute-start.4) | collective-permute-done | bytes 118816 | tf_op jit(solution)/shard_map/ppermute | solution.py:727
  19.8 2.0 %collective-permute-done.5 = bf16[320,128]{1,0:T(8,128)(2,1)S(1)} collective-permute-done((bf16[320,128]{1,0:T(8,128)(2,1)S(1)}, bf16[320,128]{1,0:T(8,128)(2,1)S(1)}, u32[]{:S(2)}, u32[]{:S(2)}) %collective-permute-start.5) | collective-permute-done | bytes 81952 | tf_op jit(solution)/shard_map/ppermute | solution.py:727
  22.0 0.1 collective-permute-start.7
  22.7 0.0 copy-start
  22.7 0.0 copy-start.1
  22.8 0.0 copy-start.3
  22.8 0.0 copy-start.4
  22.8 0.0 copy-start.5
  22.8 0.0 copy-start.6
  22.9 0.9 %collective-permute-done.7 = bf16[1568,128]{1,0:T(8,128)(2,1)S(1)} collective-permute-done((bf16[1568,128]{1,0:T(8,128)(2,1)S(1)}, bf16[1568,128]{1,0:T(8,128)(2,1)S(1)}, u32[]{:S(2)}, u32[]{:S(2)}) %collective-permute-start.7) | collective-permute-done | bytes 401440 | tf_op jit(solution)/shard_map/ppermute | solution.py:727
  23.9 1.6 %spectrum.2.refs_5_ = f32[16,128,128]{2,1,0:T(8,128)S(1)} custom-call(s32[1,6]{1,0:T(1,128)S(1)} %bitcast.18, s32[1,2,6]{2,1,0:T(2,128)S(1)} %bitcast.20, f32[1,2,6]{2,1,0:T(2,128)S(1)} %bitcast.22, s32[1,32]{1,0:T(1,128)S(1)} %bitcast.24, bf16[16,80,128]{2,1,0:T(8,128)(2,1)S(1)} %bitcast.12, bf16[16,80,128]{2,1,0:T(8,128)(2,1)S(1)} %bitcast.14, ...), custom_call_target="tpu_custom_call" | custom-call | tf_op jit(solution)/shard_map/spectrum/pallas_call | solution.py:698
  25.6 5.7 %first.1 = (f32[2,768,128]{2,1,0:T(8,128)S(1)}, bf16[256,128]{1,0:T(8,128)(2,1)S(1)}, bf16[144,128]{1,0:T(8,128)(2,1)S(1)}, bf16[144,128]{1,0:T(8,128)(2,1)S(1)}...) custom-call(s32[1,1]{1,0:T(1,128)} %bitcast.10.tissue, s32[1,6]{1,0:T(1,128)S(1)} %copy-done.12, ...), custom_call_target="tpu_custom_call" | custom-call | tf_op jit(solution)/shard_map/first/pallas_call | solution.py:698
  31.3 0.6 %collective-permute-start.8 = (bf16[256,128]{1,0:T(8,128)(2,1)S(1)}, bf16[256,128]{1,0:T(8,128)(2,1)S(1)}, u32[]{:S(2)}, u32[]{:S(2)}) collective-permute-start(bf16[256,128]{1,0:T(8,128)(2,1)S(1)} %get-tuple-element.71), channel_id=1, source_target_pairs={{0,2},{1,3},{2,0},{3,1},{4,6},{5,7},{6,4},{7,5},{8,10},{9,11},{10,... | collective-permute-start | bytes 196616 | tf_op jit(solution)/shard_map/ppermute | solution.py:727
  31.9 2.2 %collective-permute-start.9 = (bf16[144,128]{1,0:T(8,128)(2,1)S(1)}, bf16[144,128]{1,0:T(8,128)(2,1)S(1)}, u32[]{:S(2)}, u32[]{:S(2)}) collective-permute-start(bf16[144,128]{1,0:T(8,128)(2,1)S(1)} %get-tuple-element.72), channel_id=1, source_target_pairs={{0,16},{1,17},{2,18},{3,19},{4,20},{5,21},{6,22},{7,23},{8,24},{9,... | collective-permute-start | bytes 110600 | tf_op jit(solution)/shard_map/ppermute | solution.py:727
  34.0 1.1 %collective-permute-start.11 = (bf16[144,128]{1,0:T(8,128)(2,1)S(1)}, bf16[144,128]{1,0:T(8,128)(2,1)S(1)}, u32[]{:S(2)}, u32[]{:S(2)}) collective-permute-start(bf16[144,128]{1,0:T(8,128)(2,1)S(1)} %get-tuple-element.74), channel_id=1, source_target_pairs={{0,2},{1,8},{2,0},{3,10},{4,6},{5,12},{6,4},{7,14},{8,1},{9,11},{1... | collective-permute-start | bytes 110600 | tf_op jit(solution)/shard_map/ppermute | solution.py:733
  35.1 0.9 %collective-permute-start.12 = (bf16[144,128]{1,0:T(8,128)(2,1)S(1)}, bf16[144,128]{1,0:T(8,128)(2,1)S(1)}, u32[]{:S(2)}, u32[]{:S(2)}) collective-permute-start(bf16[144,128]{1,0:T(8,128)(2,1)S(1)} %get-tuple-element.75), channel_id=1, source_target_pairs={{0,1},{1,0},{2,3},{3,2},{4,5},{5,4},{6,7},{7,6},{8,9},{9,8},{10,11... | collective-permute-start | bytes 110600 | tf_op jit(solution)/shard_map/ppermute | solution.py:727
  36.0 1.6 %spectrum.3.refs_5_ = f32[16,128,128]{2,1,0:T(8,128)S(1)} custom-call(s32[1,6]{1,0:T(1,128)S(1)} %bitcast.19, s32[1,2,6]{2,1,0:T(2,128)S(1)} %bitcast.21, f32[1,2,6]{2,1,0:T(2,128)S(1)} %bitcast.23, s32[1,32]{1,0:T(1,128)S(1)} %bitcast.25, bf16[16,80,128]{2,1,0:T(8,128)(2,1)S(1)} %bitcast.13, bf16[16,80,128]{2,1,0:T(8,128)(2,1)S(1)} %bitcast.15, ...), custom_call_target="tpu_custom_call" | custom-call | tf_op jit(solution)/shard_map/spectrum/pallas_call | solution.py:698
  37.6 0.4 collective-permute-done.11.refs_3_
  38.0 6.2 %last.1 = f32[864,128]{1,0:T(8,128)} custom-call(s32[1,1]{1,0:T(1,128)} %bitcast.11.tissue, s32[1,6]{1,0:T(1,128)S(1)} %copy-done.12, f32[2,768,128]{2,1,0:T(8,128)S(1)} %get-tuple-element.70.u, bf16[256,128]{1,0:T(8,128)(2,1)S(1)} %collective-permute-done.8.refs_0_, bf16[144,128]{1,0:T(8,128)(2,1)S(1)} %collective-permute-done.9.refs_1_, ...), custom_call_target="tpu_custom_call" | custom-call | tf_op jit(solution)/shard_map/last/pallas_call | solution.py:698
  (49 shorter events, 0.3 us)
Async XLA Ops:
  2.1 8.3 %collective-permute-start = (bf16[224,128]{1,0:T(8,128)(2,1)S(1)}, bf16[224,128]{1,0:T(8,128)(2,1)S(1)}, u32[]{:S(2)}, u32[]{:S(2)}) collective-permute-start(bf16[224,128]{1,0:T(8,128)(2,1)S(1)} %pad_maximum_fusion.1), channel_id=1, source_target_pairs={{0,16},{1,17},{2,18},{3,19},{4,20},{5,21},{6,22},{7,23},{8,24},{9,... | collective-permute-start | bytes 172040 | tf_op jit(solution)/shard_map/ppermute | solution.py:727
  6.2 4.2 %collective-permute-start.1 = (bf16[80,128]{1,0:T(8,128)(2,1)S(1)}, bf16[80,128]{1,0:T(8,128)(2,1)S(1)}, u32[]{:S(2)}, u32[]{:S(2)}) collective-permute-start(bf16[80,128]{1,0:T(8,128)(2,1)S(1)} %get-tuple-element.50), channel_id=1, source_target_pairs={{0,4},{1,5},{2,6},{3,7},{4,0},{5,1},{6,2},{7,3},{8,12},{9,13},{10,... | collective-permute-start | bytes 61448 | tf_op jit(solution)/shard_map/ppermute | solution.py:727
  7.7 5.6 %collective-permute-start.2 = (bf16[80,128]{1,0:T(8,128)(2,1)S(1)}, bf16[80,128]{1,0:T(8,128)(2,1)S(1)}, u32[]{:S(2)}, u32[]{:S(2)}) collective-permute-start(bf16[80,128]{1,0:T(8,128)(2,1)S(1)} %get-tuple-element.50), channel_id=1, source_target_pairs={{0,20},{1,21},{2,22},{3,23},{4,16},{5,17},{6,18},{7,19},{8,28},{9,... | collective-permute-start | bytes 61448 | tf_op jit(solution)/shard_map/ppermute | solution.py:727
  10.3 13.5 %copy-start.2 = (f32[2,17,8,128]{3,2,1,0:T(8,128)S(1)}, f32[2,17,8,128]{3,2,1,0:T(8,128)}, u32[]{:S(2)}) copy-start(f32[2,17,8,128]{3,2,1,0:T(8,128)} %constant.25.clone.turns) | copy-start | bytes 417796
  10.3 13.5 %copy-start.7 = (bf16[128,256]{1,0:T(8,128)(2,1)S(1)}, bf16[128,256]{1,0:T(8,128)(2,1)}, u32[]{:S(2)}) copy-start(bf16[128,256]{1,0:T(8,128)(2,1)} %constant.24.clone.table) | copy-start | bytes 196612
  10.4 13.5 %copy-start.8 = (bf16[128,144]{1,0:T(8,128)(2,1)S(1)}, bf16[128,144]{1,0:T(8,128)(2,1)}, u32[]{:S(2)}) copy-start(bf16[128,144]{1,0:T(8,128)(2,1)} %constant.23.clone.table_y_ref) | copy-start | bytes 110596
  10.4 13.5 %copy-start.9 = (s32[6]{0:T(128)S(1)}, s32[6]{0:T(128)}, u32[]{:S(2)}) copy-start(s32[6]{0:T(128)} %param.26) | copy-start | bytes 76
  10.4 13.5 %copy-start.10 = (s32[1,6,2]{1,2,0:T(2,128)S(1)}, s32[1,6,2]{1,2,0:T(2,128)}, u32[]{:S(2)}) copy-start(s32[1,6,2]{1,2,0:T(2,128)} %param.23) | copy-start | bytes 148
  10.4 13.5 %copy-start.11 = (f32[1,6,2]{1,2,0:T(2,128)S(1)}, f32[1,6,2]{1,2,0:T(2,128)}, u32[]{:S(2)}) copy-start(f32[1,6,2]{1,2,0:T(2,128)} %param.24) | copy-start | bytes 148
  10.4 13.5 %copy-start.13 = (s32[32]{0:T(128)S(1)}, s32[32]{0:T(128)}, u32[]{:S(2)}) copy-start(s32[32]{0:T(128)} %param.25) | copy-start | bytes 388
  13.4 6.4 %collective-permute-start.3 = (bf16[576,128]{1,0:T(8,128)(2,1)S(1)}, bf16[576,128]{1,0:T(8,128)(2,1)S(1)}, u32[]{:S(2)}, u32[]{:S(2)}) collective-permute-start(bf16[576,128]{1,0:T(8,128)(2,1)S(1)} %constant_dynamic-update-slice_fusion.4), channel_id=1, source_target_pairs={{0,2},{1,3},{2,0},{3,1},{4,6},{5,7},{6,4},{7,5},{8,10},{9,11},{10,... | collective-permute-start | bytes 442376 | tf_op jit(solution)/shard_map/ppermute | solution.py:727
  15.0 4.8 %collective-permute-start.4 = (bf16[464,128]{1,0:T(8,128)(2,1)S(1)}, bf16[464,128]{1,0:T(8,128)(2,1)S(1)}, u32[]{:S(2)}, u32[]{:S(2)}) collective-permute-start(bf16[464,128]{1,0:T(8,128)(2,1)S(1)} %constant_dynamic-update-slice_fusion.9), channel_id=1, source_target_pairs={{0,8},{1,9},{2,10},{3,11},{4,12},{5,13},{6,14},{7,15},{8,0},{9,1},... | collective-permute-start | bytes 356360 | tf_op jit(solution)/shard_map/ppermute | solution.py:727
  16.6 5.3 %collective-permute-start.5 = (bf16[320,128]{1,0:T(8,128)(2,1)S(1)}, bf16[320,128]{1,0:T(8,128)(2,1)S(1)}, u32[]{:S(2)}, u32[]{:S(2)}) collective-permute-start(bf16[320,128]{1,0:T(8,128)(2,1)S(1)} %get-tuple-element.57), channel_id=1, source_target_pairs={{0,10},{1,11},{2,8},{3,9},{4,14},{5,15},{6,12},{7,13},{8,2},{9,3},... | collective-permute-start | bytes 245768 | tf_op jit(solution)/shard_map/ppermute | solution.py:727
  17.0 2.9 %collective-permute-start.6 = (bf16[144,128]{1,0:T(8,128)(2,1)S(1)}, bf16[144,128]{1,0:T(8,128)(2,1)S(1)}, u32[]{:S(2)}, u32[]{:S(2)}) collective-permute-start(bf16[144,128]{1,0:T(8,128)(2,1)S(1)} %get-tuple-element.56), channel_id=1, source_target_pairs={{0,1},{1,0},{2,3},{3,2},{4,16},{5,17},{6,18},{7,19},{8,9},{9,8},{1... | collective-permute-start | bytes 110600 | tf_op jit(solution)/shard_map/ppermute | solution.py:733
  22.0 1.8 %collective-permute-start.7 = (bf16[1568,128]{1,0:T(8,128)(2,1)S(1)}, bf16[1568,128]{1,0:T(8,128)(2,1)S(1)}, u32[]{:S(2)}, u32[]{:S(2)}) collective-permute-start(bf16[1568,128]{1,0:T(8,128)(2,1)S(1)} %constant_dynamic-update-slice_fusion.14), channel_id=1, source_target_pairs={{0,1},{1,0},{2,3},{3,2},{4,5},{5,4},{6,7},{7,6},{8,9},{9,8},{10,11... | collective-permute-start | bytes 1204232 | tf_op jit(solution)/shard_map/ppermute | solution.py:727
  22.7 2.8 %copy-start = (bf16[768,256]{1,0:T(8,128)(2,1)S(1)}, bf16[768,256]{1,0:T(8,128)(2,1)}, u32[]{:S(2)}) copy-start(bf16[768,256]{1,0:T(8,128)(2,1)} %constant.18.clone.refs_7_) | copy-start | bytes 1179652
  22.7 2.8 %copy-start.1 = (bf16[768,256]{1,0:T(8,128)(2,1)S(1)}, bf16[768,256]{1,0:T(8,128)(2,1)}, u32[]{:S(2)}) copy-start(bf16[768,256]{1,0:T(8,128)(2,1)} %constant.19.clone.refs_9_) | copy-start | bytes 1179652
  22.8 2.8 %copy-start.3 = (f32[2,16,8,128]{3,2,1,0:T(8,128)S(1)}, f32[2,16,8,128]{3,2,1,0:T(8,128)}, u32[]{:S(2)}) copy-start(f32[2,16,8,128]{3,2,1,0:T(8,128)} %constant.26.clone.refs_12_) | copy-start | bytes 393220
  22.8 2.8 %copy-start.4 = (bf16[128,384]{1,0:T(8,128)(2,1)S(1)}, bf16[128,384]{1,0:T(8,128)(2,1)}, u32[]{:S(2)}) copy-start(bf16[128,384]{1,0:T(8,128)(2,1)} %constant.20.clone.refs_8_) | copy-start | bytes 294916
  22.8 2.8 %copy-start.5 = (bf16[128,288]{1,0:T(8,128)(2,1)S(1)}, bf16[128,288]{1,0:T(8,128)(2,1)}, u32[]{:S(2)}) copy-start(bf16[128,288]{1,0:T(8,128)(2,1)} %constant.21.clone.refs_10_) | copy-start | bytes 221188
  22.8 2.8 %copy-start.6 = (bf16[96,384]{1,0:T(8,128)(2,1)S(1)}, bf16[96,384]{1,0:T(8,128)(2,1)}, u32[]{:S(2)}) copy-start(bf16[96,384]{1,0:T(8,128)(2,1)} %constant.22.clone.refs_11_) | copy-start | bytes 221188
  22.8 2.8 %copy-start.12 = (s32[1,6]{1,0:T(1,128)S(1)}, s32[1,6]{1,0:T(1,128)}, u32[]{:S(2)}) copy-start(s32[1,6]{1,0:T(1,128)} %present.3) | copy-start | bytes 76
  31.3 6.7 %collective-permute-start.8 = (bf16[256,128]{1,0:T(8,128)(2,1)S(1)}, bf16[256,128]{1,0:T(8,128)(2,1)S(1)}, u32[]{:S(2)}, u32[]{:S(2)}) collective-permute-start(bf16[256,128]{1,0:T(8,128)(2,1)S(1)} %get-tuple-element.71), channel_id=1, source_target_pairs={{0,2},{1,3},{2,0},{3,1},{4,6},{5,7},{6,4},{7,5},{8,10},{9,11},{10,... | collective-permute-start | bytes 196616 | tf_op jit(solution)/shard_map/ppermute | solution.py:727
  31.9 5.7 %collective-permute-start.9 = (bf16[144,128]{1,0:T(8,128)(2,1)S(1)}, bf16[144,128]{1,0:T(8,128)(2,1)S(1)}, u32[]{:S(2)}, u32[]{:S(2)}) collective-permute-start(bf16[144,128]{1,0:T(8,128)(2,1)S(1)} %get-tuple-element.72), channel_id=1, source_target_pairs={{0,16},{1,17},{2,18},{3,19},{4,20},{5,21},{6,22},{7,23},{8,24},{9,... | collective-permute-start | bytes 110600 | tf_op jit(solution)/shard_map/ppermute | solution.py:727
  34.0 3.6 %collective-permute-start.10 = (bf16[144,128]{1,0:T(8,128)(2,1)S(1)}, bf16[144,128]{1,0:T(8,128)(2,1)S(1)}, u32[]{:S(2)}, u32[]{:S(2)}) collective-permute-start(bf16[144,128]{1,0:T(8,128)(2,1)S(1)} %get-tuple-element.73), channel_id=1, source_target_pairs={{0,1},{1,0},{2,3},{3,2},{4,16},{5,17},{6,18},{7,19},{8,9},{9,8},{1... | collective-permute-start | bytes 110600 | tf_op jit(solution)/shard_map/ppermute | solution.py:733
  34.0 4.0 %collective-permute-start.11 = (bf16[144,128]{1,0:T(8,128)(2,1)S(1)}, bf16[144,128]{1,0:T(8,128)(2,1)S(1)}, u32[]{:S(2)}, u32[]{:S(2)}) collective-permute-start(bf16[144,128]{1,0:T(8,128)(2,1)S(1)} %get-tuple-element.74), channel_id=1, source_target_pairs={{0,2},{1,8},{2,0},{3,10},{4,6},{5,12},{6,4},{7,14},{8,1},{9,11},{1... | collective-permute-start | bytes 110600 | tf_op jit(solution)/shard_map/ppermute | solution.py:733
  35.1 2.9 %collective-permute-start.12 = (bf16[144,128]{1,0:T(8,128)(2,1)S(1)}, bf16[144,128]{1,0:T(8,128)(2,1)S(1)}, u32[]{:S(2)}, u32[]{:S(2)}) collective-permute-start(bf16[144,128]{1,0:T(8,128)(2,1)S(1)} %get-tuple-element.75), channel_id=1, source_target_pairs={{0,1},{1,0},{2,3},{3,2},{4,5},{5,4},{6,7},{7,6},{8,9},{9,8},{10,11... | collective-permute-start | bytes 110600 | tf_op jit(solution)/shard_map/ppermute | solution.py:727
